TPU v7x, 32 devices: a whole 2x2x4 slice. The times are simulated.
32 devices in a mesh: ctx: 8 (over y, x, core), grp: 4 (over z).
Axes of the slice: x: 2, y: 2, z: 4, core: 2. Of those that a mesh axis runs over, the one named last changes fastest.
Arguments:
- tokens: bfloat16 [8192, 2560], P(('ctx', 'grp')), may hold values from -6 to 6
- norm_gain: bfloat16 [2560], replicated, may hold values from 0.5 to 1.5
- w_query: bfloat16 [2560, 2560], P('grp'), may hold values from -0.125 to 0.125
- w_key: bfloat16 [2560, 512], P('grp'), may hold values from -0.125 to 0.125
- w_value: bfloat16 [2560, 512], P('grp'), may hold values from -0.125 to 0.125
- b_query: bfloat16 [2560], replicated, may hold values from -3 to 3
- b_key: bfloat16 [512], replicated, may hold values from -3 to 3
- b_value: bfloat16 [512], replicated, may hold values from -3 to 3
- cache_keys: bfloat16 [1024, 512], P('ctx'), may hold values from -140 to 140
- cache_values: bfloat16 [1024, 512], P('ctx'), may hold values from -6 to 6
- block_lists: int32 [20, 64, 4], P(None, ('ctx', 'grp')), may hold values from -1 to 7, as said below
- start_position: int32 [1], replicated, may hold values from 0 to 1040384
Outputs:
- context: float32 [8192, 2560], P(('ctx', 'grp'))
- keys_new: float32 [8192, 512], P(('ctx', 'grp'))
- values_new: float32 [8192, 512], P(('ctx', 'grp'))
Inputs may be any that keep to these rules, and one draw needn't show every extreme that they name: `block_lists`: each list names distinct blocks of 128 prefix positions, named blocks first and -1 in the empty slots after them; every list names at least one block, some list names 4 and some only one.
All inputs are finite; a program needn't handle non-finite values.
Results may differ from a plain program's by a relative error of at most 0.034.
Values may be sent and summed in bfloat16 or wider, within the bound.
No kernel may reach another device: no remote copies, remote signals or barrier semaphores. Data moves between devices by JAX's collectives and lax.ppermute only.
A program may use at most 128 MiB of HBM per device.

v0:
```python
import jax
import jax.numpy as jnp
import numpy as np
from jax import lax
from jax.sharding import PartitionSpec as P

HD = 128
GROUP = 5
QBLK = 128


norm_eps = 1e-06
rope_base = 10000000.0


def angle_tables(head_dim):
    half_dim = head_dim // 2
    frequency = rope_base ** (-2.0 * np.arange(half_dim) / head_dim)
    return np.stack(
        [np.mod(frequency * 32.0**digit_level, 2.0 * np.pi) for digit_level in range(4)]
    )


def rotate(values, positions):
    head_dim = values.shape[-1]
    half_dim = head_dim // 2
    tables = jnp.asarray(angle_tables(head_dim), jnp.float32)
    angles = jnp.zeros((positions.shape[0], half_dim), jnp.float32)
    remaining = positions
    for digit_level in range(4):
        digit_value = (remaining % 32).astype(jnp.float32)
        angles = angles + digit_value[:, None] * tables[digit_level][None, :]
        remaining = remaining // 32
    cosine = jnp.cos(angles)[:, None, :]
    sine_part = jnp.sin(angles)[:, None, :]
    lower_half = values[..., :half_dim]
    upper_half = values[..., half_dim:]
    return jnp.concatenate(
        [
            lower_half * cosine - upper_half * sine_part,
            upper_half * cosine + lower_half * sine_part,
        ],
        axis=-1,
    )


def on_device(
    tokens,
    norm_gain,
    w_query,
    w_key,
    w_value,
    b_query,
    b_key,
    b_value,
    cache_keys,
    cache_values,
    block_lists,
    start_position,
):
    row_count = tokens.shape[0]
    query_width = w_query.shape[1]
    kv_width = w_key.shape[1]
    heads_kv = kv_width // HD
    block_count = row_count // QBLK
    widened = tokens.astype(jnp.float32)
    normed = (
        widened
        * lax.rsqrt(jnp.mean(widened * widened, axis=-1, keepdims=True) + norm_eps)
        * norm_gain.astype(jnp.float32)
    ).astype(jnp.bfloat16)
    panels = (
        lax.all_gather(w_query, "grp", axis=0, tiled=True),
        lax.all_gather(w_key, "grp", axis=0, tiled=True),
        lax.all_gather(w_value, "grp", axis=0, tiled=True),
    )
    query_lin, key_lin, value_lin = tuple(
        (jnp.dot(normed, panel, preferred_element_type=jnp.float32) for panel in panels)
    )
    row_start = (lax.axis_index("ctx") * lax.axis_size("grp") + lax.axis_index("grp")) * row_count
    positions = start_position[0] + row_start + jnp.arange(row_count, dtype=jnp.int32)
    query = rotate(
        (query_lin + b_query.astype(jnp.float32)).reshape(row_count, heads_kv * GROUP, HD),
        positions,
    )
    keys_new = rotate(
        (key_lin + b_key.astype(jnp.float32)).reshape(row_count, heads_kv, HD), positions
    ).reshape(row_count, kv_width)
    values_new = value_lin + b_value.astype(jnp.float32)
    score_scale = HD ** (-0.5)
    query_heads = query.reshape(row_count, heads_kv, GROUP, HD)
    query_blocks = query.reshape(block_count, QBLK, heads_kv, GROUP, HD)
    key_blocks = keys_new.reshape(block_count, QBLK, heads_kv, HD)
    value_blocks = values_new.reshape(block_count, QBLK, heads_kv, HD)
    near_scores = jnp.einsum("bqkgd,bskd->kgbqs", query_blocks, key_blocks) * score_scale
    causal = lax.broadcasted_iota(jnp.int32, (QBLK, QBLK), 0) >= lax.broadcasted_iota(
        jnp.int32, (QBLK, QBLK), 1
    )
    near_scores = jnp.where(causal, near_scores, -jnp.inf)
    near_max = jnp.max(near_scores, axis=-1)
    near_exp = jnp.exp(near_scores - near_max[..., None])
    near_total = jnp.sum(near_exp, axis=-1)
    near_weighted = jnp.einsum("kgbqs,bskd->kgbqd", near_exp, value_blocks)
    initial_state = (
        near_max.reshape(heads_kv, GROUP, row_count),
        near_total.reshape(heads_kv, GROUP, row_count),
        near_weighted.reshape(heads_kv, GROUP, row_count, HD),
    )
    piece_keys = lax.all_gather(cache_keys, "ctx", axis=0, tiled=True)
    piece_values = lax.all_gather(cache_values, "ctx", axis=0, tiled=True)
    key_count = piece_keys.shape[0]

    def one_key_block(block_step, state_inner):
        old_max, old_total, old_weighted = state_inner
        block_keys = (
            lax.dynamic_slice_in_dim(piece_keys, block_step * QBLK, QBLK, 0)
            .reshape(QBLK, heads_kv, HD)
            .astype(jnp.float32)
        )
        block_values = (
            lax.dynamic_slice_in_dim(piece_values, block_step * QBLK, QBLK, 0)
            .reshape(QBLK, heads_kv, HD)
            .astype(jnp.float32)
        )
        attention_affinity = jnp.einsum("rkgd,pkd->kgrp", query_heads, block_keys) * score_scale
        listed = jnp.any(block_lists == block_step, axis=2).reshape(
            heads_kv, GROUP, block_count, 1, 1
        )
        attention_affinity = jnp.where(
            listed, attention_affinity.reshape(heads_kv, GROUP, block_count, QBLK, QBLK), -jnp.inf
        ).reshape(heads_kv, GROUP, row_count, QBLK)
        new_max = jnp.maximum(old_max, jnp.max(attention_affinity, axis=-1))
        factor = jnp.exp(old_max - new_max)
        weights = jnp.exp(attention_affinity - new_max[..., None])
        new_total = old_total * factor + jnp.sum(weights, axis=-1)
        new_weighted = old_weighted * factor[..., None] + jnp.einsum(
            "kgrp,pkd->kgrd", weights, block_values
        )
        return (new_max, new_total, new_weighted)

    final_max, row_total, weighted = lax.fori_loop(
        0, key_count // QBLK, one_key_block, initial_state
    )
    context = jnp.transpose(weighted / row_total[..., None], (2, 0, 1, 3)).reshape(
        row_count, query_width
    )
    return (context, keys_new, values_new)


def solution(mesh):
    in_specs = (
        P(("ctx", "grp"), None),
        P(),
        P("grp", None),
        P("grp", None),
        P("grp", None),
        P(),
        P(),
        P(),
        P("ctx", None),
        P("ctx", None),
        P(None, ("ctx", "grp"), None),
        P(),
    )
    out_specs = (P(("ctx", "grp"), None), P(("ctx", "grp"), None), P(("ctx", "grp"), None))
    return jax.shard_map(
        on_device, mesh=mesh, in_specs=in_specs, out_specs=out_specs, check_vma=False
    )
```

profile of v0, /device:TPU:0, one launch (start us, length us, event | category | flops | bytes accessed | tf_op | source)
XLA Modules:
  0.0 457.3 jit_solution(17581474270468559938)
XLA Ops:
  12.9 54.2 %all-gather.6.cloned.1.call-done = bf16[2560,512]{1,0:T(8,128)(2,1)} async-done(((bf16[640,512]{1,0:T(8,128)(2,1)}), bf16[2560,512]{1,0:T(8,128)(2,1)}) %all-gather.6.cloned.1.call-update) | async-done | bytes 2621456 | tf_op jit(solution)/shard_map/all_gather | solution.py:74
  67.2 2.6 convolution_add_fusion.2
  70.9 51.4 %all-gather.10.cloned.1.call-done = bf16[2560,512]{1,0:T(8,128)(2,1)} async-done(((bf16[640,512]{1,0:T(8,128)(2,1)}), bf16[2560,512]{1,0:T(8,128)(2,1)}) %all-gather.10.cloned.1.call-update) | async-done | bytes 2621456 | tf_op jit(solution)/shard_map/all_gather | solution.py:75
  122.3 2.6 convolution_add_fusion.1
  125.9 223.6 %all-gather.8.cloned.1.call-done = bf16[2560,2560]{1,0:T(8,128)(2,1)} async-done(((bf16[640,2560]{1,0:T(8,128)(2,1)}), bf16[2560,2560]{1,0:T(8,128)(2,1)}) %all-gather.8.cloned.1.call-update) | async-done | bytes 13107216 | tf_op jit(solution)/shard_map/all_gather | solution.py:73
  349.5 9.8 %convolution_add_fusion = f32[256,2560]{1,0:T(8,128)} fusion(bf16[2560,2560]{1,0:T(8,128)(2,1)} %all-gather.8.cloned.1.call-done, f32[2560]{0:T(1024)S(1)} %convert_element_type.64, bf16[256,2560]{1,0:T(8,128)(2,1)S(1)} %copy-done.2, f32[2560]{0:T(1024)S(1)} %convert_element_type.57, f32[256]{0:T(256)S(1)} %add_rsqrt_fusion), kind=kOutput, calls=%fused_computation.17 | convolution fusion | flops 3358720000 | bytes 17060864 | tf_op jit(solution)/shard_map/dot_general | solution.py:78
  359.3 2.1 copy.52
  363.4 1.5 copy-done
  366.0 2.5 copy.62
  368.4 2.3 fusion.15
  370.8 2.3 all-gather.12.cloned.1.call-done
  373.0 25.3 %all-gather.14.cloned.1.call-done = bf16[1024,512]{0,1:T(8,128)(2,1)} async-done(((bf16[128,512]{0,1:T(8,128)(2,1)}), bf16[1024,512]{0,1:T(8,128)(2,1)}) %all-gather.14.cloned.1.call-update) | async-done | bytes 1048592 | tf_op jit(solution)/shard_map/all_gather | solution.py:110
  398.3 46.1 %while.17 = (s32[]{:T(128)}, f32[4,5,256]{2,1,0:T(8,128)S(1)}, f32[4,5,256]{2,1,0:T(8,128)S(1)}, f32[4,5,256,128]{3,2,1,0:T(8,128)S(1)}, s32[20,2,4]{0,2,1:T(4,1...) while((s32[]{:T(128)}, f32[4,5,256]{2,1,0:T(8,128)S(1)}, ...), condition=%wide.region_7.8_spmd, body=%wide.region_3.7_spmd.sunk | while | flops 343419168 | bytes 15574043 | solution.py:141
  399.7 1.9 fusion.51
  402.3 1.8 multiply_add_fusion.8
  405.5 1.9 fusion.51
  408.1 1.8 multiply_add_fusion.8
  411.3 1.9 fusion.51
  413.8 1.8 multiply_add_fusion.8
  417.0 1.9 fusion.51
  419.6 1.8 multiply_add_fusion.8
  422.8 1.9 fusion.51
  425.4 1.8 multiply_add_fusion.8
  428.6 1.9 fusion.51
  431.2 1.8 multiply_add_fusion.8
  434.4 1.9 fusion.51
  436.9 1.8 multiply_add_fusion.8
  440.1 1.9 fusion.51
  442.7 1.8 multiply_add_fusion.8
  444.5 2.1 copy.63
  446.6 2.0 broadcast_divide_fusion
  448.6 2.1 copy.64
  (153 shorter events, 25.9 us)
Async XLA Ops:
  7.2 2.4 copy-start.4
  7.2 3.2 copy-start.5
  7.2 4.7 %copy-start.7 = (bf16[2560]{0:T(1024)(128)(2,1)S(1)}, bf16[2560]{0:T(1024)(128)(2,1)}, u32[]{:S(2)}) copy-start(bf16[2560]{0:T(1024)(128)(2,1)} %param.17) | copy-start | bytes 15364
  7.2 4.7 %copy-start.2 = (bf16[256,2560]{1,0:T(8,128)(2,1)S(1)}, bf16[256,2560]{1,0:T(8,128)(2,1)}, u32[]{:S(2)}) copy-start(bf16[256,2560]{1,0:T(8,128)(2,1)} %param.16) | copy-start | bytes 3932164
  7.2 59.9 %all-gather.6.cloned.1.call-start = ((), (), s32[]{:S(2)}) async-start(), calls=%async_computation | async-start | bytes 3276800 | tf_op jit(solution)/shard_map/all_gather | solution.py:74
  7.9 114.4 %all-gather.10.cloned.1.call-start = ((), (), s32[]{:S(2)}) async-start(), calls=%async_computation.2 | async-start | bytes 3276800 | tf_op jit(solution)/shard_map/all_gather | solution.py:75
  8.7 3.6 copy-start.8
  8.7 3.6 copy-start.11
  8.7 3.6 copy-start.12
  8.7 3.6 copy-start.13
  8.7 3.6 copy-start.14
  8.8 4.2 copy-start.9
  8.8 4.2 copy-start.10
  8.8 340.7 %all-gather.8.cloned.1.call-start = ((), (), s32[]{:S(2)}) async-start(), calls=%async_computation.1 | async-start | bytes 16384000 | tf_op jit(solution)/shard_map/all_gather | solution.py:73
  9.5 363.5 %all-gather.12.cloned.1.call-start = ((), (), s32[]{:S(2)}) async-start(), calls=%async_computation.3 | async-start | bytes 1179648 | tf_op jit(solution)/shard_map/all_gather | solution.py:109
  10.4 388.0 %all-gather.14.cloned.1.call-start = ((), (), s32[]{:S(2)}) async-start(), calls=%async_computation.4 | async-start | bytes 1179648 | tf_op jit(solution)/shard_map/all_gather | solution.py:110
  125.0 224.5 %copy-start.3 = (f32[256,512]{1,0:T(8,128)}, f32[256,512]{1,0:T(8,128)S(1)}, u32[]{:S(2)}) copy-start(f32[256,512]{1,0:T(8,128)S(1)} %convolution_add_fusion.1) | copy-start | bytes 1572868
  361.9 1.4 copy-start.1
  363.4 1.5 copy-start
  366.0 32.4 %copy-start.6 = (s32[20,2,4]{0,2,1:T(4,128)S(1)}, s32[20,2,4]{0,2,1:T(4,128)}, u32[]{:S(2)}) copy-start(s32[20,2,4]{0,2,1:T(4,128)} %param.26) | copy-start | bytes 1924
Sparse Core Ops, SparseCore 0:
  9.6 57.4 all-gather.5
  68.7 53.5 all-gather.9
  123.9 225.5 all-gather.7
  351.2 21.7 all-gather.11
  374.7 23.5 all-gather.13
where the time goes:
time: 458 us; the launch traced here: 457 us
  waiting for transfers between devices  359 us (78%)
  matrix products  45.9 us (10%)
  local copies, waits for them, and re-layouts  25 us (5%)
  between operations  14.8 us (3%)
  other arithmetic  11.8 us (3%)
    all_gather x1, waiting for transfers between devices, on_device(): lax.all_gather(w_query, 'grp', axis=0, tiled=True)  224 us
    all_gather x1, waiting for transfers between devices, on_device(): lax.all_gather(w_key, 'grp', axis=0, tiled=True)  54.2 us
    all_gather x1, waiting for transfers between devices, on_device(): lax.all_gather(w_value, 'grp', axis=0, tiled=True)  51.4 us
    all_gather x1, waiting for transfers between devices, on_device(): piece_values = lax.all_gather(cache_values, 'ctx', axis=0, tiled=True)  25.3 us
    dot_general x8, matrix products, one_key_block(): jnp.einsum('rkgd,pkd->kgrp', query_heads, block_keys) * score_scale  15.3 us
    dot_general x3, matrix products, on_device(): jnp.dot(normed, panel, preferred_element_type=jnp.float32)  15 us
    dot_general x8, matrix products, one_key_block(): jnp.einsum('kgrp,pkd->kgrd', weights, block_values)  14.2 us
  transfers between devices with their start and end apart: 5, of which 5 were waited for; matrix products, arithmetic and copies ran while one was open for 6% of the time, Pallas kernels for 0%

commit v1 on v0

v1 whole, which is shorter than its diff:
```python
import functools

import jax
import jax.numpy as jnp
import numpy as np
from jax import lax
from jax.experimental import pallas as pl
from jax.experimental.pallas import tpu as pltpu
from jax.sharding import PartitionSpec as P

HD = 128
GROUP = 5
QBLK = 128
SEL = 4
TEAM = 4

norm_eps = 1e-06
rope_base = 10000000.0

CHUNKS = ((0, 2), (2, 4), (4, 6), (6, 7))


def angle_tables(head_dim):
    half_dim = head_dim // 2
    frequency = rope_base ** (-2.0 * np.arange(half_dim) / head_dim)
    return np.stack(
        [np.mod(frequency * 32.0**digit_level, 2.0 * np.pi) for digit_level in range(4)]
    )


def rope_tables(positions):
    tables = jnp.asarray(np.tile(angle_tables(HD), (1, 2)), jnp.float32)
    angles = jnp.zeros((positions.shape[0], HD), jnp.float32)
    remaining = positions
    for digit_level in range(4):
        digit_value = (remaining % 32).astype(jnp.float32)
        angles = angles + digit_value[:, None] * tables[digit_level][None, :]
        remaining = remaining // 32
    sign = jnp.where(jnp.arange(HD) < HD // 2, -1.0, 1.0).astype(jnp.float32)
    return jnp.cos(angles), jnp.sin(angles) * sign


def swap(value, axis, bit):
    size = lax.axis_size(axis)
    return lax.ppermute(value, axis, [(i, i ^ bit) for i in range(size)])


def bits_of(size, low):
    bits = []
    bit = low
    while bit < size:
        bits.append(bit)
        bit *= 2
    return bits[::-1]


def turned(value, cosine, sine):
    return value * cosine + pltpu.roll(value, HD // 2, 1) * sine


def heads_kernel(tiles, piece_count, piece_rows, *refs):
    first_tile, last_tile = tiles
    has_kv = first_tile == 0
    query_first = max(first_tile, 2)
    query_count = last_tile - query_first
    width = (last_tile - first_tile) * HD
    refs = list(refs)

    def take(count):
        taken = refs[:count]
        del refs[:count]
        return taken

    (offsets_ref,) = take(1)
    if query_count:
        (lists_ref,) = take(1)
    x_refs = take(TEAM)
    piece_refs = take(piece_count)
    wq_ref, wk_ref, wv_ref = take(3)
    bias_ref, cosine_ref, sine_ref = take(3)
    if query_count:
        (cache_ref,) = take(1)
    if not has_kv:
        (kv_ref,) = take(1)
    if has_kv:
        kv_own_ref, kv_ref = take(2)
    if query_count:
        out_refs = take(TEAM)
    x_buf, w_buf, x_sem, w_sem = take(4)
    if query_count:
        q_buf, o_buf = take(2)

    rows = x_refs[0].shape[0]
    shard = wq_ref.shape[0]
    group = offsets_ref[0]
    local = pl.ds(pl.multiple_of(offsets_ref[1], 16), shard)
    copies = []
    if has_kv:
        column = pl.ds(pl.multiple_of(group * HD, HD), HD)
        copies.append((wk_ref.at[:, column], w_buf.at[local, pl.ds(0, HD)]))
        copies.append((wv_ref.at[:, column], w_buf.at[local, pl.ds(HD, HD)]))
    if query_count:
        column = pl.ds(
            pl.multiple_of((group * GROUP + query_first - 2) * HD, HD), query_count * HD
        )
        copies.append(
            (
                wq_ref.at[:, column],
                w_buf.at[local, pl.ds((query_first - first_tile) * HD, query_count * HD)],
            )
        )
    for index, piece in enumerate(piece_refs):
        start = pl.multiple_of(offsets_ref[2 + index], 16)
        copies.append((piece, w_buf.at[pl.ds(start, piece_rows), :]))
    copies = [
        pltpu.make_async_copy(source, target, w_sem.at[index])
        for index, (source, target) in enumerate(copies)
    ]
    x_copies = [
        pltpu.make_async_copy(x_refs[r], x_buf.at[pl.ds(r * rows, rows), :], x_sem.at[r])
        for r in range(TEAM)
    ]
    for copy in copies:
        copy.start()
    for copy in x_copies:
        copy.start()
    for copy in copies:
        copy.wait()
    for r in range(TEAM):
        x_copies[r].wait()
        span = pl.ds(r * rows, rows)
        lin = (
            jnp.dot(x_buf[span, :], w_buf[...], preferred_element_type=jnp.float32)
            + bias_ref[...]
        )
        cosine, sine = cosine_ref[span, :], sine_ref[span, :]
        for tile in range(first_tile, last_tile):
            at = (tile - first_tile) * HD
            value = lin[:, at : at + HD]
            if tile != 1:
                value = turned(value, cosine, sine)
            if tile >= 2:
                q_buf[span, pl.ds((tile - query_first) * HD, HD)] = value.astype(jnp.bfloat16)
            else:
                kv_ref[span, pl.ds(at, HD)] = value.astype(jnp.bfloat16)
                if r == 0:
                    kv_own_ref[:, pl.ds(at, HD)] = value
    if not query_count:
        return

    scale = HD ** (-0.5)
    causal = lax.broadcasted_iota(jnp.int32, (QBLK, QBLK), 0) >= lax.broadcasted_iota(
        jnp.int32, (QBLK, QBLK), 1
    )
    blocks = TEAM * rows // QBLK
    contract_last = (((1,), (1,)), ((), ()))

    def one_block(block, carry):
        span = pl.ds(pl.multiple_of(block * QBLK, QBLK), QBLK)
        near_key = kv_ref[span, pl.ds(0, HD)]
        near_value = kv_ref[span, pl.ds(HD, HD)]
        for head in range(query_count):
            query = q_buf[span, pl.ds(head * HD, HD)]
            at = ((query_first - 2 + head) * blocks + block) * SEL
            slots = [lists_ref[at + j] for j in range(SEL)]
            places = [jnp.maximum(slot, 0) for slot in slots]
            keys = jnp.concatenate(
                [near_key] + [cache_ref[place, :, pl.ds(0, HD)] for place in places], axis=0
            )
            values = jnp.concatenate(
                [near_value] + [cache_ref[place, :, pl.ds(HD, HD)] for place in places], axis=0
            )
            scores = (
                lax.dot_general(query, keys, contract_last, preferred_element_type=jnp.float32)
                * scale
            )
            parts = [jnp.where(causal, scores[:, :QBLK], -jnp.inf)]
            for j in range(SEL):
                part = scores[:, (j + 1) * QBLK : (j + 2) * QBLK]
                parts.append(part + jnp.where(slots[j] >= 0, 0.0, -jnp.inf))
            top = functools.reduce(jnp.maximum, parts)
            top = jnp.max(top, axis=-1, keepdims=True)
            parts = [jnp.exp(part - top) for part in parts]
            total = jnp.sum(functools.reduce(jnp.add, parts), axis=-1, keepdims=True)
            weights = jnp.concatenate([part.astype(jnp.bfloat16) for part in parts], axis=1)
            mixed = jnp.dot(weights, values, preferred_element_type=jnp.float32)
            o_buf[span, pl.ds(head * HD, HD)] = mixed / total
        return carry

    lax.fori_loop(0, blocks, one_block, 0)
    for r in range(TEAM):
        out_refs[r][...] = o_buf[pl.ds(r * rows, rows), :].astype(out_refs[r].dtype)


def heads(tiles, offsets, lists, x_parts, pieces, weights, bias, cosine, sine, cache, kv):
    first_tile, last_tile = tiles
    has_kv = first_tile == 0
    query_count = last_tile - max(first_tile, 2)
    width = (last_tile - first_tile) * HD
    rows, depth = x_parts[0].shape
    everything = TEAM * rows
    smem = pl.BlockSpec(memory_space=pltpu.SMEM)
    hbm = pl.BlockSpec(memory_space=pl.ANY)
    vmem = pl.BlockSpec(memory_space=pltpu.VMEM)
    operands, specs = [offsets], [smem]

    def add(values, spec):
        operands.extend(values)
        specs.extend([spec] * len(values))

    if query_count:
        add([lists], smem)
    add(x_parts, hbm)
    add(pieces, hbm)
    add(weights, hbm)
    add([bias, cosine, sine], vmem)
    if query_count:
        add([cache], vmem)
    if not has_kv:
        add([kv], vmem)
    shapes = []
    if has_kv:
        shapes.append(jax.ShapeDtypeStruct((rows, 2 * HD), jnp.float32))
        shapes.append(jax.ShapeDtypeStruct((everything, 2 * HD), jnp.bfloat16))
    if query_count:
        for r in range(TEAM):
            dtype = jnp.float32 if r == 0 else jnp.bfloat16
            shapes.append(jax.ShapeDtypeStruct((rows, query_count * HD), dtype))
    scratch = [
        pltpu.VMEM((everything, depth), jnp.bfloat16),
        pltpu.VMEM((depth, width), jnp.bfloat16),
        pltpu.SemaphoreType.DMA((TEAM,)),
        pltpu.SemaphoreType.DMA((len(pieces) + 3,)),
    ]
    if query_count:
        scratch.append(pltpu.VMEM((everything, query_count * HD), jnp.bfloat16))
        scratch.append(pltpu.VMEM((everything, query_count * HD), jnp.float32))
    return pl.pallas_call(
        functools.partial(heads_kernel, tiles, len(pieces), pieces[0].shape[0]),
        out_shape=shapes,
        in_specs=specs,
        out_specs=[vmem] * len(shapes),
        scratch_shapes=scratch,
        compiler_params=pltpu.CompilerParams(vmem_limit_bytes=48 * 1024 * 1024),
        cost_estimate=pl.CostEstimate(
            flops=2 * everything * depth * width,
            bytes_accessed=2 * depth * (everything + width),
            transcendentals=everything * query_count * (SEL + 1) * QBLK,
        ),
    )(*operands)


def finish_kernel(chunk_count, places_ref, *refs):
    kv_refs = refs[:TEAM]
    context_refs = refs[TEAM : TEAM + TEAM * chunk_count]
    context_ref, keys_ref, values_ref = refs[TEAM + TEAM * chunk_count :]
    for r in range(TEAM):
        place = places_ref[r]
        column = pl.ds(pl.multiple_of(place * HD, HD), HD)
        keys_ref[:, column] = kv_refs[r][:, pl.ds(0, HD)].astype(jnp.float32)
        values_ref[:, column] = kv_refs[r][:, pl.ds(HD, HD)].astype(jnp.float32)
        at = place * (GROUP * HD)
        for chunk in range(chunk_count):
            ref = context_refs[chunk * TEAM + r]
            wide = ref.shape[1]
            context_ref[:, pl.ds(pl.multiple_of(at, HD), wide)] = ref[...].astype(jnp.float32)
            at = at + wide


def finish(places, kv_parts, context_parts):
    rows = kv_parts[0].shape[0]
    vmem = pl.BlockSpec(memory_space=pltpu.VMEM)
    flat = list(kv_parts) + [part for chunk in context_parts for part in chunk]
    wide = TEAM * GROUP * HD
    return pl.pallas_call(
        functools.partial(finish_kernel, len(context_parts)),
        out_shape=[
            jax.ShapeDtypeStruct((rows, wide), jnp.float32),
            jax.ShapeDtypeStruct((rows, TEAM * HD), jnp.float32),
            jax.ShapeDtypeStruct((rows, TEAM * HD), jnp.float32),
        ],
        in_specs=[pl.BlockSpec(memory_space=pltpu.SMEM)] + [vmem] * len(flat),
        out_specs=[vmem] * 3,
        compiler_params=pltpu.CompilerParams(vmem_limit_bytes=32 * 1024 * 1024),
    )(places, *flat)


def on_device(
    tokens,
    norm_gain,
    w_query,
    w_key,
    w_value,
    b_query,
    b_key,
    b_value,
    cache_keys,
    cache_values,
    block_lists,
    start_position,
):
    rows = tokens.shape[0]
    shard = w_query.shape[0]
    ctx_size, grp_size = lax.axis_size("ctx"), lax.axis_size("grp")
    me, layer = lax.axis_index("ctx"), lax.axis_index("grp")
    group = me % TEAM
    side = me // TEAM
    sides = ctx_size // TEAM
    if (shard // sides) % 16:
        sides = 1
        side = side * 0
    piece_rows = shard // sides

    half_key = lax.dynamic_slice(w_key, (side * piece_rows, group * HD), (piece_rows, HD))
    half_value = lax.dynamic_slice(w_value, (side * piece_rows, group * HD), (piece_rows, HD))
    half_query = lax.dynamic_slice(
        w_query, (side * piece_rows, group * GROUP * HD), (piece_rows, GROUP * HD)
    )
    half = jnp.concatenate([half_key, half_value, half_query], axis=1)
    grp_bits = bits_of(grp_size, 1)
    side_bits = bits_of(ctx_size, TEAM) if sides > 1 else []
    chunk_pieces, piece_places = [], None
    for first_tile, last_tile in CHUNKS:
        held = {0: half[:, first_tile * HD : last_tile * HD]}
        for bit in grp_bits:
            for far in sorted(held):
                held[far ^ bit] = swap(held[far], "grp", bit)
        pieces = {(far, 0): held[far] for far in held if far}
        for bit in side_bits:
            for far, over in sorted(pieces):
                pieces[(far, over ^ (bit // TEAM))] = swap(pieces[(far, over)], "ctx", bit)
        order = sorted(pieces)
        chunk_pieces.append([pieces[key] for key in order])
        piece_places = order
    offsets = jnp.stack(
        [group, layer * shard]
        + [(layer ^ far) * shard + (side ^ over) * piece_rows for far, over in piece_places]
    ).astype(jnp.int32)

    widened = tokens.astype(jnp.float32)
    normed = (
        widened
        * lax.rsqrt(jnp.mean(widened * widened, axis=-1, keepdims=True) + norm_eps)
        * norm_gain.astype(jnp.float32)
    ).astype(jnp.bfloat16)
    normed_two = swap(normed, "ctx", 2)
    x_parts = [normed, swap(normed, "ctx", 1), normed_two, swap(normed_two, "ctx", 1)]

    lists_two = swap(block_lists, "ctx", 2)
    list_parts = [
        block_lists,
        swap(block_lists, "ctx", 1),
        lists_two,
        swap(lists_two, "ctx", 1),
    ]
    lists = jnp.concatenate(
        [lax.dynamic_slice_in_dim(part, group * GROUP, GROUP, 0) for part in list_parts], axis=1
    )

    prefix = cache_keys.shape[0]
    store = jnp.concatenate(
        [
            cache_keys.reshape(prefix, TEAM, HD).transpose(1, 0, 2),
            cache_values.reshape(prefix, TEAM, HD).transpose(1, 0, 2),
        ],
        axis=2,
    )[:, None]
    distances = [0]
    for bit in bits_of(ctx_size, TEAM):
        store = jnp.concatenate([store, swap(store, "ctx", bit)], axis=1)
        distances = distances + [distance ^ bit for distance in distances]
    for bit, keep in ((2, 2), (1, 1)):
        mine = (me // bit) % 2
        kept = lax.dynamic_slice_in_dim(store, mine * keep, keep, 0)
        sent = lax.dynamic_slice_in_dim(store, (1 - mine) * keep, keep, 0)
        store = jnp.concatenate([kept, swap(sent, "ctx", bit)], axis=1)
        distances = distances + [distance ^ bit for distance in distances]
    blocks_each = prefix // QBLK
    cache = store.reshape(ctx_size * blocks_each, QBLK, 2 * HD)
    place_of = np.zeros((ctx_size,), np.int32)
    place_of[np.asarray(distances)] = np.arange(ctx_size)
    owner = jnp.maximum(lists, 0) // blocks_each
    place = jnp.zeros_like(owner)
    for distance in range(ctx_size):
        place = jnp.where((owner ^ me) == distance, int(place_of[distance]), place)
    place = place * blocks_each + jnp.maximum(lists, 0) % blocks_each
    lists = jnp.where(lists >= 0, place, -1).reshape(-1).astype(jnp.int32)

    positions = jnp.concatenate(
        [
            start_position[0]
            + ((me ^ r) * grp_size + layer) * rows
            + jnp.arange(rows, dtype=jnp.int32)
            for r in range(TEAM)
        ]
    )
    cosine, sine = rope_tables(positions)
    bias = jnp.concatenate(
        [
            lax.dynamic_slice_in_dim(b_key, group * HD, HD),
            lax.dynamic_slice_in_dim(b_value, group * HD, HD),
            lax.dynamic_slice_in_dim(b_query, group * GROUP * HD, GROUP * HD),
        ]
    ).astype(jnp.float32)[None, :]

    kv, kv_parts, context_parts = None, None, []
    for tiles, pieces in zip(CHUNKS, chunk_pieces):
        first_tile, last_tile = tiles
        results = heads(
            tiles,
            offsets,
            lists,
            x_parts,
            pieces,
            (w_query, w_key, w_value),
            bias[:, first_tile * HD : last_tile * HD],
            cosine,
            sine,
            cache,
            kv,
        )
        if first_tile == 0:
            kv_own, kv = results[:2]
            results = results[2:]
            kv_parts = [kv_own] + [
                swap(kv[r * rows : (r + 1) * rows], "ctx", r) for r in range(1, TEAM)
            ]
        if results:
            context_parts.append(
                [results[0]] + [swap(results[r], "ctx", r) for r in range(1, TEAM)]
            )
    places = jnp.stack([group ^ r for r in range(TEAM)]).astype(jnp.int32)
    return tuple(finish(places, kv_parts, context_parts))


def solution(mesh):
    in_specs = (
        P(("ctx", "grp"), None),
        P(),
        P("grp", None),
        P("grp", None),
        P("grp", None),
        P(),
        P(),
        P(),
        P("ctx", None),
        P("ctx", None),
        P(None, ("ctx", "grp"), None),
        P(),
    )
    out_specs = (P(("ctx", "grp"), None), P(("ctx", "grp"), None), P(("ctx", "grp"), None))
    return jax.shard_map(
        on_device, mesh=mesh, in_specs=in_specs, out_specs=out_specs, check_vma=False
    )
```

time: 458 us -> 169 us (0.37)
  waiting for transfers between devices: 359 us -> 36.6 us
  starting transfers between devices: 0.19 us -> 50.9 us
  matrix products: 45.9 us -> 0 us
  Pallas kernels: 0 us -> 43.5 us
  between operations: 14.8 us -> 1.69 us
    all_gather x5 -> x0, waiting for transfers between devices: 357 us -> none  [the longest x1 224 us: on_device(): lax.all_gather(w_query, 'grp', axis=0, tiled=True)]
    ppermute x0 -> x45, starting transfers between devices: none -> 50.9 us  [swap(): return lax.ppermute(value, axis, [(i, i ^ bit) for i in range(size)])]
    dot_general x21 -> x0, matrix products: 45.9 us -> none  [the longest x8 15.3 us: one_key_block(): jnp.einsum('rkgd,pkd->kgrp', query_heads, block_keys) * score_scale]
    pallas_call x0 -> x5, Pallas kernels: none -> 43.5 us  [the longest x4 40.8 us: heads(): pl.pallas_call(functools.partial(heads_kernel, tiles, len(pieces), pieces...]
    ppermute x0 -> x45, waiting for transfers between devices: none -> 36.6 us  [swap(): return lax.ppermute(value, axis, [(i, i ^ bit) for i in range(size)])]
    reduce_sum x9 -> x0, other arithmetic: 7.18 us -> none  [the longest x8 4.87 us: one_key_block(): new_total = old_total * factor + jnp.sum(weights, axis=-1)]
    unnamed x34 -> x60, local copies, waits for them, and re-layouts: 6.05 us -> 11.3 us
    dynamic_slice x8 -> x7, local copies, waits for them, and re-layouts: 7.96 us -> 3.31 us  [the longest x4 1.64 us: on_device(): lax.dynamic_slice_in_dim(part, group * GROUP, GROUP, 0)]
  transfers between devices with their start and end apart: 5 -> 45, of which waited for: 5 -> 15; matrix products, arithmetic and copies ran while one was open for 6% -> 14% of each run, Pallas kernels for 0% -> 24%
where the time goes in v1:
time: 169 us
  starting transfers between devices  50.9 us (30%)
  Pallas kernels  43.5 us (26%)
  waiting for transfers between devices  36.6 us (22%)
  local copies, waits for them, and re-layouts  22.4 us (13%)
  other arithmetic  13.6 us (8%)
  between operations  1.69 us (1%)
    ppermute x45, starting transfers between devices, swap(): return lax.ppermute(value, axis, [(i, i ^ bit) for i in range(size)])  50.9 us
    pallas_call x4, Pallas kernels, heads(): pl.pallas_call(functools.partial(heads_kernel, tiles, len(pieces), pieces...  40.8 us
    ppermute x45, waiting for transfers between devices, swap(): return lax.ppermute(value, axis, [(i, i ^ bit) for i in range(size)])  36.6 us
    unnamed x60, local copies, waits for them, and re-layouts  11.3 us
  transfers between devices with their start and end apart: 45, of which 15 were waited for; matrix products, arithmetic and copies ran while one was open for 14% of the time, Pallas kernels for 24%

profile of v1, /device:TPU:0, one launch (start us, length us, event | category | flops | bytes accessed | tf_op | source)
XLA Modules:
  0.0 168.7 jit_solution(2559685613880040278)
XLA Ops:
  1.5 1.7 fusion
  3.1 1.7 fusion.2.refs_1_.refs_2_
  4.9 3.0 %collective-permute-start.1 = (bf16[256,2560]{1,0:T(8,128)(2,1)S(1)}, bf16[256,2560]{1,0:T(8,128)(2,1)}, u32[]{:S(2)}, u32[]{:S(2)}) collective-permute-start(bf16[256,2560]{1,0:T(8,128)(2,1)S(1)} %fusion.2.refs_1_.refs_2_), channel_id=1, source_target_pairs={{0,8},{4,12},{8,0},{12,4},{16,24},{20,28},{24,16},{28,20},{1,9},{5... | collective-permute-start | bytes 3932168 | tf_op jit(solution)/shard_map/ppermute | solution.py:45
  9.5 2.6 %collective-permute-start.5 = (bf16[320,256]{1,0:T(8,128)(2,1)}, bf16[320,256]{1,0:T(8,128)(2,1)S(1)}, u32[]{:S(2)}, u32[]{:S(2)}) collective-permute-start(bf16[320,256]{1,0:T(8,128)(2,1)} %pad_maximum_fusion), channel_id=1, source_target_pairs={{0,2},{1,3},{2,0},{3,1},{4,6},{5,7},{6,4},{7,5},{8,10},{9,11},{10,... | collective-permute-start | bytes 491528 | tf_op jit(solution)/shard_map/ppermute | solution.py:45
  15.0 2.0 %sine_multiply_fusion = (f32[1024,128]{1,0:T(8,128)S(1)}, f32[1024,128]{1,0:T(8,128)S(1)}) fusion(f32[128]{0:T(128)S(1)} %compare_select_fusion, f32[128]{0:T(128)S(1)} %copy-done.26, f32[1024]{0:T(1024)S(1)} %get-tuple-element.44, f32[128]{0:T(128)S(1)} %copy-done.25, f32[1024]{0:T(1024)S(1)} %get-tuple-element.43, f32[128]{0:T(128)S(1)} %copy-done.24, ...), kind=kLoop, calls=%fused_computation.14 | loop fusion | flops 1048576 | bytes 1067520 | tf_op jit(solution)/shard_map/mul | solution.py:40
  17.0 1.7 %fusion.19 = (bf16[320,256]{1,0:T(8,128)(2,1)}, bf16[320,256]{1,0:T(8,128)(2,1)}) fusion(bf16[640,2560]{1,0:T(8,128)(2,1)} %refs_12_.7, s32[]{:T(128)S(6)} %select_n.182, s32[]{:T(128)S(6)} %add.282, s32[]{:T(128)S(6)} %select_n.184), kind=kLoop, calls=%fused_computation.74 | loop fusion | bytes 655372 | tf_op jit(solution)/shard_map/slice | solution.py:324
  18.7 1.7 copy.17
  20.4 1.7 copy.18
  22.0 1.7 copy.19
  23.7 1.7 copy.20
  25.4 11.4 %collective-permute-done.13 = s32[20,2,4]{0,2,1:T(4,128)S(1)} collective-permute-done((s32[20,2,4]{0,2,1:T(4,128)S(1)}, s32[20,2,4]{0,2,1:T(4,128)S(1)}, u32[]{:S(2)}, u32[]{:S(2)}) %collective-permute-start.13) | collective-permute-done | bytes 672 | tf_op jit(solution)/shard_map/ppermute | solution.py:45
  36.8 1.7 %maximum_bitcast_fusion.1 = bf16[4,1,128,256]{3,2,1,0:T(8,128)(2,1)} fusion(bf16[4,128,128]{2,1,0:T(8,128)(2,1)} %bitcast.31, bf16[4,128,128]{2,1,0:T(8,128)(2,1)} %bitcast.30), kind=kLoop, calls=%fused_computation.21 | loop fusion | flops 524288 | bytes 524288 | tf_op jit(solution)/shard_map/broadcast_in_dim | solution.py:361
  39.4 2.9 %collective-permute-start.38 = (bf16[320,128]{1,0:T(8,128)(2,1)S(1)}, bf16[320,128]{1,0:T(8,128)(2,1)S(1)}, u32[]{:S(2)}, u32[]{:S(2)}) collective-permute-start(bf16[320,128]{1,0:T(8,128)(2,1)S(1)} %dynamic-slice.2), channel_id=1, source_target_pairs={{0,2},{1,3},{2,0},{3,1},{4,6},{5,7},{6,4},{7,5},{8,10},{9,11},{10,... | collective-permute-start | bytes 245768 | tf_op jit(solution)/shard_map/ppermute | solution.py:45
  44.8 2.5 %collective-permute-done.38.refs_8_ = bf16[320,128]{1,0:T(8,128)(2,1)S(1)} collective-permute-done((bf16[320,128]{1,0:T(8,128)(2,1)S(1)}, bf16[320,128]{1,0:T(8,128)(2,1)S(1)}, u32[]{:S(2)}, u32[]{:S(2)}) %collective-permute-start.38) | collective-permute-done | bytes 81952 | tf_op jit(solution)/shard_map/ppermute | solution.py:45
  50.5 2.7 %collective-permute-start.40 = (bf16[320,128]{1,0:T(8,128)(2,1)S(1)}, bf16[320,128]{1,0:T(8,128)(2,1)}, u32[]{:S(2)}, u32[]{:S(2)}) collective-permute-start(bf16[320,128]{1,0:T(8,128)(2,1)S(1)} %collective-permute-done.38.refs_8_), channel_id=1, source_target_pairs={{0,1},{1,0},{2,3},{3,2},{4,5},{5,4},{6,7},{7,6},{8,9},{9,8},{10,11... | collective-permute-start | bytes 245768 | tf_op jit(solution)/shard_map/ppermute | solution.py:45
  53.2 3.4 %collective-permute-done.40.refs_10_ = bf16[320,128]{1,0:T(8,128)(2,1)} collective-permute-done((bf16[320,128]{1,0:T(8,128)(2,1)S(1)}, bf16[320,128]{1,0:T(8,128)(2,1)}, u32[]{:S(2)}, u32[]{:S(2)}) %collective-permute-start.40) | collective-permute-done | bytes 81952 | tf_op jit(solution)/shard_map/ppermute | solution.py:45
  58.6 1.9 %fusion.6 = (bf16[2,2,128,256]{3,2,1,0:T(8,128)(2,1)}, bf16[2,2,128,256]{3,2,1,0:T(8,128)(2,1)}) fusion(s32[]{:T(128)S(6)} %select_n.207, bf16[4,1,128,256]{3,2,1,0:T(8,128)(2,1)} %maximum_bitcast_fusion.1, bf16[4,1,128,256]{3,2,1,0:T(8,128)(2,1)} %collective-permute-done.21, s32[]{:T(128)S(6)} %select_n.206), kind=kLoop, calls=%fused_computation.19 | loop fusion | flops 262144 | bytes 1048584 | tf_op jit(solution)/shard_map/concatenate | solution.py:370
  60.6 1.9 %collective-permute-done.37.refs_7_ = bf16[320,128]{1,0:T(8,128)(2,1)S(1)} collective-permute-done((bf16[320,128]{1,0:T(8,128)(2,1)S(1)}, bf16[320,128]{1,0:T(8,128)(2,1)S(1)}, u32[]{:S(2)}, u32[]{:S(2)}) %collective-permute-start.37) | collective-permute-done | bytes 81952 | tf_op jit(solution)/shard_map/ppermute | solution.py:45
  63.0 2.6 %collective-permute-start.27 = (bf16[320,256]{1,0:T(8,128)(2,1)}, bf16[320,256]{1,0:T(8,128)(2,1)}, u32[]{:S(2)}, u32[]{:S(2)}) collective-permute-start(bf16[320,256]{1,0:T(8,128)(2,1)} %get-tuple-element.31), channel_id=1, source_target_pairs={{0,1},{1,0},{2,3},{3,2},{4,5},{5,4},{6,7},{7,6},{8,9},{9,8},{10,11... | collective-permute-start | bytes 491528 | tf_op jit(solution)/shard_map/ppermute | solution.py:45
  68.9 1.7 %collective-permute-done.27.refs_6_ = bf16[320,256]{1,0:T(8,128)(2,1)} collective-permute-done((bf16[320,256]{1,0:T(8,128)(2,1)}, bf16[320,256]{1,0:T(8,128)(2,1)}, u32[]{:S(2)}, u32[]{:S(2)}) %collective-permute-start.27) | collective-permute-done | bytes 163872 | tf_op jit(solution)/shard_map/ppermute | solution.py:45
  70.6 2.5 %collective-permute-start.15 = (bf16[320,256]{1,0:T(8,128)(2,1)}, bf16[320,256]{1,0:T(8,128)(2,1)S(1)}, u32[]{:S(2)}, u32[]{:S(2)}) collective-permute-start(bf16[320,256]{1,0:T(8,128)(2,1)} %get-tuple-element.32), channel_id=1, source_target_pairs={{0,1},{1,0},{2,3},{3,2},{4,5},{5,4},{6,7},{7,6},{8,9},{9,8},{10,11... | collective-permute-start | bytes 491528 | tf_op jit(solution)/shard_map/ppermute | solution.py:45
  74.3 3.0 %collective-permute-start.7 = (bf16[320,256]{1,0:T(8,128)(2,1)S(1)}, bf16[320,256]{1,0:T(8,128)(2,1)}, u32[]{:S(2)}, u32[]{:S(2)}) collective-permute-start(bf16[320,256]{1,0:T(8,128)(2,1)S(1)} %collective-permute-done.5.refs_7_), channel_id=1, source_target_pairs={{0,1},{1,0},{2,3},{3,2},{4,5},{5,4},{6,7},{7,6},{8,9},{9,8},{10,11... | collective-permute-start | bytes 491528 | tf_op jit(solution)/shard_map/ppermute | solution.py:45
  78.5 1.9 %fusion.5 = (bf16[1,4,128,256]{3,2,1,0:T(8,128)(2,1)}, bf16[1,4,128,256]{3,2,1,0:T(8,128)(2,1)}) fusion(s32[]{:T(128)S(6)} %select_n.209, bf16[2,2,128,256]{3,2,1,0:T(8,128)(2,1)} %get-tuple-element.36, bf16[2,2,128,256]{3,2,1,0:T(8,128)(2,1)} %collective-permute-done.22, s32[]{:T(128)S(6)} %select_n.210), kind=kLoop, calls=%fused_computation.18 | loop fusion | flops 262144 | bytes 1048584 | tf_op jit(solution)/shard_map/concatenate | solution.py:376
  100.2 6.3 %shard_map.148 = (f32[256,256]{1,0:T(8,128)S(1)}, bf16[1024,256]{1,0:T(8,128)(2,1)S(1)}) custom-call(s32[8]{0:T(128)S(1)} %stack.52.refs_0_, bf16[256,2560]{1,0:T(8,128)(2,1)S(1)} %fusion.2.refs_1_.refs_2_, bf16[256,2560]{1,0:T(8,128)(2,1)} %collective-permute-done.refs_2_.refs_3_, bf16[256,2560]{1,0:T(8,128)(2,1)} %collective-permute-done.1.refs_3_.refs_4_, ...), custom_call_target="tpu_custom_call" | custom-call | flops 1342177280 | bytes 6553600 | tf_op jit(solution)/shard_map/pallas_call | solution.py:238
  109.7 8.3 %shard_map.151 = (f32[256,128]{1,0:T(8,128)S(1)}, bf16[256,128]{1,0:T(8,128)(2,1)S(1)}, bf16[256,128]{1,0:T(8,128)(2,1)S(1)}, bf16[256,128]{1,0:T(8,128)(2,1)S(1)}) custom-call(s32[8]{0:T(128)S(1)} %stack.52.refs_0_, s32[160]{0:T(256)S(1)} %reshape.433.refs_1_, bf16[256,2560]{1,0:T(8,128)(2,1)S(1)} %fusion.2.refs_1_.refs_2_, ...), custom_call_target="tpu_custom_call" | custom-call | flops 671088640 | bytes 5898240 | tf_op jit(solution)/shard_map/pallas_call | solution.py:238
  119.7 12.6 %shard_map.150 = (f32[256,256]{1,0:T(8,128)S(1)}, bf16[256,256]{1,0:T(8,128)(2,1)S(1)}, bf16[256,256]{1,0:T(8,128)(2,1)S(1)}, bf16[256,256]{1,0:T(8,128)(2,1)S(1)}) custom-call(s32[8]{0:T(128)S(1)} %stack.52.refs_0_, s32[160]{0:T(256)S(1)} %reshape.433.refs_1_, bf16[256,2560]{1,0:T(8,128)(2,1)} %copy-done, ...), custom_call_target="tpu_custom_call" | custom-call | flops 1342177280 | bytes 6553600 | tf_op jit(solution)/shard_map/pallas_call | solution.py:238
  134.5 13.7 %shard_map.149 = (f32[256,256]{1,0:T(8,128)S(1)}, bf16[256,256]{1,0:T(8,128)(2,1)S(1)}, bf16[256,256]{1,0:T(8,128)(2,1)}, bf16[256,256]{1,0:T(8,128)(2,1)}) custom-call(s32[8]{0:T(128)S(1)} %stack.52.refs_0_, s32[160]{0:T(256)S(1)} %reshape.433.refs_1_, bf16[256,2560]{1,0:T(8,128)(2,1)} %copy-done, bf16[256,2560]{1,0:T(8,128)(2,1)} %collective-permute-done.refs_2_.refs_3_, ...), custom_call_target="tpu_custom_call" | custom-call | flops 1342177280 | bytes 6553600 | tf_op jit(solution)/shard_map/pallas_call | solution.py:238
  154.7 2.2 %collective-permute-done.25.refs_6_ = bf16[256,256]{1,0:T(8,128)(2,1)S(1)} collective-permute-done((bf16[256,256]{1,0:T(8,128)(2,1)}, bf16[256,256]{1,0:T(8,128)(2,1)S(1)}, u32[]{:S(2)}, u32[]{:S(2)}) %collective-permute-start.25) | collective-permute-done | bytes 131104 | tf_op jit(solution)/shard_map/ppermute | solution.py:45
  156.9 2.7 %collective-permute-done.26.refs_7_ = bf16[256,256]{1,0:T(8,128)(2,1)S(1)} collective-permute-done((bf16[256,256]{1,0:T(8,128)(2,1)}, bf16[256,256]{1,0:T(8,128)(2,1)S(1)}, u32[]{:S(2)}, u32[]{:S(2)}) %collective-permute-start.26) | collective-permute-done | bytes 131104 | tf_op jit(solution)/shard_map/ppermute | solution.py:45
  159.6 3.0 %collective-permute-done.10.refs_2_ = bf16[256,256]{1,0:T(8,128)(2,1)S(1)} collective-permute-done((bf16[256,256]{1,0:T(8,128)(2,1)S(1)}, bf16[256,256]{1,0:T(8,128)(2,1)S(1)}, u32[]{:S(2)}, u32[]{:S(2)}) %collective-permute-start.10) | collective-permute-done | bytes 131104 | tf_op jit(solution)/shard_map/ppermute | solution.py:45
  162.5 2.7 %collective-permute-done.11.refs_3_ = bf16[256,256]{1,0:T(8,128)(2,1)S(1)} collective-permute-done((bf16[256,256]{1,0:T(8,128)(2,1)S(1)}, bf16[256,256]{1,0:T(8,128)(2,1)S(1)}, u32[]{:S(2)}, u32[]{:S(2)}) %collective-permute-start.11) | collective-permute-done | bytes 131104 | tf_op jit(solution)/shard_map/ppermute | solution.py:45
  166.0 2.7 %shard_map.152 = (f32[256,2560]{1,0:T(8,128)}, f32[256,512]{1,0:T(8,128)}, f32[256,512]{1,0:T(8,128)}) custom-call(s32[4]{0:T(128)S(1)} %pad_add_fusion.2.places_ref, f32[256,256]{1,0:T(8,128)S(1)} %get-tuple-element.17.refs_0_, bf16[256,256]{1,0:T(8,128)(2,1)S(1)} %collective-permute-done.9.refs_1_, bf16[256,256]{1,0:T(8,128)(2,1)S(1)} %collective-permute-done.10.refs_2_, ...), custom_call_target="tpu_custom_call" | custom-call | tf_op jit(solution)/shard_map/pallas_call | solution.py:275
  (159 shorter events, 53.6 us)
Async XLA Ops:
  4.9 44.3 %collective-permute-start.1 = (bf16[256,2560]{1,0:T(8,128)(2,1)S(1)}, bf16[256,2560]{1,0:T(8,128)(2,1)}, u32[]{:S(2)}, u32[]{:S(2)}) collective-permute-start(bf16[256,2560]{1,0:T(8,128)(2,1)S(1)} %fusion.2.refs_1_.refs_2_), channel_id=1, source_target_pairs={{0,8},{4,12},{8,0},{12,4},{16,24},{20,28},{24,16},{28,20},{1,9},{5... | collective-permute-start | bytes 3932168 | tf_op jit(solution)/shard_map/ppermute | solution.py:45
  9.5 39.7 %collective-permute-start.5 = (bf16[320,256]{1,0:T(8,128)(2,1)}, bf16[320,256]{1,0:T(8,128)(2,1)S(1)}, u32[]{:S(2)}, u32[]{:S(2)}) collective-permute-start(bf16[320,256]{1,0:T(8,128)(2,1)} %pad_maximum_fusion), channel_id=1, source_target_pairs={{0,2},{1,3},{2,0},{3,1},{4,6},{5,7},{6,4},{7,5},{8,10},{9,11},{10,... | collective-permute-start | bytes 491528 | tf_op jit(solution)/shard_map/ppermute | solution.py:45
  12.1 38.4 %collective-permute-start.3 = (bf16[320,256]{1,0:T(8,128)(2,1)}, bf16[320,256]{1,0:T(8,128)(2,1)S(1)}, u32[]{:S(2)}, u32[]{:S(2)}) collective-permute-start(bf16[320,256]{1,0:T(8,128)(2,1)} %pad_maximum_fusion), channel_id=1, source_target_pairs={{0,1},{1,0},{2,3},{3,2},{4,5},{5,4},{6,7},{7,6},{8,9},{9,8},{10,11... | collective-permute-start | bytes 491528 | tf_op jit(solution)/shard_map/ppermute | solution.py:45
  13.6 23.2 %collective-permute-start.13 = (s32[20,2,4]{0,2,1:T(4,128)S(1)}, s32[20,2,4]{0,2,1:T(4,128)S(1)}, u32[]{:S(2)}, u32[]{:S(2)}) collective-permute-start(s32[20,2,4]{0,2,1:T(4,128)S(1)} %copy-done.20), channel_id=1, source_target_pairs={{0,8},{4,12},{8,0},{12,4},{16,24},{20,28},{24,16},{28,20},{1,9},{5... | collective-permute-start | bytes 1928 | tf_op jit(solution)/shard_map/ppermute | solution.py:45
  14.2 25.2 %collective-permute-start.12 = (s32[20,2,4]{0,2,1:T(4,128)S(1)}, s32[20,2,4]{0,2,1:T(4,128)S(1)}, u32[]{:S(2)}, u32[]{:S(2)}) collective-permute-start(s32[20,2,4]{0,2,1:T(4,128)S(1)} %copy-done.20), channel_id=1, source_target_pairs={{0,4},{4,0},{8,12},{12,8},{16,20},{20,16},{24,28},{28,24},{1,5},{5... | collective-permute-start | bytes 1928 | tf_op jit(solution)/shard_map/ppermute | solution.py:45
  39.4 7.9 %collective-permute-start.38 = (bf16[320,128]{1,0:T(8,128)(2,1)S(1)}, bf16[320,128]{1,0:T(8,128)(2,1)S(1)}, u32[]{:S(2)}, u32[]{:S(2)}) collective-permute-start(bf16[320,128]{1,0:T(8,128)(2,1)S(1)} %dynamic-slice.2), channel_id=1, source_target_pairs={{0,2},{1,3},{2,0},{3,1},{4,6},{5,7},{6,4},{7,5},{8,10},{9,11},{10,... | collective-permute-start | bytes 245768 | tf_op jit(solution)/shard_map/ppermute | solution.py:45
  47.3 47.0 %collective-permute-start = (bf16[256,2560]{1,0:T(8,128)(2,1)S(1)}, bf16[256,2560]{1,0:T(8,128)(2,1)}, u32[]{:S(2)}, u32[]{:S(2)}) collective-permute-start(bf16[256,2560]{1,0:T(8,128)(2,1)S(1)} %fusion.2.refs_1_.refs_2_), channel_id=1, source_target_pairs={{0,4},{4,0},{8,12},{12,8},{16,20},{20,16},{24,28},{28,24},{1,5},{5... | collective-permute-start | bytes 3932168 | tf_op jit(solution)/shard_map/ppermute | solution.py:45
  47.5 9.6 %collective-permute-start.21 = (bf16[4,1,128,256]{3,2,1,0:T(8,128)(2,1)}, bf16[4,1,128,256]{3,2,1,0:T(8,128)(2,1)}, u32[]{:S(2)}, u32[]{:S(2)}) collective-permute-start(bf16[4,1,128,256]{3,2,1,0:T(8,128)(2,1)} %maximum_bitcast_fusion.1), channel_id=1, source_target_pairs={{0,16},{4,20},{8,24},{12,28},{16,0},{20,4},{24,8},{28,12},{1,17},{... | collective-permute-start | bytes 786440 | tf_op jit(solution)/shard_map/ppermute | solution.py:45
  49.1 46.3 %collective-permute-start.2 = (bf16[256,2560]{1,0:T(8,128)(2,1)}, bf16[256,2560]{1,0:T(8,128)(2,1)}, u32[]{:S(2)}, u32[]{:S(2)}) collective-permute-start(bf16[256,2560]{1,0:T(8,128)(2,1)} %collective-permute-done.1.refs_3_.refs_4_), channel_id=1, source_target_pairs={{0,4},{4,0},{8,12},{12,8},{16,20},{20,16},{24,28},{28,24},{1,5},{5... | collective-permute-start | bytes 3932168 | tf_op jit(solution)/shard_map/ppermute | solution.py:45
  49.1 18.1 %collective-permute-start.29 = (bf16[320,256]{1,0:T(8,128)(2,1)}, bf16[320,256]{1,0:T(8,128)(2,1)}, u32[]{:S(2)}, u32[]{:S(2)}) collective-permute-start(bf16[320,256]{1,0:T(8,128)(2,1)} %get-tuple-element.31), channel_id=1, source_target_pairs={{0,2},{1,3},{2,0},{3,1},{4,6},{5,7},{6,4},{7,5},{8,10},{9,11},{10,... | collective-permute-start | bytes 491528 | tf_op jit(solution)/shard_map/ppermute | solution.py:45
  56.6 9.0 %collective-permute-start.39 = (bf16[320,128]{1,0:T(8,128)(2,1)S(1)}, bf16[320,128]{1,0:T(8,128)(2,1)S(1)}, u32[]{:S(2)}, u32[]{:S(2)}) collective-permute-start(bf16[320,128]{1,0:T(8,128)(2,1)S(1)} %collective-permute-done.38.refs_8_), channel_id=1, source_target_pairs={{0,16},{4,20},{8,24},{12,28},{16,0},{20,4},{24,8},{28,12},{1,17},{... | collective-permute-start | bytes 245768 | tf_op jit(solution)/shard_map/ppermute | solution.py:45
  66.3 8.0 %collective-permute-start.17 = (bf16[320,256]{1,0:T(8,128)(2,1)}, bf16[320,256]{1,0:T(8,128)(2,1)}, u32[]{:S(2)}, u32[]{:S(2)}) collective-permute-start(bf16[320,256]{1,0:T(8,128)(2,1)} %get-tuple-element.32), channel_id=1, source_target_pairs={{0,2},{1,3},{2,0},{3,1},{4,6},{5,7},{6,4},{7,5},{8,10},{9,11},{10,... | collective-permute-start | bytes 491528 | tf_op jit(solution)/shard_map/ppermute | solution.py:45
  67.3 10.1 %collective-permute-start.22 = (bf16[2,2,128,256]{3,2,1,0:T(8,128)(2,1)}, bf16[2,2,128,256]{3,2,1,0:T(8,128)(2,1)}, u32[]{:S(2)}, u32[]{:S(2)}) collective-permute-start(bf16[2,2,128,256]{3,2,1,0:T(8,128)(2,1)} %get-tuple-element.35), channel_id=1, source_target_pairs={{0,8},{4,12},{8,0},{12,4},{16,24},{20,28},{24,16},{28,20},{1,9},{5... | collective-permute-start | bytes 786440 | tf_op jit(solution)/shard_map/ppermute | solution.py:45
  70.6 9.8 %collective-permute-start.15 = (bf16[320,256]{1,0:T(8,128)(2,1)}, bf16[320,256]{1,0:T(8,128)(2,1)S(1)}, u32[]{:S(2)}, u32[]{:S(2)}) collective-permute-start(bf16[320,256]{1,0:T(8,128)(2,1)} %get-tuple-element.32), channel_id=1, source_target_pairs={{0,1},{1,0},{2,3},{3,2},{4,5},{5,4},{6,7},{7,6},{8,9},{9,8},{10,11... | collective-permute-start | bytes 491528 | tf_op jit(solution)/shard_map/ppermute | solution.py:45
  81.4 9.5 %collective-permute-start.23 = (bf16[1,4,128,256]{3,2,1,0:T(8,128)(2,1)}, bf16[1,4,128,256]{3,2,1,0:T(8,128)(2,1)}, u32[]{:S(2)}, u32[]{:S(2)}) collective-permute-start(bf16[1,4,128,256]{3,2,1,0:T(8,128)(2,1)} %get-tuple-element.34), channel_id=1, source_target_pairs={{0,4},{4,0},{8,12},{12,8},{16,20},{20,16},{24,28},{28,24},{1,5},{5... | collective-permute-start | bytes 786440 | tf_op jit(solution)/shard_map/ppermute | solution.py:45
  89.7 17.9 %collective-permute-start.28 = (bf16[320,256]{1,0:T(8,128)(2,1)}, bf16[320,256]{1,0:T(8,128)(2,1)S(1)}, u32[]{:S(2)}, u32[]{:S(2)}) collective-permute-start(bf16[320,256]{1,0:T(8,128)(2,1)} %collective-permute-done.27.refs_6_), channel_id=1, source_target_pairs={{0,16},{4,20},{8,24},{12,28},{16,0},{20,4},{24,8},{28,12},{1,17},{... | collective-permute-start | bytes 491528 | tf_op jit(solution)/shard_map/ppermute | solution.py:45
  90.8 17.8 %collective-permute-start.19 = (bf16[320,256]{1,0:T(8,128)(2,1)}, bf16[320,256]{1,0:T(8,128)(2,1)S(1)}, u32[]{:S(2)}, u32[]{:S(2)}) collective-permute-start(bf16[320,256]{1,0:T(8,128)(2,1)} %collective-permute-done.17.refs_8_), channel_id=1, source_target_pairs={{0,1},{1,0},{2,3},{3,2},{4,5},{5,4},{6,7},{7,6},{8,9},{9,8},{10,11... | collective-permute-start | bytes 491528 | tf_op jit(solution)/shard_map/ppermute | solution.py:45
  93.3 24.7 %collective-permute-start.30 = (bf16[320,256]{1,0:T(8,128)(2,1)}, bf16[320,256]{1,0:T(8,128)(2,1)S(1)}, u32[]{:S(2)}, u32[]{:S(2)}) collective-permute-start(bf16[320,256]{1,0:T(8,128)(2,1)} %collective-permute-done.29.refs_8_), channel_id=1, source_target_pairs={{0,16},{4,20},{8,24},{12,28},{16,0},{20,4},{24,8},{28,12},{1,17},{... | collective-permute-start | bytes 491528 | tf_op jit(solution)/shard_map/ppermute | solution.py:45
  94.3 12.2 %collective-permute-start.41 = (bf16[320,128]{1,0:T(8,128)(2,1)}, bf16[320,128]{1,0:T(8,128)(2,1)S(1)}, u32[]{:S(2)}, u32[]{:S(2)}) collective-permute-start(bf16[320,128]{1,0:T(8,128)(2,1)} %collective-permute-done.40.refs_10_), channel_id=1, source_target_pairs={{0,16},{4,20},{8,24},{12,28},{16,0},{20,4},{24,8},{28,12},{1,17},{... | collective-permute-start | bytes 245768 | tf_op jit(solution)/shard_map/ppermute | solution.py:45
  95.4 22.7 %collective-permute-start.32 = (bf16[320,256]{1,0:T(8,128)(2,1)}, bf16[320,256]{1,0:T(8,128)(2,1)S(1)}, u32[]{:S(2)}, u32[]{:S(2)}) collective-permute-start(bf16[320,256]{1,0:T(8,128)(2,1)} %collective-permute-done.31.refs_10_), channel_id=1, source_target_pairs={{0,16},{4,20},{8,24},{12,28},{16,0},{20,4},{24,8},{28,12},{1,17},{... | collective-permute-start | bytes 491528 | tf_op jit(solution)/shard_map/ppermute | solution.py:45
  106.5 26.1 %collective-permute-start.18 = (bf16[320,256]{1,0:T(8,128)(2,1)}, bf16[320,256]{1,0:T(8,128)(2,1)S(1)}, u32[]{:S(2)}, u32[]{:S(2)}) collective-permute-start(bf16[320,256]{1,0:T(8,128)(2,1)} %collective-permute-done.17.refs_8_), channel_id=1, source_target_pairs={{0,16},{4,20},{8,24},{12,28},{16,0},{20,4},{24,8},{28,12},{1,17},{... | collective-permute-start | bytes 491528 | tf_op jit(solution)/shard_map/ppermute | solution.py:45
  107.7 24.6 %collective-permute-start.16 = (bf16[320,256]{1,0:T(8,128)(2,1)S(1)}, bf16[320,256]{1,0:T(8,128)(2,1)S(1)}, u32[]{:S(2)}, u32[]{:S(2)}) collective-permute-start(bf16[320,256]{1,0:T(8,128)(2,1)S(1)} %copy-done.7), channel_id=1, source_target_pairs={{0,16},{4,20},{8,24},{12,28},{16,0},{20,4},{24,8},{28,12},{1,17},{... | collective-permute-start | bytes 491528 | tf_op jit(solution)/shard_map/ppermute | solution.py:45
  108.6 24.4 %collective-permute-start.20 = (bf16[320,256]{1,0:T(8,128)(2,1)S(1)}, bf16[320,256]{1,0:T(8,128)(2,1)S(1)}, u32[]{:S(2)}, u32[]{:S(2)}) collective-permute-start(bf16[320,256]{1,0:T(8,128)(2,1)S(1)} %collective-permute-done.19.refs_10_), channel_id=1, source_target_pairs={{0,16},{4,20},{8,24},{12,28},{16,0},{20,4},{24,8},{28,12},{1,17},{... | collective-permute-start | bytes 491528 | tf_op jit(solution)/shard_map/ppermute | solution.py:45
  118.0 30.1 %collective-permute-start.42 = (bf16[256,128]{1,0:T(8,128)(2,1)S(1)}, bf16[256,128]{1,0:T(8,128)(2,1)S(1)}, u32[]{:S(2)}, u32[]{:S(2)}) collective-permute-start(bf16[256,128]{1,0:T(8,128)(2,1)S(1)} %get-tuple-element.28), channel_id=1, source_target_pairs={{0,4},{4,0},{8,12},{12,8},{16,20},{20,16},{24,28},{28,24},{1,5},{5... | collective-permute-start | bytes 196616 | tf_op jit(solution)/shard_map/ppermute | solution.py:45
  118.1 30.1 %collective-permute-start.43 = (bf16[256,128]{1,0:T(8,128)(2,1)S(1)}, bf16[256,128]{1,0:T(8,128)(2,1)S(1)}, u32[]{:S(2)}, u32[]{:S(2)}) collective-permute-start(bf16[256,128]{1,0:T(8,128)(2,1)S(1)} %get-tuple-element.29), channel_id=1, source_target_pairs={{0,8},{4,12},{8,0},{12,4},{16,24},{20,28},{24,16},{28,20},{1,9},{5... | collective-permute-start | bytes 196616 | tf_op jit(solution)/shard_map/ppermute | solution.py:45
  132.3 16.7 %collective-permute-start.44 = (bf16[256,128]{1,0:T(8,128)(2,1)S(1)}, bf16[256,128]{1,0:T(8,128)(2,1)S(1)}, u32[]{:S(2)}, u32[]{:S(2)}) collective-permute-start(bf16[256,128]{1,0:T(8,128)(2,1)S(1)} %get-tuple-element.30), channel_id=1, source_target_pairs={{0,12},{4,8},{8,4},{12,0},{16,28},{20,24},{24,20},{28,16},{1,13},{... | collective-permute-start | bytes 196616 | tf_op jit(solution)/shard_map/ppermute | solution.py:45
  132.6 18.4 %collective-permute-start.33 = (bf16[256,256]{1,0:T(8,128)(2,1)S(1)}, bf16[256,256]{1,0:T(8,128)(2,1)S(1)}, u32[]{:S(2)}, u32[]{:S(2)}) collective-permute-start(bf16[256,256]{1,0:T(8,128)(2,1)S(1)} %get-tuple-element.24), channel_id=1, source_target_pairs={{0,4},{4,0},{8,12},{12,8},{16,20},{20,16},{24,28},{28,24},{1,5},{5... | collective-permute-start | bytes 393224 | tf_op jit(solution)/shard_map/ppermute | solution.py:45
  133.0 18.1 %collective-permute-start.34 = (bf16[256,256]{1,0:T(8,128)(2,1)S(1)}, bf16[256,256]{1,0:T(8,128)(2,1)S(1)}, u32[]{:S(2)}, u32[]{:S(2)}) collective-permute-start(bf16[256,256]{1,0:T(8,128)(2,1)S(1)} %get-tuple-element.25), channel_id=1, source_target_pairs={{0,8},{4,12},{8,0},{12,4},{16,24},{20,28},{24,16},{28,20},{1,9},{5... | collective-permute-start | bytes 393224 | tf_op jit(solution)/shard_map/ppermute | solution.py:45
  151.0 8.5 %collective-permute-start.26 = (bf16[256,256]{1,0:T(8,128)(2,1)}, bf16[256,256]{1,0:T(8,128)(2,1)S(1)}, u32[]{:S(2)}, u32[]{:S(2)}) collective-permute-start(bf16[256,256]{1,0:T(8,128)(2,1)} %get-tuple-element.22), channel_id=1, source_target_pairs={{0,12},{4,8},{8,4},{12,0},{16,28},{20,24},{24,20},{28,16},{1,13},{... | collective-permute-start | bytes 393224 | tf_op jit(solution)/shard_map/ppermute | solution.py:45
  151.1 11.5 %collective-permute-start.10 = (bf16[256,256]{1,0:T(8,128)(2,1)S(1)}, bf16[256,256]{1,0:T(8,128)(2,1)S(1)}, u32[]{:S(2)}, u32[]{:S(2)}) collective-permute-start(bf16[256,256]{1,0:T(8,128)(2,1)S(1)} %get-tuple-element.38), channel_id=1, source_target_pairs={{0,8},{4,12},{8,0},{12,4},{16,24},{20,28},{24,16},{28,20},{1,9},{5... | collective-permute-start | bytes 393224 | tf_op jit(solution)/shard_map/ppermute | solution.py:45
  153.9 11.2 %collective-permute-start.11 = (bf16[256,256]{1,0:T(8,128)(2,1)S(1)}, bf16[256,256]{1,0:T(8,128)(2,1)S(1)}, u32[]{:S(2)}, u32[]{:S(2)}) collective-permute-start(bf16[256,256]{1,0:T(8,128)(2,1)S(1)} %get-tuple-element.37), channel_id=1, source_target_pairs={{0,12},{4,8},{8,4},{12,0},{16,28},{20,24},{24,20},{28,16},{1,13},{... | collective-permute-start | bytes 393224 | tf_op jit(solution)/shard_map/ppermute | solution.py:45
  154.2 10.9 %collective-permute-start.9 = (bf16[256,256]{1,0:T(8,128)(2,1)S(1)}, bf16[256,256]{1,0:T(8,128)(2,1)S(1)}, u32[]{:S(2)}, u32[]{:S(2)}) collective-permute-start(bf16[256,256]{1,0:T(8,128)(2,1)S(1)} %get-tuple-element.39), channel_id=1, source_target_pairs={{0,4},{4,0},{8,12},{12,8},{16,20},{20,16},{24,28},{28,24},{1,5},{5... | collective-permute-start | bytes 393224 | tf_op jit(solution)/shard_map/ppermute | solution.py:45
  (42 other events, 506.0 us)

commit v2 on v1

v2 whole, which is shorter than its diff:
```python
import functools

import jax
import jax.numpy as jnp
import numpy as np
from jax import lax
from jax.experimental import pallas as pl
from jax.experimental.pallas import tpu as pltpu
from jax.sharding import PartitionSpec as P

HD = 128
GROUP = 5
QBLK = 128
SEL = 4
TEAM = 4

norm_eps = 1e-06
rope_base = 10000000.0

CHUNKS = ((0, 3), (3, 5), (5, 7))

SMEM = pl.BlockSpec(memory_space=pltpu.SMEM)
VMEM = pl.BlockSpec(memory_space=pltpu.VMEM)
ANY = pl.BlockSpec(memory_space=pl.ANY)


def angle_tables(head_dim):
    half_dim = head_dim // 2
    frequency = rope_base ** (-2.0 * np.arange(half_dim) / head_dim)
    return np.stack(
        [np.mod(frequency * 32.0**digit_level, 2.0 * np.pi) for digit_level in range(4)]
    )


def rope_tables(positions):
    tables = jnp.asarray(np.tile(angle_tables(HD), (1, 2)), jnp.float32)
    angles = jnp.zeros((positions.shape[0], HD), jnp.float32)
    remaining = positions
    for digit_level in range(4):
        digit_value = (remaining % 32).astype(jnp.float32)
        angles = angles + digit_value[:, None] * tables[digit_level][None, :]
        remaining = remaining // 32
    sign = jnp.where(jnp.arange(HD) < HD // 2, -1.0, 1.0).astype(jnp.float32)
    return jnp.cos(angles), jnp.sin(angles) * sign


def swap(value, axis, bit):
    size = lax.axis_size(axis)
    return lax.ppermute(value, axis, [(i, i ^ bit) for i in range(size)])


def bits_of(size, low):
    bits = []
    bit = low
    while bit < size:
        bits.append(bit)
        bit *= 2
    return bits[::-1]


def tile_sources(first, last, group):
    parts = []
    for source in (0, 1):
        if first <= source < last:
            parts.append((source, group * HD, 1))
    query_first = max(first, 2)
    if last > query_first:
        parts.append((2, (group * GROUP + query_first - 2) * HD, last - query_first))
    return parts


def prep_kernel(piece_rows, *refs):
    place_ref, tokens_ref, gain_ref, wq_ref, wk_ref, wv_ref, ck_ref, cv_ref = refs[:8]
    normed_ref = refs[8]
    half_refs = refs[9 : 9 + len(CHUNKS)]
    kept_ref, sent_ref, sem = refs[9 + len(CHUNKS) :]
    group = place_ref[0]
    local = pl.ds(pl.multiple_of(place_ref[1], 16), piece_rows)
    copies = []
    for (first, last), half_ref in zip(CHUNKS, half_refs):
        at = 0
        for source, column, tiles in tile_sources(first, last, group):
            copies.append(
                (
                    (wk_ref, wv_ref, wq_ref)[source].at[
                        local, pl.ds(pl.multiple_of(column, HD), tiles * HD)
                    ],
                    half_ref.at[:, pl.ds(at, tiles * HD)],
                )
            )
            at += tiles * HD
    pair = group // 2
    for target, first in ((sent_ref, 1 - pair), (kept_ref, pair)):
        for core in range(2):
            column = pl.ds(pl.multiple_of((first * 2 + core) * HD, HD), HD)
            copies.append((ck_ref.at[:, column], target.at[core, :, pl.ds(0, HD)]))
            copies.append((cv_ref.at[:, column], target.at[core, :, pl.ds(HD, HD)]))
    copies = [
        pltpu.make_async_copy(source, target, sem.at[index])
        for index, (source, target) in enumerate(copies)
    ]
    for copy in copies:
        copy.start()
    widened = tokens_ref[...].astype(jnp.float32)
    normed_ref[...] = (
        widened
        * lax.rsqrt(jnp.mean(widened * widened, axis=-1, keepdims=True) + norm_eps)
        * gain_ref[...].astype(jnp.float32)
    ).astype(jnp.bfloat16)
    for copy in copies:
        copy.wait()


def prep(place, piece_rows, tokens, norm_gain, weights, caches):
    prefix = caches[0].shape[0]
    shapes = [jax.ShapeDtypeStruct(tokens.shape, jnp.bfloat16)]
    count = 8
    for first, last in CHUNKS:
        shapes.append(jax.ShapeDtypeStruct((piece_rows, (last - first) * HD), jnp.bfloat16))
        count += len(tile_sources(first, last, 0))
    shapes += [jax.ShapeDtypeStruct((2, prefix, 2 * HD), jnp.bfloat16)] * 2
    return pl.pallas_call(
        functools.partial(prep_kernel, piece_rows),
        out_shape=shapes,
        in_specs=[SMEM, VMEM, VMEM] + [ANY] * 5,
        out_specs=[VMEM] + [ANY] * (len(shapes) - 1),
        scratch_shapes=[pltpu.SemaphoreType.DMA((count,))],
        compiler_params=pltpu.CompilerParams(vmem_limit_bytes=24 * 1024 * 1024),
        name="prep",
    )(place, tokens, norm_gain[None, :], *weights, *caches)


def turned(value, cosine, sine):
    return value * cosine + pltpu.roll(value, HD // 2, 1) * sine


def heads_kernel(tiles, piece_count, piece_rows, cache_places, *refs):
    first_tile, last_tile = tiles
    has_kv = first_tile == 0
    query_first = max(first_tile, 2)
    query_count = last_tile - query_first
    refs = list(refs)

    def take(count):
        taken = refs[:count]
        del refs[:count]
        return taken

    offsets_ref, lists_ref = take(2)
    x_refs = take(TEAM)
    piece_refs = take(piece_count)
    wq_ref, wk_ref, wv_ref = take(3)
    bias_ref, cosine_ref, sine_ref = take(3)
    if has_kv:
        cache_refs = take(len(cache_places))
        kv_out_refs = take(TEAM)
        key_ref, value_t_ref, cache_key_ref, cache_value_t_ref = take(4)
    else:
        key_ref, value_t_ref, cache_key_ref, cache_value_t_ref = take(4)
    out_refs = take(TEAM)
    w_buf, w_sem = take(2)
    if has_kv:
        cache_buf, cache_sem = take(2)

    rows = x_refs[0].shape[0]
    shard = wq_ref.shape[0]
    group = offsets_ref[0]
    local = pl.ds(pl.multiple_of(offsets_ref[1], 16), shard)
    copies = []
    at = 0
    for source, column, count in tile_sources(first_tile, last_tile, group):
        copies.append(
            (
                (wk_ref, wv_ref, wq_ref)[source].at[
                    :, pl.ds(pl.multiple_of(column, HD), count * HD)
                ],
                w_buf.at[local, pl.ds(at, count * HD)],
            )
        )
        at += count * HD
    for index, piece in enumerate(piece_refs):
        start = pl.multiple_of(offsets_ref[2 + index], 16)
        copies.append((piece, w_buf.at[pl.ds(start, piece_rows), :]))
    copies = [
        pltpu.make_async_copy(source, target, w_sem.at[index])
        for index, (source, target) in enumerate(copies)
    ]
    for copy in copies:
        copy.start()
    if has_kv:
        core = group % 2
        owner = offsets_ref[2 + piece_count]
        blocks_each = cache_refs[0].shape[1] // QBLK
        cache_copies = []
        for place, cache_ref in zip(cache_places, cache_refs):
            for block in range(blocks_each):
                cache_copies.append(
                    pltpu.make_async_copy(
                        cache_ref.at[core, pl.ds(block * QBLK, QBLK), :],
                        cache_buf.at[(owner ^ place) * blocks_each + block],
                        cache_sem.at[len(cache_copies)],
                    )
                )
        for copy in cache_copies:
            copy.start()
        for copy in cache_copies:
            copy.wait()
        for block in range(blocks_each * len(cache_places)):
            cache_key_ref[block] = cache_buf[block, :, pl.ds(0, HD)]
            cache_value_t_ref[block] = cache_buf[block, :, pl.ds(HD, HD)].T
    for copy in copies:
        copy.wait()

    factor = HD ** (-0.5) * float(np.log2(np.e))
    causal = lax.broadcasted_iota(jnp.int32, (QBLK, QBLK), 0) <= lax.broadcasted_iota(
        jnp.int32, (QBLK, QBLK), 1
    )
    contract_last = (((1,), (1,)), ((), ()))
    blocks = rows // QBLK
    list_rows = blocks * SEL

    for r in range(TEAM):
        span = pl.ds(r * rows, rows)
        lin = (
            jnp.dot(x_refs[r][...], w_buf[...], preferred_element_type=jnp.float32)
            + bias_ref[...]
        )
        cosine, sine = cosine_ref[span, :], sine_ref[span, :]
        queries = []
        for tile in range(first_tile, last_tile):
            at = (tile - first_tile) * HD
            value = lin[:, at : at + HD]
            if tile != 1:
                value = turned(value, cosine, sine)
            if tile >= 2:
                queries.append(value.astype(jnp.bfloat16))
                continue
            kv_out_refs[r][:, pl.ds(at, HD)] = value.astype(kv_out_refs[r].dtype)
            if tile == 0:
                key_ref[span, :] = value.astype(jnp.bfloat16)
            else:
                value_t_ref[:, span] = value.astype(jnp.bfloat16).T
        for block in range(blocks):
            part_span = pl.ds(r * rows + block * QBLK, QBLK)
            near_key = key_ref[part_span, :]
            near_value = value_t_ref[:, part_span]
            for head in range(query_count):
                query = queries[head][block * QBLK : (block + 1) * QBLK, :]
                at = (group * GROUP + query_first - 2 + head) * list_rows + block * SEL
                slots = [lists_ref[r, at + j] for j in range(SEL)]
                places = [jnp.maximum(slot, 0) for slot in slots]
                keys = jnp.concatenate(
                    [near_key] + [cache_key_ref[place] for place in places], axis=0
                )
                values = jnp.concatenate(
                    [near_value] + [cache_value_t_ref[place] for place in places], axis=1
                )
                scores = lax.dot_general(
                    keys, query, contract_last, preferred_element_type=jnp.float32
                )
                parts = [jnp.where(causal, scores[:QBLK], -jnp.inf)]
                for j in range(SEL):
                    part = scores[(j + 1) * QBLK : (j + 2) * QBLK]
                    parts.append(part + jnp.where(slots[j] >= 0, 0.0, -jnp.inf))
                top = functools.reduce(jnp.maximum, parts)
                top = jnp.max(top, axis=0, keepdims=True) * factor
                parts = [jnp.exp2(part * factor - top) for part in parts]
                total = jnp.sum(functools.reduce(jnp.add, parts), axis=0, keepdims=True)
                weights = jnp.concatenate([part.astype(jnp.bfloat16) for part in parts], axis=0)
                mixed = jnp.dot(values, weights, preferred_element_type=jnp.float32)
                out_refs[r][pl.ds(block * QBLK, QBLK), pl.ds(head * HD, HD)] = (
                    (mixed / total).T.astype(out_refs[r].dtype)
                )


def heads(tiles, offsets, lists, x_parts, pieces, weights, bias, cosine, sine, caches, near):
    first_tile, last_tile = tiles
    has_kv = first_tile == 0
    query_count = last_tile - max(first_tile, 2)
    width = (last_tile - first_tile) * HD
    rows, depth = x_parts[0].shape
    everything = TEAM * rows
    operands, specs = [], []

    def add(values, spec):
        operands.extend(values)
        specs.extend([spec] * len(values))

    add([offsets, lists], SMEM)
    add(x_parts, VMEM)
    add(pieces, ANY)
    add(weights, ANY)
    add([bias, cosine, sine], VMEM)
    shapes, out_specs = [], []
    scratch = [
        pltpu.VMEM((depth, width), jnp.bfloat16),
        pltpu.SemaphoreType.DMA((len(pieces) + 3,)),
    ]
    cache_places = ()
    if has_kv:
        cache_places, cache_parts = zip(*caches)
        add(cache_parts, ANY)
        for r in range(TEAM):
            dtype = jnp.float32 if r == 0 else jnp.bfloat16
            shapes.append(jax.ShapeDtypeStruct((rows, 2 * HD), dtype))
        total_blocks = len(caches) * cache_parts[0].shape[1] // QBLK
        shapes.append(jax.ShapeDtypeStruct((everything, HD), jnp.bfloat16))
        shapes.append(jax.ShapeDtypeStruct((HD, everything), jnp.bfloat16))
        shapes.append(jax.ShapeDtypeStruct((total_blocks, QBLK, HD), jnp.bfloat16))
        shapes.append(jax.ShapeDtypeStruct((total_blocks, HD, QBLK), jnp.bfloat16))
        scratch.append(pltpu.VMEM((total_blocks, QBLK, 2 * HD), jnp.bfloat16))
        scratch.append(pltpu.SemaphoreType.DMA((total_blocks,)))
    else:
        add(near, VMEM)
    for r in range(TEAM):
        dtype = jnp.float32 if r == 0 else jnp.bfloat16
        shapes.append(jax.ShapeDtypeStruct((rows, query_count * HD), dtype))
    return pl.pallas_call(
        functools.partial(
            heads_kernel, tiles, len(pieces), pieces[0].shape[0], tuple(cache_places)
        ),
        out_shape=shapes,
        in_specs=specs,
        out_specs=[VMEM] * len(shapes),
        scratch_shapes=scratch,
        compiler_params=pltpu.CompilerParams(vmem_limit_bytes=32 * 1024 * 1024),
        cost_estimate=pl.CostEstimate(
            flops=2 * everything * depth * width,
            bytes_accessed=2 * depth * (everything + width),
            transcendentals=everything * query_count * (SEL + 1) * QBLK,
        ),
        name="heads",
    )(*operands)


def finish_kernel(chunk_count, places_ref, *refs):
    kv_refs = refs[:TEAM]
    context_refs = refs[TEAM : TEAM + TEAM * chunk_count]
    context_ref, keys_ref, values_ref = refs[TEAM + TEAM * chunk_count :]
    for r in range(TEAM):
        place = places_ref[0] ^ r
        column = pl.ds(pl.multiple_of(place * HD, HD), HD)
        keys_ref[:, column] = kv_refs[r][:, pl.ds(0, HD)].astype(jnp.float32)
        values_ref[:, column] = kv_refs[r][:, pl.ds(HD, HD)].astype(jnp.float32)
        at = place * (GROUP * HD)
        for chunk in range(chunk_count):
            ref = context_refs[chunk * TEAM + r]
            wide = ref.shape[1]
            context_ref[:, pl.ds(pl.multiple_of(at, HD), wide)] = ref[...].astype(jnp.float32)
            at = at + wide


def finish(places, kv_parts, context_parts):
    rows = kv_parts[0].shape[0]
    flat = list(kv_parts) + [part for chunk in context_parts for part in chunk]
    wide = TEAM * GROUP * HD
    return pl.pallas_call(
        functools.partial(finish_kernel, len(context_parts)),
        out_shape=[
            jax.ShapeDtypeStruct((rows, wide), jnp.float32),
            jax.ShapeDtypeStruct((rows, TEAM * HD), jnp.float32),
            jax.ShapeDtypeStruct((rows, TEAM * HD), jnp.float32),
        ],
        in_specs=[SMEM] + [VMEM] * len(flat),
        out_specs=[VMEM] * 3,
        compiler_params=pltpu.CompilerParams(vmem_limit_bytes=24 * 1024 * 1024),
        name="finish",
    )(places, *flat)


def on_device(
    tokens,
    norm_gain,
    w_query,
    w_key,
    w_value,
    b_query,
    b_key,
    b_value,
    cache_keys,
    cache_values,
    block_lists,
    start_position,
):
    rows = tokens.shape[0]
    shard = w_query.shape[0]
    ctx_size, grp_size = lax.axis_size("ctx"), lax.axis_size("grp")
    me, layer = lax.axis_index("ctx"), lax.axis_index("grp")
    group = me % TEAM
    sides = ctx_size // TEAM
    side = me // TEAM
    if (shard // sides) % 16:
        sides = 1
        side = side * 0
    piece_rows = shard // sides
    weights = (w_query, w_key, w_value)

    grp_bits = bits_of(grp_size, 1)
    side_bits = bits_of(ctx_size, TEAM) if sides > 1 else []
    grp_order = [0]
    for bit in grp_bits:
        grp_order += [far ^ bit for far in grp_order]
    piece_places = [(far, 0) for far in sorted(grp_order) if far]
    for bit in side_bits:
        piece_places += [(far, over ^ (bit // TEAM)) for far, over in piece_places]
    piece_places = sorted(piece_places)
    offsets = jnp.stack(
        [group, layer * shard]
        + [(layer ^ far) * shard + (side ^ over) * piece_rows for far, over in piece_places]
        + [me]
    ).astype(jnp.int32)
    place = jnp.stack([group, side * piece_rows]).astype(jnp.int32)

    normed, *rest = prep(
        place, piece_rows, tokens, norm_gain, weights, (cache_keys, cache_values)
    )
    halves, (cache_kept, cache_sent) = rest[: len(CHUNKS)], rest[len(CHUNKS) :]

    chunk_pieces = []
    for half in halves:
        held = {0: half}
        for bit in grp_bits:
            for far in sorted(held):
                held[far ^ bit] = swap(held[far], "grp", bit)
        pieces = {(far, 0): held[far] for far in held if far}
        for bit in side_bits:
            for far, over in sorted(pieces):
                pieces[(far, over ^ (bit // TEAM))] = swap(pieces[(far, over)], "ctx", bit)
        chunk_pieces.append([pieces[key] for key in piece_places])

    normed_two = swap(normed, "ctx", 2)
    x_parts = [normed, swap(normed, "ctx", 1), normed_two, swap(normed_two, "ctx", 1)]

    flat_lists = block_lists.reshape(-1)
    lists_two = swap(flat_lists, "ctx", 2)
    lists = jnp.stack(
        [flat_lists, swap(flat_lists, "ctx", 1), lists_two, swap(lists_two, "ctx", 1)]
    )

    caches = [(0, cache_kept), (2, swap(cache_sent, "ctx", 2))]
    for bit in bits_of(ctx_size, TEAM) + [1]:
        caches += [(distance ^ bit, swap(value, "ctx", bit)) for distance, value in caches]

    positions = jnp.concatenate(
        [
            start_position[0]
            + ((me ^ r) * grp_size + layer) * rows
            + jnp.arange(rows, dtype=jnp.int32)
            for r in range(TEAM)
        ]
    )
    cosine, sine = rope_tables(positions)
    bias = jnp.concatenate(
        [
            lax.dynamic_slice_in_dim(b_key, group * HD, HD),
            lax.dynamic_slice_in_dim(b_value, group * HD, HD),
            lax.dynamic_slice_in_dim(b_query, group * GROUP * HD, GROUP * HD),
        ]
    ).astype(jnp.float32)[None, :]

    near, kv_parts, context_parts = None, None, []
    for tiles, pieces in zip(CHUNKS, chunk_pieces):
        first_tile, last_tile = tiles
        results = heads(
            tiles,
            offsets,
            lists,
            x_parts,
            pieces,
            weights,
            bias[:, first_tile * HD : last_tile * HD],
            cosine,
            sine,
            caches,
            near,
        )
        if first_tile == 0:
            kv_parts = [results[0]] + [swap(results[r], "ctx", r) for r in range(1, TEAM)]
            near = results[TEAM : TEAM + 4]
            results = results[TEAM + 4 :]
        context_parts.append([results[0]] + [swap(results[r], "ctx", r) for r in range(1, TEAM)])
    return tuple(finish(place, kv_parts, context_parts))


def solution(mesh):
    in_specs = (
        P(("ctx", "grp"), None),
        P(),
        P("grp", None),
        P("grp", None),
        P("grp", None),
        P(),
        P(),
        P(),
        P("ctx", None),
        P("ctx", None),
        P(None, ("ctx", "grp"), None),
        P(),
    )
    out_specs = (P(("ctx", "grp"), None), P(("ctx", "grp"), None), P(("ctx", "grp"), None))
    return jax.shard_map(
        on_device, mesh=mesh, in_specs=in_specs, out_specs=out_specs, check_vma=False
    )
```

time: 169 us -> 187 us (1.11)
  waiting for transfers between devices: 36.6 us -> 77 us
  starting transfers between devices: 50.9 us -> 39.2 us
  other arithmetic: 13.6 us -> 5.12 us
    ppermute x45 -> x43, waiting for transfers between devices: 36.6 us -> 77 us  [swap(): return lax.ppermute(value, axis, [(i, i ^ bit) for i in range(size)])]
    ppermute x45 -> x43, starting transfers between devices: 50.9 us -> 39.2 us  [swap(): return lax.ppermute(value, axis, [(i, i ^ bit) for i in range(size)])]
    unnamed x60 -> x59, local copies, waits for them, and re-layouts: 11.3 us -> 18.3 us
    concatenate x3 -> x0, other arithmetic: 4.55 us -> none  [the longest x1 1.93 us: on_device(): store = jnp.concatenate([kept, swap(sent, 'ctx', bit)], axis=1)]
    pallas_call x4 -> x3, Pallas kernels: 40.8 us -> 36.7 us  [heads(): pl.pallas_call(functools.partial(heads_kernel, tiles, len(pieces), pieces...]
    reshape x2 -> x1, local copies, waits for them, and re-layouts: 3.33 us -> 0.11 us  [on_device(): flat_lists = block_lists.reshape(-1)]
    pallas_call x0 -> x1, Pallas kernels: none -> 2.77 us  [prep(): pl.pallas_call(functools.partial(prep_kernel, piece_rows), out_shape=shap...]
    slice x3 -> x0, local copies, waits for them, and re-layouts: 2.66 us -> none  [the longest x2 2.63 us: on_device(): held = {0: half[:, first_tile * HD:last_tile * HD]}]
  transfers between devices with their start and end apart: 45 -> 43, of which waited for: 15 -> 14; matrix products, arithmetic and copies ran while one was open for 14% -> 4% of each run, Pallas kernels for 24% -> 20%
where the time goes in v2:
time: 187 us
  waiting for transfers between devices  77 us (41%)
  Pallas kernels  42.2 us (23%)
  starting transfers between devices  39.2 us (21%)
  local copies, waits for them, and re-layouts  21.4 us (11%)
  other arithmetic  5.12 us (3%)
    ppermute x43, waiting for transfers between devices, swap(): return lax.ppermute(value, axis, [(i, i ^ bit) for i in range(size)])  77 us
    ppermute x43, starting transfers between devices, swap(): return lax.ppermute(value, axis, [(i, i ^ bit) for i in range(size)])  39.2 us
    pallas_call x3, Pallas kernels, heads(): pl.pallas_call(functools.partial(heads_kernel, tiles, len(pieces), pieces...  36.7 us
    unnamed x59, local copies, waits for them, and re-layouts  18.3 us
    mul x1, other arithmetic, rope_tables(): return (jnp.cos(angles), jnp.sin(angles) * sign)  4.26 us
  transfers between devices with their start and end apart: 43, of which 14 were waited for; matrix products, arithmetic and copies ran while one was open for 4% of the time, Pallas kernels for 20%

profile of v2, /device:TPU:0, one launch (start us, length us, event | category | flops | bytes accessed | tf_op | source)
XLA Modules:
  0.0 186.6 jit_solution(5346547479310218963)
XLA Ops:
  1.4 1.9 %copy-done = bf16[640,2560]{1,0:T(8,128)(2,1)S(1)} copy-done((bf16[640,2560]{1,0:T(8,128)(2,1)S(1)}, bf16[640,2560]{1,0:T(8,128)(2,1)}, u32[]{:S(2)}) %copy-start) | copy-done | bytes 3276824
  8.7 2.8 %prep.1 = (bf16[256,2560]{1,0:T(8,128)(2,1)}, bf16[320,384]{1,0:T(8,128)(2,1)S(1)}, bf16[320,256]{1,0:T(8,128)(2,1)S(1)}, bf16[320,256]{1,0:T(8,128)(2,1)}, bf16...) custom-call(s32[2]{0:T(128)S(1)} %pad_add_fusion.2.refs_0_.places_ref, bf16[256,2560]{1,0:T(8,128)(2,1)S(1)} %copy-done.10, ...), custom_call_target="tpu_custom_call" | custom-call | tf_op jit(solution)/shard_map/prep/pallas_call | solution.py:122
  12.8 2.9 %collective-permute-start.4 = (bf16[256,2560]{1,0:T(8,128)(2,1)}, bf16[256,2560]{1,0:T(8,128)(2,1)}, u32[]{:S(2)}, u32[]{:S(2)}) collective-permute-start(bf16[256,2560]{1,0:T(8,128)(2,1)} %get-tuple-element.29.refs_2_), channel_id=1, source_target_pairs={{0,8},{4,12},{8,0},{12,4},{16,24},{20,28},{24,16},{28,20},{1,9},{5... | collective-permute-start | bytes 3932168 | tf_op jit(solution)/shard_map/ppermute | solution.py:49
  15.8 2.0 %collective-permute-start.13 = (bf16[2,128,256]{2,1,0:T(8,128)(2,1)}, bf16[2,128,256]{2,1,0:T(8,128)(2,1)}, u32[]{:S(2)}, u32[]{:S(2)}) collective-permute-start(bf16[2,128,256]{2,1,0:T(8,128)(2,1)} %get-tuple-element.31.refs_18_), channel_id=1, source_target_pairs={{0,16},{4,20},{8,24},{12,28},{16,0},{20,4},{24,8},{28,12},{1,17},{... | collective-permute-start | bytes 393224 | tf_op jit(solution)/shard_map/ppermute | solution.py:49
  17.8 2.6 %collective-permute-start.36 = (bf16[320,256]{1,0:T(8,128)(2,1)}, bf16[320,256]{1,0:T(8,128)(2,1)}, u32[]{:S(2)}, u32[]{:S(2)}) collective-permute-start(bf16[320,256]{1,0:T(8,128)(2,1)} %get-tuple-element.50), channel_id=1, source_target_pairs={{0,2},{1,3},{2,0},{3,1},{4,6},{5,7},{6,4},{7,5},{8,10},{9,11},{10,... | collective-permute-start | bytes 491528 | tf_op jit(solution)/shard_map/ppermute | solution.py:49
  20.6 1.6 collective-permute-start.1
  22.2 25.4 %collective-permute-done.1 = s32[160]{0:T(256)S(1)} collective-permute-done((s32[160]{0:T(256)S(1)}, s32[160]{0:T(256)S(1)}, u32[]{:S(2)}, u32[]{:S(2)}) %collective-permute-start.1) | collective-permute-done | bytes 672 | tf_op jit(solution)/shard_map/ppermute | solution.py:49
  49.9 1.8 collective-permute-start.34
  52.4 2.6 %collective-permute-start.8 = (bf16[320,384]{1,0:T(8,128)(2,1)}, bf16[320,384]{1,0:T(8,128)(2,1)S(1)}, u32[]{:S(2)}, u32[]{:S(2)}) collective-permute-start(bf16[320,384]{1,0:T(8,128)(2,1)} %copy-done.21), channel_id=1, source_target_pairs={{0,2},{1,3},{2,0},{3,1},{4,6},{5,7},{6,4},{7,5},{8,10},{9,11},{10,... | collective-permute-start | bytes 737288 | tf_op jit(solution)/shard_map/ppermute | solution.py:49
  57.0 1.8 collective-permute-done.34.refs_6_
  59.4 14.4 %collective-permute-done.27.refs_8_ = bf16[320,256]{1,0:T(8,128)(2,1)} collective-permute-done((bf16[320,256]{1,0:T(8,128)(2,1)}, bf16[320,256]{1,0:T(8,128)(2,1)}, u32[]{:S(2)}, u32[]{:S(2)}) %collective-permute-start.27) | collective-permute-done | bytes 163872 | tf_op jit(solution)/shard_map/ppermute | solution.py:49
  74.4 1.6 collective-permute-start.14
  76.1 5.0 %collective-permute-done.6.refs_6_ = bf16[320,384]{1,0:T(8,128)(2,1)} collective-permute-done((bf16[320,384]{1,0:T(8,128)(2,1)}, bf16[320,384]{1,0:T(8,128)(2,1)}, u32[]{:S(2)}, u32[]{:S(2)}) %collective-permute-start.6) | collective-permute-done | bytes 245792 | tf_op jit(solution)/shard_map/ppermute | solution.py:49
  85.3 3.0 %collective-permute-done.38.refs_10_ = bf16[320,256]{1,0:T(8,128)(2,1)} collective-permute-done((bf16[320,256]{1,0:T(8,128)(2,1)}, bf16[320,256]{1,0:T(8,128)(2,1)}, u32[]{:S(2)}, u32[]{:S(2)}) %collective-permute-start.38) | collective-permute-done | bytes 163872 | tf_op jit(solution)/shard_map/ppermute | solution.py:49
  89.1 4.3 %sine_multiply_fusion = (f32[1024,128]{1,0:T(8,128)}, f32[1024,128]{1,0:T(8,128)}) fusion(f32[128]{0:T(128)S(1)} %compare_select_fusion, f32[128]{0:T(128)} %constant.124, f32[1024]{0:T(1024)S(1)} %get-tuple-element.59, f32[128]{0:T(128)} %constant.122, f32[1024]{0:T(1024)S(1)} %get-tuple-element.58, f32[128]{0:T(128)} %constant.120, ...), kind=kLoop, calls=%fused_computation | loop fusion | flops 1048576 | bytes 1067520 | tf_op jit(solution)/shard_map/mul | solution.py:44
  94.9 2.4 %collective-permute-start.9 = (bf16[320,384]{1,0:T(8,128)(2,1)S(1)}, bf16[320,384]{1,0:T(8,128)(2,1)}, u32[]{:S(2)}, u32[]{:S(2)}) collective-permute-start(bf16[320,384]{1,0:T(8,128)(2,1)S(1)} %collective-permute-done.8.refs_8_), channel_id=1, source_target_pairs={{0,16},{4,20},{8,24},{12,28},{16,0},{20,4},{24,8},{28,12},{1,17},{... | collective-permute-start | bytes 737288 | tf_op jit(solution)/shard_map/ppermute | solution.py:49
  97.3 1.9 %collective-permute-start.11 = (bf16[320,384]{1,0:T(8,128)(2,1)}, bf16[320,384]{1,0:T(8,128)(2,1)}, u32[]{:S(2)}, u32[]{:S(2)}) collective-permute-start(bf16[320,384]{1,0:T(8,128)(2,1)} %collective-permute-done.10.refs_10_), channel_id=1, source_target_pairs={{0,16},{4,20},{8,24},{12,28},{16,0},{20,4},{24,8},{28,12},{1,17},{... | collective-permute-start | bytes 737288 | tf_op jit(solution)/shard_map/ppermute | solution.py:49
  100.8 8.6 %collective-permute-done.7.refs_7_ = bf16[320,384]{1,0:T(8,128)(2,1)} collective-permute-done((bf16[320,384]{1,0:T(8,128)(2,1)}, bf16[320,384]{1,0:T(8,128)(2,1)}, u32[]{:S(2)}, u32[]{:S(2)}) %collective-permute-start.7) | collective-permute-done | bytes 245792 | tf_op jit(solution)/shard_map/ppermute | solution.py:49
  109.4 1.9 %collective-permute-start.37 = (bf16[320,256]{1,0:T(8,128)(2,1)}, bf16[320,256]{1,0:T(8,128)(2,1)S(1)}, u32[]{:S(2)}, u32[]{:S(2)}) collective-permute-start(bf16[320,256]{1,0:T(8,128)(2,1)} %collective-permute-done.36.refs_8_), channel_id=1, source_target_pairs={{0,16},{4,20},{8,24},{12,28},{16,0},{20,4},{24,8},{28,12},{1,17},{... | collective-permute-start | bytes 491528 | tf_op jit(solution)/shard_map/ppermute | solution.py:49
  111.5 3.2 %collective-permute-done.11.refs_11_ = bf16[320,384]{1,0:T(8,128)(2,1)} collective-permute-done((bf16[320,384]{1,0:T(8,128)(2,1)}, bf16[320,384]{1,0:T(8,128)(2,1)}, u32[]{:S(2)}, u32[]{:S(2)}) %collective-permute-start.11) | collective-permute-done | bytes 245792 | tf_op jit(solution)/shard_map/ppermute | solution.py:49
  114.7 1.9 %collective-permute-start.26 = (bf16[320,256]{1,0:T(8,128)(2,1)}, bf16[320,256]{1,0:T(8,128)(2,1)S(1)}, u32[]{:S(2)}, u32[]{:S(2)}) collective-permute-start(bf16[320,256]{1,0:T(8,128)(2,1)} %collective-permute-done.25.refs_6_), channel_id=1, source_target_pairs={{0,16},{4,20},{8,24},{12,28},{16,0},{20,4},{24,8},{28,12},{1,17},{... | collective-permute-start | bytes 491528 | tf_op jit(solution)/shard_map/ppermute | solution.py:49
  116.7 1.9 %collective-permute-start.30 = (bf16[320,256]{1,0:T(8,128)(2,1)}, bf16[320,256]{1,0:T(8,128)(2,1)S(1)}, u32[]{:S(2)}, u32[]{:S(2)}) collective-permute-start(bf16[320,256]{1,0:T(8,128)(2,1)} %collective-permute-done.29.refs_10_), channel_id=1, source_target_pairs={{0,16},{4,20},{8,24},{12,28},{16,0},{20,4},{24,8},{28,12},{1,17},{... | collective-permute-start | bytes 491528 | tf_op jit(solution)/shard_map/ppermute | solution.py:49
  125.7 10.1 %heads.3 = (f32[256,256]{1,0:T(8,128)S(1)}, bf16[256,256]{1,0:T(8,128)(2,1)S(1)}, bf16[256,256]{1,0:T(8,128)(2,1)S(1)}, bf16[256,256]{1,0:T(8,128)(2,1)S(1)}, bf...) custom-call(s32[9]{0:T(128)S(1)} %stack.60.refs_0_, ...), custom_call_target="tpu_custom_call" | custom-call | flops 2013265920 | bytes 7208960 | tf_op jit(solution)/shard_map/heads/pallas_call | solution.py:318
  135.8 13.3 %heads.5 = (f32[256,256]{1,0:T(8,128)S(1)}, bf16[256,256]{1,0:T(8,128)(2,1)S(1)}, bf16[256,256]{1,0:T(8,128)(2,1)S(1)}, bf16[256,256]{1,0:T(8,128)(2,1)S(1)}) custom-call(s32[9]{0:T(128)S(1)} %stack.60.refs_0_, s32[4,160]{1,0:T(4,128)S(1)} %pad_add_fusion.refs_1_, bf16[256,2560]{1,0:T(8,128)(2,1)} %get-tuple-element.29.refs_2_, ...), custom_call_target="tpu_custom_call" | custom-call | flops 1342177280 | bytes 6553600 | tf_op jit(solution)/shard_map/heads/pallas_call | solution.py:318
  149.2 1.6 collective-permute-start.41
  152.9 13.3 %heads.4 = (f32[256,256]{1,0:T(8,128)S(1)}, bf16[256,256]{1,0:T(8,128)(2,1)S(1)}, bf16[256,256]{1,0:T(8,128)(2,1)S(1)}, bf16[256,256]{1,0:T(8,128)(2,1)S(1)}) custom-call(s32[9]{0:T(128)S(1)} %stack.60.refs_0_, s32[4,160]{1,0:T(4,128)S(1)} %pad_add_fusion.refs_1_, bf16[256,2560]{1,0:T(8,128)(2,1)} %get-tuple-element.29.refs_2_, ...), custom_call_target="tpu_custom_call" | custom-call | flops 1342177280 | bytes 6553600 | tf_op jit(solution)/shard_map/heads/pallas_call | solution.py:318
  167.0 3.2 %collective-permute-done.24.refs_7_ = bf16[256,128]{1,0:T(8,128)(2,1)S(1)} collective-permute-done((bf16[256,128]{1,0:T(8,128)(2,1)S(1)}, bf16[256,128]{1,0:T(8,128)(2,1)S(1)}, u32[]{:S(2)}, u32[]{:S(2)}) %collective-permute-start.24) | collective-permute-done | bytes 65568 | tf_op jit(solution)/shard_map/ppermute | solution.py:49
  173.8 2.7 %collective-permute-done.32.refs_10_ = bf16[256,256]{1,0:T(8,128)(2,1)S(1)} collective-permute-done((bf16[256,256]{1,0:T(8,128)(2,1)S(1)}, bf16[256,256]{1,0:T(8,128)(2,1)S(1)}, u32[]{:S(2)}, u32[]{:S(2)}) %collective-permute-start.32) | collective-permute-done | bytes 131104 | tf_op jit(solution)/shard_map/ppermute | solution.py:49
  176.6 1.7 collective-permute-done.33.refs_11_
  178.3 3.9 %collective-permute-done.20.refs_2_ = bf16[256,256]{1,0:T(8,128)(2,1)S(1)} collective-permute-done((bf16[256,256]{1,0:T(8,128)(2,1)S(1)}, bf16[256,256]{1,0:T(8,128)(2,1)S(1)}, u32[]{:S(2)}, u32[]{:S(2)}) %collective-permute-start.20) | collective-permute-done | bytes 131104 | tf_op jit(solution)/shard_map/ppermute | solution.py:49
  182.2 1.7 collective-permute-done.21.refs_3_
  183.9 2.7 %finish.1 = (f32[256,2560]{1,0:T(8,128)}, f32[256,512]{1,0:T(8,128)}, f32[256,512]{1,0:T(8,128)}) custom-call(s32[2]{0:T(128)S(1)} %pad_add_fusion.2.refs_0_.places_ref, f32[256,256]{1,0:T(8,128)S(1)} %get-tuple-element.33.refs_0_, bf16[256,256]{1,0:T(8,128)(2,1)S(1)} %collective-permute-done.19.refs_1_, ...), custom_call_target="tpu_custom_call" | custom-call | tf_op jit(solution)/shard_map/finish/pallas_call | solution.py:357
  (135 shorter events, 35.0 us)
Async XLA Ops:
  12.8 46.0 %collective-permute-start.4 = (bf16[256,2560]{1,0:T(8,128)(2,1)}, bf16[256,2560]{1,0:T(8,128)(2,1)}, u32[]{:S(2)}, u32[]{:S(2)}) collective-permute-start(bf16[256,2560]{1,0:T(8,128)(2,1)} %get-tuple-element.29.refs_2_), channel_id=1, source_target_pairs={{0,8},{4,12},{8,0},{12,4},{16,24},{20,28},{24,16},{28,20},{1,9},{5... | collective-permute-start | bytes 3932168 | tf_op jit(solution)/shard_map/ppermute | solution.py:49
  15.8 36.0 %collective-permute-start.12 = (bf16[2,128,256]{2,1,0:T(8,128)(2,1)}, bf16[2,128,256]{2,1,0:T(8,128)(2,1)S(1)}, u32[]{:S(2)}, u32[]{:S(2)}) collective-permute-start(bf16[2,128,256]{2,1,0:T(8,128)(2,1)} %get-tuple-element.32), channel_id=1, source_target_pairs={{0,8},{4,12},{8,0},{12,4},{16,24},{20,28},{24,16},{28,20},{1,9},{5... | collective-permute-start | bytes 393224 | tf_op jit(solution)/shard_map/ppermute | solution.py:49
  15.8 35.9 %collective-permute-start.13 = (bf16[2,128,256]{2,1,0:T(8,128)(2,1)}, bf16[2,128,256]{2,1,0:T(8,128)(2,1)}, u32[]{:S(2)}, u32[]{:S(2)}) collective-permute-start(bf16[2,128,256]{2,1,0:T(8,128)(2,1)} %get-tuple-element.31.refs_18_), channel_id=1, source_target_pairs={{0,16},{4,20},{8,24},{12,28},{16,0},{20,4},{24,8},{28,12},{1,17},{... | collective-permute-start | bytes 393224 | tf_op jit(solution)/shard_map/ppermute | solution.py:49
  17.8 38.7 %collective-permute-start.36 = (bf16[320,256]{1,0:T(8,128)(2,1)}, bf16[320,256]{1,0:T(8,128)(2,1)}, u32[]{:S(2)}, u32[]{:S(2)}) collective-permute-start(bf16[320,256]{1,0:T(8,128)(2,1)} %get-tuple-element.50), channel_id=1, source_target_pairs={{0,2},{1,3},{2,0},{3,1},{4,6},{5,7},{6,4},{7,5},{8,10},{9,11},{10,... | collective-permute-start | bytes 491528 | tf_op jit(solution)/shard_map/ppermute | solution.py:49
  20.6 27.0 %collective-permute-start.1 = (s32[160]{0:T(256)S(1)}, s32[160]{0:T(256)S(1)}, u32[]{:S(2)}, u32[]{:S(2)}) collective-permute-start(s32[160]{0:T(256)S(1)} %reshape.377), channel_id=1, source_target_pairs={{0,8},{4,12},{8,0},{12,4},{16,24},{20,28},{24,16},{28,20},{1,9},{5... | collective-permute-start | bytes 1928 | tf_op jit(solution)/shard_map/ppermute | solution.py:49
  49.9 8.9 %collective-permute-start.34 = (bf16[320,256]{1,0:T(8,128)(2,1)}, bf16[320,256]{1,0:T(8,128)(2,1)}, u32[]{:S(2)}, u32[]{:S(2)}) collective-permute-start(bf16[320,256]{1,0:T(8,128)(2,1)} %get-tuple-element.50), channel_id=1, source_target_pairs={{0,1},{1,0},{2,3},{3,2},{4,5},{5,4},{6,7},{7,6},{8,9},{9,8},{10,11... | collective-permute-start | bytes 491528 | tf_op jit(solution)/shard_map/ppermute | solution.py:49
  52.4 23.6 %collective-permute-start.8 = (bf16[320,384]{1,0:T(8,128)(2,1)}, bf16[320,384]{1,0:T(8,128)(2,1)S(1)}, u32[]{:S(2)}, u32[]{:S(2)}) collective-permute-start(bf16[320,384]{1,0:T(8,128)(2,1)} %copy-done.21), channel_id=1, source_target_pairs={{0,2},{1,3},{2,0},{3,1},{4,6},{5,7},{6,4},{7,5},{8,10},{9,11},{10,... | collective-permute-start | bytes 737288 | tf_op jit(solution)/shard_map/ppermute | solution.py:49
  55.6 18.1 %collective-permute-start.27 = (bf16[320,256]{1,0:T(8,128)(2,1)}, bf16[320,256]{1,0:T(8,128)(2,1)}, u32[]{:S(2)}, u32[]{:S(2)}) collective-permute-start(bf16[320,256]{1,0:T(8,128)(2,1)} %copy-done.22), channel_id=1, source_target_pairs={{0,2},{1,3},{2,0},{3,1},{4,6},{5,7},{6,4},{7,5},{8,10},{9,11},{10,... | collective-permute-start | bytes 491528 | tf_op jit(solution)/shard_map/ppermute | solution.py:49
  56.5 17.9 %collective-permute-start.25 = (bf16[320,256]{1,0:T(8,128)(2,1)}, bf16[320,256]{1,0:T(8,128)(2,1)}, u32[]{:S(2)}, u32[]{:S(2)}) collective-permute-start(bf16[320,256]{1,0:T(8,128)(2,1)} %copy-done.22), channel_id=1, source_target_pairs={{0,1},{1,0},{2,3},{3,2},{4,5},{5,4},{6,7},{7,6},{8,9},{9,8},{10,11... | collective-permute-start | bytes 491528 | tf_op jit(solution)/shard_map/ppermute | solution.py:49
  58.8 57.8 %collective-permute-start.3 = (bf16[256,2560]{1,0:T(8,128)(2,1)}, bf16[256,2560]{1,0:T(8,128)(2,1)}, u32[]{:S(2)}, u32[]{:S(2)}) collective-permute-start(bf16[256,2560]{1,0:T(8,128)(2,1)} %get-tuple-element.29.refs_2_), channel_id=1, source_target_pairs={{0,4},{4,0},{8,12},{12,8},{16,20},{20,16},{24,28},{28,24},{1,5},{5... | collective-permute-start | bytes 3932168 | tf_op jit(solution)/shard_map/ppermute | solution.py:49
  58.8 57.9 %collective-permute-start.5 = (bf16[256,2560]{1,0:T(8,128)(2,1)}, bf16[256,2560]{1,0:T(8,128)(2,1)}, u32[]{:S(2)}, u32[]{:S(2)}) collective-permute-start(bf16[256,2560]{1,0:T(8,128)(2,1)} %collective-permute-done.4.refs_4_), channel_id=1, source_target_pairs={{0,4},{4,0},{8,12},{12,8},{16,20},{20,16},{24,28},{28,24},{1,5},{5... | collective-permute-start | bytes 3932168 | tf_op jit(solution)/shard_map/ppermute | solution.py:49
  73.7 7.3 %collective-permute-start.6 = (bf16[320,384]{1,0:T(8,128)(2,1)}, bf16[320,384]{1,0:T(8,128)(2,1)}, u32[]{:S(2)}, u32[]{:S(2)}) collective-permute-start(bf16[320,384]{1,0:T(8,128)(2,1)} %copy-done.21), channel_id=1, source_target_pairs={{0,1},{1,0},{2,3},{3,2},{4,5},{5,4},{6,7},{7,6},{8,9},{9,8},{10,11... | collective-permute-start | bytes 737288 | tf_op jit(solution)/shard_map/ppermute | solution.py:49
  81.1 7.3 %collective-permute-start.38 = (bf16[320,256]{1,0:T(8,128)(2,1)}, bf16[320,256]{1,0:T(8,128)(2,1)}, u32[]{:S(2)}, u32[]{:S(2)}) collective-permute-start(bf16[320,256]{1,0:T(8,128)(2,1)} %collective-permute-done.36.refs_8_), channel_id=1, source_target_pairs={{0,1},{1,0},{2,3},{3,2},{4,5},{5,4},{6,7},{7,6},{8,9},{9,8},{10,11... | collective-permute-start | bytes 491528 | tf_op jit(solution)/shard_map/ppermute | solution.py:49
  84.0 10.8 %collective-permute-start.29 = (bf16[320,256]{1,0:T(8,128)(2,1)}, bf16[320,256]{1,0:T(8,128)(2,1)}, u32[]{:S(2)}, u32[]{:S(2)}) collective-permute-start(bf16[320,256]{1,0:T(8,128)(2,1)} %collective-permute-done.27.refs_8_), channel_id=1, source_target_pairs={{0,1},{1,0},{2,3},{3,2},{4,5},{5,4},{6,7},{7,6},{8,9},{9,8},{10,11... | collective-permute-start | bytes 491528 | tf_op jit(solution)/shard_map/ppermute | solution.py:49
  88.4 9.0 %collective-permute-start.10 = (bf16[320,384]{1,0:T(8,128)(2,1)S(1)}, bf16[320,384]{1,0:T(8,128)(2,1)}, u32[]{:S(2)}, u32[]{:S(2)}) collective-permute-start(bf16[320,384]{1,0:T(8,128)(2,1)S(1)} %collective-permute-done.8.refs_8_), channel_id=1, source_target_pairs={{0,1},{1,0},{2,3},{3,2},{4,5},{5,4},{6,7},{7,6},{8,9},{9,8},{10,11... | collective-permute-start | bytes 737288 | tf_op jit(solution)/shard_map/ppermute | solution.py:49
  89.1 8.2 %collective-permute-start.18 = (bf16[2,128,256]{2,1,0:T(8,128)(2,1)}, bf16[2,128,256]{2,1,0:T(8,128)(2,1)}, u32[]{:S(2)}, u32[]{:S(2)}) collective-permute-start(bf16[2,128,256]{2,1,0:T(8,128)(2,1)} %collective-permute-done.14.refs_21_), channel_id=1, source_target_pairs={{0,4},{4,0},{8,12},{12,8},{16,20},{20,16},{24,28},{28,24},{1,5},{5... | collective-permute-start | bytes 393224 | tf_op jit(solution)/shard_map/ppermute | solution.py:49
  94.9 16.5 %collective-permute-start.9 = (bf16[320,384]{1,0:T(8,128)(2,1)S(1)}, bf16[320,384]{1,0:T(8,128)(2,1)}, u32[]{:S(2)}, u32[]{:S(2)}) collective-permute-start(bf16[320,384]{1,0:T(8,128)(2,1)S(1)} %collective-permute-done.8.refs_8_), channel_id=1, source_target_pairs={{0,16},{4,20},{8,24},{12,28},{16,0},{20,4},{24,8},{28,12},{1,17},{... | collective-permute-start | bytes 737288 | tf_op jit(solution)/shard_map/ppermute | solution.py:49
  97.2 12.2 %collective-permute-start.7 = (bf16[320,384]{1,0:T(8,128)(2,1)}, bf16[320,384]{1,0:T(8,128)(2,1)}, u32[]{:S(2)}, u32[]{:S(2)}) collective-permute-start(bf16[320,384]{1,0:T(8,128)(2,1)} %collective-permute-done.6.refs_6_), channel_id=1, source_target_pairs={{0,16},{4,20},{8,24},{12,28},{16,0},{20,4},{24,8},{28,12},{1,17},{... | collective-permute-start | bytes 737288 | tf_op jit(solution)/shard_map/ppermute | solution.py:49
  97.3 17.4 %collective-permute-start.11 = (bf16[320,384]{1,0:T(8,128)(2,1)}, bf16[320,384]{1,0:T(8,128)(2,1)}, u32[]{:S(2)}, u32[]{:S(2)}) collective-permute-start(bf16[320,384]{1,0:T(8,128)(2,1)} %collective-permute-done.10.refs_10_), channel_id=1, source_target_pairs={{0,16},{4,20},{8,24},{12,28},{16,0},{20,4},{24,8},{28,12},{1,17},{... | collective-permute-start | bytes 737288 | tf_op jit(solution)/shard_map/ppermute | solution.py:49
  109.4 26.4 %collective-permute-start.37 = (bf16[320,256]{1,0:T(8,128)(2,1)}, bf16[320,256]{1,0:T(8,128)(2,1)S(1)}, u32[]{:S(2)}, u32[]{:S(2)}) collective-permute-start(bf16[320,256]{1,0:T(8,128)(2,1)} %collective-permute-done.36.refs_8_), channel_id=1, source_target_pairs={{0,16},{4,20},{8,24},{12,28},{16,0},{20,4},{24,8},{28,12},{1,17},{... | collective-permute-start | bytes 491528 | tf_op jit(solution)/shard_map/ppermute | solution.py:49
  111.4 39.7 %collective-permute-start.28 = (bf16[320,256]{1,0:T(8,128)(2,1)}, bf16[320,256]{1,0:T(8,128)(2,1)S(1)}, u32[]{:S(2)}, u32[]{:S(2)}) collective-permute-start(bf16[320,256]{1,0:T(8,128)(2,1)} %collective-permute-done.27.refs_8_), channel_id=1, source_target_pairs={{0,16},{4,20},{8,24},{12,28},{16,0},{20,4},{24,8},{28,12},{1,17},{... | collective-permute-start | bytes 491528 | tf_op jit(solution)/shard_map/ppermute | solution.py:49
  114.7 36.1 %collective-permute-start.26 = (bf16[320,256]{1,0:T(8,128)(2,1)}, bf16[320,256]{1,0:T(8,128)(2,1)S(1)}, u32[]{:S(2)}, u32[]{:S(2)}) collective-permute-start(bf16[320,256]{1,0:T(8,128)(2,1)} %collective-permute-done.25.refs_6_), channel_id=1, source_target_pairs={{0,16},{4,20},{8,24},{12,28},{16,0},{20,4},{24,8},{28,12},{1,17},{... | collective-permute-start | bytes 491528 | tf_op jit(solution)/shard_map/ppermute | solution.py:49
  116.6 19.2 %collective-permute-start.39 = (bf16[320,256]{1,0:T(8,128)(2,1)}, bf16[320,256]{1,0:T(8,128)(2,1)S(1)}, u32[]{:S(2)}, u32[]{:S(2)}) collective-permute-start(bf16[320,256]{1,0:T(8,128)(2,1)} %collective-permute-done.38.refs_10_), channel_id=1, source_target_pairs={{0,16},{4,20},{8,24},{12,28},{16,0},{20,4},{24,8},{28,12},{1,17},{... | collective-permute-start | bytes 491528 | tf_op jit(solution)/shard_map/ppermute | solution.py:49
  116.7 34.7 %collective-permute-start.30 = (bf16[320,256]{1,0:T(8,128)(2,1)}, bf16[320,256]{1,0:T(8,128)(2,1)S(1)}, u32[]{:S(2)}, u32[]{:S(2)}) collective-permute-start(bf16[320,256]{1,0:T(8,128)(2,1)} %collective-permute-done.29.refs_10_), channel_id=1, source_target_pairs={{0,16},{4,20},{8,24},{12,28},{16,0},{20,4},{24,8},{28,12},{1,17},{... | collective-permute-start | bytes 491528 | tf_op jit(solution)/shard_map/ppermute | solution.py:49
  149.1 21.6 %collective-permute-start.40 = (bf16[256,256]{1,0:T(8,128)(2,1)S(1)}, bf16[256,256]{1,0:T(8,128)(2,1)S(1)}, u32[]{:S(2)}, u32[]{:S(2)}) collective-permute-start(bf16[256,256]{1,0:T(8,128)(2,1)S(1)} %get-tuple-element.52), channel_id=1, source_target_pairs={{0,4},{4,0},{8,12},{12,8},{16,20},{20,16},{24,28},{28,24},{1,5},{5... | collective-permute-start | bytes 393224 | tf_op jit(solution)/shard_map/ppermute | solution.py:49
  149.2 22.7 %collective-permute-start.41 = (bf16[256,256]{1,0:T(8,128)(2,1)S(1)}, bf16[256,256]{1,0:T(8,128)(2,1)S(1)}, u32[]{:S(2)}, u32[]{:S(2)}) collective-permute-start(bf16[256,256]{1,0:T(8,128)(2,1)S(1)} %get-tuple-element.53), channel_id=1, source_target_pairs={{0,8},{4,12},{8,0},{12,4},{16,24},{20,28},{24,16},{28,20},{1,9},{5... | collective-permute-start | bytes 393224 | tf_op jit(solution)/shard_map/ppermute | solution.py:49
  150.8 21.6 %collective-permute-start.42 = (bf16[256,256]{1,0:T(8,128)(2,1)S(1)}, bf16[256,256]{1,0:T(8,128)(2,1)S(1)}, u32[]{:S(2)}, u32[]{:S(2)}) collective-permute-start(bf16[256,256]{1,0:T(8,128)(2,1)S(1)} %get-tuple-element.54), channel_id=1, source_target_pairs={{0,12},{4,8},{8,4},{12,0},{16,28},{20,24},{24,20},{28,16},{1,13},{... | collective-permute-start | bytes 393224 | tf_op jit(solution)/shard_map/ppermute | solution.py:49
  151.1 15.1 %collective-permute-start.22 = (bf16[256,128]{1,0:T(8,128)(2,1)S(1)}, bf16[256,128]{1,0:T(8,128)(2,1)S(1)}, u32[]{:S(2)}, u32[]{:S(2)}) collective-permute-start(bf16[256,128]{1,0:T(8,128)(2,1)S(1)} %get-tuple-element.38), channel_id=1, source_target_pairs={{0,4},{4,0},{8,12},{12,8},{16,20},{20,16},{24,28},{28,24},{1,5},{5... | collective-permute-start | bytes 196616 | tf_op jit(solution)/shard_map/ppermute | solution.py:49
  151.4 14.9 %collective-permute-start.23 = (bf16[256,128]{1,0:T(8,128)(2,1)S(1)}, bf16[256,128]{1,0:T(8,128)(2,1)S(1)}, u32[]{:S(2)}, u32[]{:S(2)}) collective-permute-start(bf16[256,128]{1,0:T(8,128)(2,1)S(1)} %get-tuple-element.39), channel_id=1, source_target_pairs={{0,8},{4,12},{8,0},{12,4},{16,24},{20,28},{24,16},{28,20},{1,9},{5... | collective-permute-start | bytes 196616 | tf_op jit(solution)/shard_map/ppermute | solution.py:49
  170.8 7.5 %collective-permute-start.33 = (bf16[256,256]{1,0:T(8,128)(2,1)S(1)}, bf16[256,256]{1,0:T(8,128)(2,1)S(1)}, u32[]{:S(2)}, u32[]{:S(2)}) collective-permute-start(bf16[256,256]{1,0:T(8,128)(2,1)S(1)} %get-tuple-element.49), channel_id=1, source_target_pairs={{0,12},{4,8},{8,4},{12,0},{16,28},{20,24},{24,20},{28,16},{1,13},{... | collective-permute-start | bytes 393224 | tf_op jit(solution)/shard_map/ppermute | solution.py:49
  172.4 9.8 %collective-permute-start.20 = (bf16[256,256]{1,0:T(8,128)(2,1)S(1)}, bf16[256,256]{1,0:T(8,128)(2,1)S(1)}, u32[]{:S(2)}, u32[]{:S(2)}) collective-permute-start(bf16[256,256]{1,0:T(8,128)(2,1)S(1)} %get-tuple-element.35), channel_id=1, source_target_pairs={{0,8},{4,12},{8,0},{12,4},{16,24},{20,28},{24,16},{28,20},{1,9},{5... | collective-permute-start | bytes 393224 | tf_op jit(solution)/shard_map/ppermute | solution.py:49
  172.9 10.9 %collective-permute-start.21 = (bf16[256,256]{1,0:T(8,128)(2,1)S(1)}, bf16[256,256]{1,0:T(8,128)(2,1)S(1)}, u32[]{:S(2)}, u32[]{:S(2)}) collective-permute-start(bf16[256,256]{1,0:T(8,128)(2,1)S(1)} %get-tuple-element.36), channel_id=1, source_target_pairs={{0,12},{4,8},{8,4},{12,0},{16,28},{20,24},{24,20},{28,16},{1,13},{... | collective-permute-start | bytes 393224 | tf_op jit(solution)/shard_map/ppermute | solution.py:49
  (40 other events, 238.5 us)

commit v3 on v2

v3 whole, which is shorter than its diff:
```python
import functools

import jax
import jax.numpy as jnp
import numpy as np
from jax import lax
from jax.experimental import pallas as pl
from jax.experimental.pallas import tpu as pltpu
from jax.sharding import PartitionSpec as P

HD = 128
GROUP = 5
QBLK = 128
SEL = 4
TEAM = 4

norm_eps = 1e-06
rope_base = 10000000.0

CHUNKS = ((0, 3), (3, 5), (5, 7))
MIB = 1024 * 1024

SMEM = pl.BlockSpec(memory_space=pltpu.SMEM)
VMEM = pl.BlockSpec(memory_space=pltpu.VMEM)
ANY = pl.BlockSpec(memory_space=pl.ANY)
NOTE_ROWS = 16


def angle_tables(head_dim):
    half_dim = head_dim // 2
    frequency = rope_base ** (-2.0 * np.arange(half_dim) / head_dim)
    return np.stack(
        [np.mod(frequency * 32.0**digit_level, 2.0 * np.pi) for digit_level in range(4)]
    )


def rope_table(positions):
    tables = jnp.asarray(np.tile(angle_tables(HD), (1, 2)), jnp.float32)
    quarter = jnp.where(jnp.arange(HD) < HD // 2, 0.0, -np.pi / 2).astype(jnp.float32)
    angles = jnp.broadcast_to(quarter[None, :], (positions.shape[0], HD))
    remaining = positions
    for digit_level in range(4):
        digit_value = (remaining % 32).astype(jnp.float32)
        angles = angles + digit_value[:, None] * tables[digit_level][None, :]
        remaining = remaining // 32
    return jnp.cos(angles)


def swap(value, axis, bit):
    size = lax.axis_size(axis)
    return lax.ppermute(value, axis, [(i, i ^ bit) for i in range(size)])


def bits_of(size, low):
    bits = []
    bit = low
    while bit < size:
        bits.append(bit)
        bit *= 2
    return bits[::-1]


def tile_sources(first, last, group):
    parts = []
    for source in (0, 1):
        if first <= source < last:
            parts.append((source, group * HD, 1))
    query_first = max(first, 2)
    if last > query_first:
        parts.append((2, (group * GROUP + query_first - 2) * HD, last - query_first))
    return parts


def start_all(copies, sem):
    copies = [
        pltpu.make_async_copy(source, target, sem.at[index])
        for index, (source, target) in enumerate(copies)
    ]
    for copy in copies:
        copy.start()
    return copies


def cut_kernel(cut_rows, *refs):
    place_ref, wq_ref, wk_ref, wv_ref = refs[:4]
    half_refs = refs[4 : 4 + len(CHUNKS)]
    sem = refs[-1]
    local = pl.ds(pl.multiple_of(place_ref[1], 16), cut_rows)
    copies = []
    for (first, last), half_ref in zip(CHUNKS, half_refs):
        at = 0
        for source, column, tiles in tile_sources(first, last, place_ref[0]):
            column = pl.ds(pl.multiple_of(column, HD), tiles * HD)
            copies.append(
                (
                    (wk_ref, wv_ref, wq_ref)[source].at[local, column],
                    half_ref.at[:, pl.ds(at, tiles * HD)],
                )
            )
            at += tiles * HD
    for copy in start_all(copies, sem):
        copy.wait()


def cut(place, cut_rows, weights):
    shapes = [
        jax.ShapeDtypeStruct((cut_rows, (last - first) * HD), jnp.bfloat16)
        for first, last in CHUNKS
    ]
    count = sum(len(tile_sources(first, last, 0)) for first, last in CHUNKS)
    return pl.pallas_call(
        functools.partial(cut_kernel, cut_rows),
        out_shape=shapes,
        in_specs=[SMEM] + [ANY] * 3,
        out_specs=[VMEM] * len(shapes),
        scratch_shapes=[pltpu.SemaphoreType.DMA((count,))],
        compiler_params=pltpu.CompilerParams(vmem_limit_bytes=60 * MIB),
        name="cut",
    )(place, *weights)


def prep_kernel(team_count, split, *refs):
    tokens_ref, gain_ref, lists_ref, ck_ref, cv_ref = refs[:5]
    normed_refs = refs[5 : 5 + split]
    payload_ref, note_wide, note, sem = refs[5 + split :]
    prefix = ck_ref.shape[0]
    copies = []
    for target in range(TEAM * team_count):
        column = pl.ds(target % TEAM * HD, HD)
        body = payload_ref.at[target, pl.ds(0, prefix), :]
        copies.append((ck_ref.at[:, column], body.at[:, pl.ds(0, HD)]))
        copies.append((cv_ref.at[:, column], body.at[:, pl.ds(HD, HD)]))
    note_wide[...] = jnp.zeros_like(note_wide)
    note_wide[0:1, 0 : lists_ref.shape[1]] = lists_ref[...].astype(jnp.float32)
    note[...] = note_wide[...].astype(jnp.bfloat16)
    for target in range(TEAM * team_count):
        copies.append((note, payload_ref.at[target, pl.ds(prefix, NOTE_ROWS), :]))
    copies = start_all(copies, sem)
    rows = tokens_ref.shape[0] // split
    for index in range(split):
        widened = tokens_ref[pl.ds(index * rows, rows), :].astype(jnp.float32)
        normed_refs[index][...] = (
            widened
            * lax.rsqrt(jnp.mean(widened * widened, axis=-1, keepdims=True) + norm_eps)
            * gain_ref[...].astype(jnp.float32)
        ).astype(jnp.bfloat16)
    for copy in copies:
        copy.wait()


def prep(split, team_count, tokens, norm_gain, lists, caches):
    prefix = caches[0].shape[0]
    rows, depth = tokens.shape
    everyone = TEAM * team_count
    shapes = [jax.ShapeDtypeStruct((rows // split, depth), jnp.bfloat16)] * split
    shapes.append(
        jax.ShapeDtypeStruct((everyone, prefix + NOTE_ROWS, 2 * HD), jnp.bfloat16)
    )
    return pl.pallas_call(
        functools.partial(prep_kernel, team_count, split),
        out_shape=shapes,
        in_specs=[VMEM] * 3 + [ANY] * 2,
        out_specs=[VMEM] * split + [ANY],
        scratch_shapes=[
            pltpu.VMEM((NOTE_ROWS, 2 * HD), jnp.float32),
            pltpu.VMEM((NOTE_ROWS, 2 * HD), jnp.bfloat16),
            pltpu.SemaphoreType.DMA((3 * everyone,)),
        ],
        compiler_params=pltpu.CompilerParams(vmem_limit_bytes=14 * MIB),
        name="prep",
    )(tokens, norm_gain[None, :], lists[None, :], *caches)


def turned(value, cosine, sine):
    return value * cosine + pltpu.roll(value, HD // 2, 1) * sine


def heads_kernel(tiles, piece_count, x_count, *refs):
    first_tile, last_tile = tiles
    has_kv = first_tile == 0
    query_first = max(first_tile, 2)
    query_count = last_tile - query_first
    refs = list(refs)

    def take(count):
        taken = refs[:count]
        del refs[:count]
        return taken

    offsets_ref, lists_ref = take(2)
    x_refs = take(x_count)
    piece_refs = take(piece_count)
    local_ref, bias_ref, table_ref = take(3)
    (cache_ref,) = take(1)
    if not has_kv:
        key_ref, value_t_ref, cache_value_t_ref = take(3)
    out_refs = take(TEAM)
    if has_kv:
        key_ref, value_t_ref, cache_value_t_ref = take(3)
    w_buf, w_sem, q_buf = take(3)

    rows = sum(x_ref.shape[0] for x_ref in x_refs) // TEAM
    group = offsets_ref[0]
    copies = []
    for index, piece in enumerate((local_ref, *piece_refs)):
        start = pl.multiple_of(offsets_ref[1 + index], 16)
        copies.append((piece, w_buf.at[pl.ds(start, piece.shape[0]), :]))
    copies = start_all(copies, w_sem)
    blocks_each = (cache_ref.shape[1] - NOTE_ROWS) // QBLK

    def cached(place):
        if blocks_each == 1:
            return place, pl.ds(0, QBLK)
        return place // blocks_each, pl.ds(pl.multiple_of(place % blocks_each * QBLK, QBLK), QBLK)

    if has_kv:
        for place in range(blocks_each * cache_ref.shape[0]):
            owner, part = cached(place)
            cache_value_t_ref[place] = cache_ref[owner, part, pl.ds(HD, HD)].T
    for copy in copies:
        copy.wait()

    factor = HD ** (-0.5) * float(np.log2(np.e))
    causal = lax.broadcasted_iota(jnp.int32, (QBLK, QBLK), 0) <= lax.broadcasted_iota(
        jnp.int32, (QBLK, QBLK), 1
    )
    contract_last = (((1,), (1,)), ((), ()))
    blocks = rows // QBLK
    list_rows = blocks * SEL

    low_half = lax.broadcasted_iota(jnp.int32, (rows, HD), 1) < HD // 2
    for r in range(TEAM):
        span = pl.ds(r * rows, rows)
        parts, at = [], 0
        for x_ref in x_refs:
            if at // rows == r:
                parts.append(x_ref[...])
            at += x_ref.shape[0]
        x = jnp.concatenate(parts, axis=0) if len(parts) > 1 else parts[0]
        lin = jnp.dot(x, w_buf[...], preferred_element_type=jnp.float32) + bias_ref[...]
        table = table_ref[span, :]
        swapped = pltpu.roll(table, HD // 2, 1)
        cosine = jnp.where(low_half, table, swapped)
        sine = jnp.where(low_half, -swapped, table)
        for tile in range(first_tile, last_tile):
            at = (tile - first_tile) * HD
            value = lin[:, at : at + HD]
            if tile != 1:
                value = turned(value, cosine, sine)
            if tile >= 2:
                q_buf[span, pl.ds((tile - query_first) * HD, HD)] = value.astype(jnp.bfloat16)
                continue
            out_refs[r][:, pl.ds(at, HD)] = value.astype(out_refs[r].dtype)
            if tile == 0:
                key_ref[span, :] = value.astype(jnp.bfloat16)
            else:
                value_t_ref[:, span] = value.astype(jnp.bfloat16).T

    def one_unit(r, block, head):
            part_span = pl.ds(r * rows + block * QBLK, QBLK)
            near_key = key_ref[part_span, :]
            near_value = value_t_ref[:, part_span]
            query = q_buf[part_span, pl.ds(head * HD, HD)]
            at = (group * GROUP + query_first - 2 + head) * list_rows + block * SEL
            slots = [lists_ref[group ^ r, at + j] for j in range(SEL)]
            places = [jnp.maximum(slot, 0) for slot in slots]
            keys = [near_key]
            for place in places:
                owner, part = cached(place)
                keys.append(cache_ref[owner, part, pl.ds(0, HD)])
            keys = jnp.concatenate(keys, axis=0)
            values = jnp.concatenate(
                [near_value] + [cache_value_t_ref[place] for place in places], axis=1
            )
            scores = lax.dot_general(
                keys, query, contract_last, preferred_element_type=jnp.float32
            )
            parts = [jnp.where(causal, scores[:QBLK], -jnp.inf)]
            for j in range(SEL):
                part = scores[(j + 1) * QBLK : (j + 2) * QBLK]
                parts.append(part + jnp.where(slots[j] >= 0, 0.0, -jnp.inf))
            top = functools.reduce(jnp.maximum, parts)
            top = jnp.max(top, axis=0, keepdims=True) * factor
            parts = [jnp.exp2(part * factor - top) for part in parts]
            total = jnp.sum(functools.reduce(jnp.add, parts), axis=0, keepdims=True)
            weights = jnp.concatenate([part.astype(jnp.bfloat16) for part in parts], axis=0)
            mixed = jnp.dot(values, weights, preferred_element_type=jnp.float32)
            return (mixed / total).T

    for r in range(TEAM):
        for block in range(blocks):
            for head in range(query_count):
                out_refs[r][pl.ds(block * QBLK, QBLK), pl.ds((query_first - first_tile + head) * HD, HD)] = one_unit(r, block, head).astype(out_refs[r].dtype)


def heads(tiles, offsets, lists, x_parts, pieces, local, bias, table, cache, near):
    first_tile, last_tile = tiles
    has_kv = first_tile == 0
    query_count = last_tile - max(first_tile, 2)
    width = (last_tile - first_tile) * HD
    depth = x_parts[0].shape[1]
    everything = sum(part.shape[0] for part in x_parts)
    rows = everything // TEAM
    operands, specs = [], []

    def add(values, spec):
        operands.extend(values)
        specs.extend([spec] * len(values))

    add([offsets, lists], SMEM)
    add(x_parts, VMEM)
    add(pieces + [local], ANY)
    add([bias, table, cache], VMEM)
    if not has_kv:
        add(near, VMEM)
    shapes = []
    for r in range(TEAM):
        dtype = jnp.float32 if r == 0 else jnp.bfloat16
        shapes.append(jax.ShapeDtypeStruct((rows, width), dtype))
    if has_kv:
        total_blocks = cache.shape[0] * (cache.shape[1] - NOTE_ROWS) // QBLK
        shapes.append(jax.ShapeDtypeStruct((everything, HD), jnp.bfloat16))
        shapes.append(jax.ShapeDtypeStruct((HD, everything), jnp.bfloat16))
        shapes.append(jax.ShapeDtypeStruct((total_blocks, HD, QBLK), jnp.bfloat16))
    scratch = [
        pltpu.VMEM((depth, width), jnp.bfloat16),
        pltpu.SemaphoreType.DMA((len(pieces) + 1,)),
        pltpu.VMEM((everything, query_count * HD), jnp.bfloat16),
    ]
    return pl.pallas_call(
        functools.partial(heads_kernel, tiles, len(pieces), len(x_parts)),
        out_shape=shapes,
        in_specs=specs,
        out_specs=[VMEM] * len(shapes),
        scratch_shapes=scratch,
        compiler_params=pltpu.CompilerParams(vmem_limit_bytes=14 * MIB),
        cost_estimate=pl.CostEstimate(
            flops=2 * everything * depth * width,
            bytes_accessed=2 * depth * (everything + width),
            transcendentals=everything * query_count * (SEL + 1) * QBLK,
        ),
        name="heads",
    )(*operands)


def finish_kernel(places_ref, *refs):
    parts = refs[: TEAM * len(CHUNKS)]
    context_ref, keys_ref, values_ref = refs[TEAM * len(CHUNKS) :]
    for index, (first, last) in enumerate(CHUNKS):
        for r in range(TEAM):
            part = parts[index * TEAM + r]
            place = places_ref[0] ^ r
            at = 0
            for source, column, tiles in tile_sources(first, last, place):
                target = (keys_ref, values_ref, context_ref)[source]
                target[:, pl.ds(pl.multiple_of(column, HD), tiles * HD)] = part[
                    :, pl.ds(at, tiles * HD)
                ].astype(jnp.float32)
                at += tiles * HD


def finish(places, parts):
    rows = parts[0].shape[0]
    return pl.pallas_call(
        finish_kernel,
        out_shape=[
            jax.ShapeDtypeStruct((rows, TEAM * GROUP * HD), jnp.float32),
            jax.ShapeDtypeStruct((rows, TEAM * HD), jnp.float32),
            jax.ShapeDtypeStruct((rows, TEAM * HD), jnp.float32),
        ],
        in_specs=[SMEM] + [VMEM] * len(parts),
        out_specs=[VMEM] * 3,
        compiler_params=pltpu.CompilerParams(vmem_limit_bytes=14 * MIB),
        name="finish",
    )(places, *parts)


def on_device(
    tokens,
    norm_gain,
    w_query,
    w_key,
    w_value,
    b_query,
    b_key,
    b_value,
    cache_keys,
    cache_values,
    block_lists,
    start_position,
):
    rows = tokens.shape[0]
    shard = w_query.shape[0]
    ctx_size, grp_size = lax.axis_size("ctx"), lax.axis_size("grp")
    me, layer = lax.axis_index("ctx"), lax.axis_index("grp")
    group = me % TEAM
    sides = ctx_size // TEAM
    side = me // TEAM
    if (shard // sides) % 16:
        sides = 1
        side = side * 0
    piece_rows = shard // sides
    weights = (w_query, w_key, w_value)

    grp_bits = bits_of(grp_size, 1)
    side_bits = bits_of(ctx_size, TEAM) if sides > 1 else []
    grp_order = [0]
    for bit in grp_bits:
        grp_order += [far ^ bit for far in grp_order]
    piece_places = [(far, 0) for far in sorted(grp_order) if far]
    for bit in side_bits:
        piece_places += [(far, over ^ (bit // TEAM)) for far, over in piece_places]
    piece_places = sorted(piece_places)
    offsets = jnp.stack(
        [group, layer * shard]
        + [(layer ^ far) * shard + (side ^ over) * piece_rows for far, over in piece_places]
    ).astype(jnp.int32)
    place = jnp.stack([group, side * piece_rows]).astype(jnp.int32)

    halves = list(cut(place, piece_rows, weights))
    tokens, halves[0] = lax.optimization_barrier((tokens, halves[0]))
    *own_x, payload = prep(
        2,
        ctx_size // TEAM,
        tokens,
        norm_gain,
        block_lists.reshape(-1),
        (cache_keys, cache_values),
    )
    locals_ = cut(jnp.stack([group, 0]).astype(jnp.int32), shard, weights)

    cache = lax.all_to_all(payload, "ctx", 0, 0)
    lists = lax.dynamic_slice(
        cache,
        (me // TEAM * TEAM, cache_keys.shape[0], 0),
        (TEAM, 1, 2 * HD),
    )[:, 0, :].astype(jnp.int32)

    positions = jnp.concatenate(
        [
            start_position[0]
            + ((me ^ r) * grp_size + layer) * rows
            + jnp.arange(rows, dtype=jnp.int32)
            for r in range(TEAM)
        ]
    )
    table = rope_table(positions)
    bias = jnp.concatenate(
        [
            lax.dynamic_slice_in_dim(b_key, group * HD, HD),
            lax.dynamic_slice_in_dim(b_value, group * HD, HD),
            lax.dynamic_slice_in_dim(b_query, group * GROUP * HD, GROUP * HD),
        ]
    ).astype(jnp.float32)[None, :]

    tie = lax.optimization_barrier
    far_x = [swap(own_x[0], "ctx", 2)]
    first = grp_bits[0]
    near, parts = None, []
    held = None
    waiting = None

    def spread(held, index):
        for bit in grp_bits[1:]:
            for far in sorted(held):
                held[far ^ bit] = swap(held[far], "grp", bit)
        pieces = {(far, 0): held[far] for far in held if far}
        for bit in side_bits:
            for far, over in sorted(pieces):
                pieces[(far, over ^ (bit // TEAM))] = swap(pieces[(far, over)], "ctx", bit)
        return [pieces[key] for key in piece_places]

    def run(index, pieces, near):
        first_tile, last_tile = CHUNKS[index]
        results = heads(
            CHUNKS[index],
            offsets,
            lists,
            list(own_x) + [swap_own[0], swap_own[1]] + far_x + near_x,
            pieces,
            locals_[index],
            bias[:, first_tile * HD : last_tile * HD],
            table,
            cache,
            near,
        )
        if index == 0:
            near = results[TEAM:]
        back = [results[0]] + [swap(results[r], "ctx", r) for r in range(1, TEAM)]
        return back, near

    swap_own = [swap(part, "ctx", 1) for part in own_x]
    held0 = {0: halves[0], first: swap(halves[0], "grp", first)}
    halves[1], held0[first], cache, far_x[0], moving, table, bias = tie(
        (halves[1], held0[first], cache, far_x[0], own_x[1], table, bias)
    )
    far_x.append(swap(moving, "ctx", 2))
    held1 = {0: halves[1], first: swap(halves[1], "grp", first)}
    pieces0 = spread(held0, 0)
    halves[2], held1[first], far_x[1] = tie((halves[2], held1[first], far_x[1]))
    near_x = [swap(part, "ctx", 1) for part in far_x]
    held2 = {0: halves[2], first: swap(halves[2], "grp", first)}
    pieces1 = spread(held1, 1)
    back0, near = run(0, pieces0, None)
    held2[first], *near = tie((held2[first], *near))
    pieces2 = spread(held2, 2)
    back1, _ = run(1, pieces1, near)
    pieces2[0], *back0 = tie((pieces2[0], *back0))
    back2, _ = run(2, pieces2, near)
    return tuple(finish(place, back0 + back1 + back2))


def solution(mesh):
    in_specs = (
        P(("ctx", "grp"), None),
        P(),
        P("grp", None),
        P("grp", None),
        P("grp", None),
        P(),
        P(),
        P(),
        P("ctx", None),
        P("ctx", None),
        P(None, ("ctx", "grp"), None),
        P(),
    )
    out_specs = (P(("ctx", "grp"), None), P(("ctx", "grp"), None), P(("ctx", "grp"), None))
    return jax.shard_map(
        on_device, mesh=mesh, in_specs=in_specs, out_specs=out_specs, check_vma=False
    )
```

time: 187 us -> 124 us (0.66)
  waiting for transfers between devices: 77 us -> 37.7 us
  local copies, waits for them, and re-layouts: 21.4 us -> 10.7 us
  Pallas kernels: 42.2 us -> 32.1 us
  other arithmetic: 5.12 us -> 2.54 us
    ppermute x43 -> x33, waiting for transfers between devices: 77 us -> 33.6 us  [swap(): return lax.ppermute(value, axis, [(i, i ^ bit) for i in range(size)])]
    pallas_call x5 -> x7, Pallas kernels: 42.2 us -> 32.1 us  [the longest x3 22.2 us: heads(): pl.pallas_call(functools.partial(heads_kernel, tiles, len(pieces), len(x_...]
    unnamed x59 -> x52, local copies, waits for them, and re-layouts: 18.3 us -> 9.62 us
    ppermute x43 -> x33, starting transfers between devices: 39.2 us -> 34.6 us  [swap(): return lax.ppermute(value, axis, [(i, i ^ bit) for i in range(size)])]
    mul x1 -> x0, other arithmetic: 4.26 us -> none  [rope_tables(): return (jnp.cos(angles), jnp.sin(angles) * sign)]
    all_to_all x0 -> x1, waiting for transfers between devices: none -> 4.07 us  [on_device(): cache = lax.all_to_all(payload, 'ctx', 0, 0)]
    all_to_all x0 -> x1, starting transfers between devices: none -> 3.54 us  [on_device(): cache = lax.all_to_all(payload, 'ctx', 0, 0)]
  transfers between devices with their start and end apart: 43 -> 34, of which waited for: 14 -> 12; matrix products, arithmetic and copies ran while one was open for 4% -> 2% of each run, Pallas kernels for 20% -> 21%
where the time goes in v3:
time: 124 us; the launch traced here: 123 us
  starting transfers between devices  38.2 us (31%)
  waiting for transfers between devices  37.7 us (30%)
  Pallas kernels  32.1 us (26%)
  local copies, waits for them, and re-layouts  10.7 us (9%)
  other arithmetic  2.54 us (2%)
  between operations  1.69 us (1%)
    ppermute x33, starting transfers between devices, swap(): return lax.ppermute(value, axis, [(i, i ^ bit) for i in range(size)])  34.6 us
    ppermute x33, waiting for transfers between devices, swap(): return lax.ppermute(value, axis, [(i, i ^ bit) for i in range(size)])  33.6 us
    pallas_call x3, Pallas kernels, heads(): pl.pallas_call(functools.partial(heads_kernel, tiles, len(pieces), len(x_...  22.2 us
    unnamed x52, local copies, waits for them, and re-layouts  9.62 us
    pallas_call x2, Pallas kernels, cut(): pl.pallas_call(functools.partial(cut_kernel, cut_rows), out_shape=shapes,...  5.82 us
    all_to_all x1, waiting for transfers between devices, on_device(): cache = lax.all_to_all(payload, 'ctx', 0, 0)  4.07 us
    all_to_all x1, starting transfers between devices, on_device(): cache = lax.all_to_all(payload, 'ctx', 0, 0)  3.54 us
    pallas_call x1, Pallas kernels, finish(): pl.pallas_call(finish_kernel, out_shape=[jax.ShapeDtypeStruct((rows, TEAM...  2.68 us
  transfers between devices with their start and end apart: 34, of which 12 were waited for; matrix products, arithmetic and copies ran while one was open for 2% of the time, Pallas kernels for 21%

profile of v3, /device:TPU:0, one launch (start us, length us, event | category | flops | bytes accessed | tf_op | source)
XLA Modules:
  0.0 122.9 jit_solution(11420800480876652954)
XLA Ops:
  1.3 2.8 %cut.2 = (bf16[320,384]{1,0:T(8,128)(2,1)}, bf16[320,256]{1,0:T(8,128)(2,1)}, bf16[320,256]{1,0:T(8,128)(2,1)}) custom-call(s32[2]{0:T(128)} %get-tuple-element.99.refs_0_.places_ref, bf16[640,2560]{1,0:T(8,128)(2,1)} %refs_1_.3, bf16[640,512]{1,0:T(8,128)(2,1)} %refs_2_.3, bf16[640,512]{1,0:T(8,128)(2,1)} %refs_3_.5), custom_call_target="tpu_custom_call" | custom-call | tf_op jit(solution)/shard_map/cut/pallas_call | solution.py:111
  7.1 3.0 %collective-permute-start.1 = (bf16[128,2560]{1,0:T(8,128)(2,1)S(1)}, bf16[128,2560]{1,0:T(8,128)(2,1)S(1)}, u32[]{:S(2)}, u32[]{:S(2)}) collective-permute-start(bf16[128,2560]{1,0:T(8,128)(2,1)S(1)} %get-tuple-element.54.refs_2_), channel_id=1, source_target_pairs={{0,8},{4,12},{8,0},{12,4},{16,24},{20,28},{24,16},{28,20},{1,9},{5... | collective-permute-start | bytes 1966088 | tf_op jit(solution)/shard_map/ppermute | solution.py:51
  10.2 3.5 %all-to-all-start = ((bf16[8,144,256]{2,1,0:T(8,128)(2,1)}), bf16[8,144,256]{2,1,0:T(8,128)(2,1)S(1)}, u32[]{:S(2)}, u32[]{:S(2)}) async-start(bf16[8,144,256]{2,1,0:T(8,128)(2,1)} %get-tuple-element.53), calls=%async_computation | async-start | bytes 1179648 | tf_op jit(solution)/shard_map/all_to_all | solution.py:432
  13.7 2.7 %collective-permute-start = (bf16[320,384]{1,0:T(8,128)(2,1)}, bf16[320,384]{1,0:T(8,128)(2,1)S(1)}, u32[]{:S(2)}, u32[]{:S(2)}) collective-permute-start(bf16[320,384]{1,0:T(8,128)(2,1)} %get-tuple-element.51), channel_id=1, source_target_pairs={{0,2},{1,3},{2,0},{3,1},{4,6},{5,7},{6,4},{7,5},{8,10},{9,11},{10,... | collective-permute-start | bytes 737288 | tf_op jit(solution)/shard_map/ppermute | solution.py:51
  18.0 1.9 %add_cosine_fusion.refs_18_ = f32[1024,128]{1,0:T(8,128)S(1)} fusion(f32[128]{0:T(128)S(1)} %copy-done.21, f32[1024]{0:T(1024)S(1)} %get-tuple-element.95, f32[128]{0:T(128)S(1)} %copy-done.20, f32[1024]{0:T(1024)S(1)} %get-tuple-element.94, f32[128]{0:T(128)S(1)} %copy-done.19, f32[1024]{0:T(1024)S(1)} %get-tuple-element.96, f32[128]{0:T(128)S(1)} %copy-done.18, ...), kind=kLoop, calls=%fused_computation | loop fusion | flops 1048576 | bytes 543232 | tf_op jit(solution)/shard_map/cos | solution.py:46
  19.9 8.5 %collective-permute-done.refs_12_ = bf16[320,384]{1,0:T(8,128)(2,1)S(1)} collective-permute-done((bf16[320,384]{1,0:T(8,128)(2,1)}, bf16[320,384]{1,0:T(8,128)(2,1)S(1)}, u32[]{:S(2)}, u32[]{:S(2)}) %collective-permute-start) | collective-permute-done | bytes 245792 | tf_op jit(solution)/shard_map/ppermute | solution.py:51
  28.3 4.1 %all-to-all-done.refs_19_ = bf16[8,144,256]{2,1,0:T(8,128)(2,1)S(1)} async-done(((bf16[8,144,256]{2,1,0:T(8,128)(2,1)}), bf16[8,144,256]{2,1,0:T(8,128)(2,1)S(1)}, u32[]{:S(2)}, u32[]{:S(2)}) %all-to-all-start) | async-done | bytes 589856 | tf_op jit(solution)/shard_map/all_to_all | solution.py:432
  33.1 1.6 %collective-permute-start.9 = (bf16[320,384]{1,0:T(8,128)(2,1)}, bf16[320,384]{1,0:T(8,128)(2,1)S(1)}, u32[]{:S(2)}, u32[]{:S(2)}) collective-permute-start(bf16[320,384]{1,0:T(8,128)(2,1)} %get-tuple-element.51), channel_id=1, source_target_pairs={{0,1},{1,0},{2,3},{3,2},{4,5},{5,4},{6,7},{7,6},{8,9},{9,8},{10,11... | collective-permute-start | bytes 737288 | tf_op jit(solution)/shard_map/ppermute | solution.py:51
  35.2 2.6 %collective-permute-start.2 = (bf16[320,256]{1,0:T(8,128)(2,1)}, bf16[320,256]{1,0:T(8,128)(2,1)S(1)}, u32[]{:S(2)}, u32[]{:S(2)}) collective-permute-start(bf16[320,256]{1,0:T(8,128)(2,1)} %get-tuple-element.56), channel_id=1, source_target_pairs={{0,2},{1,3},{2,0},{3,1},{4,6},{5,7},{6,4},{7,5},{8,10},{9,11},{10,... | collective-permute-start | bytes 491528 | tf_op jit(solution)/shard_map/ppermute | solution.py:51
  37.8 2.3 %collective-permute-done.9.refs_10_ = bf16[320,384]{1,0:T(8,128)(2,1)S(1)} collective-permute-done((bf16[320,384]{1,0:T(8,128)(2,1)}, bf16[320,384]{1,0:T(8,128)(2,1)S(1)}, u32[]{:S(2)}, u32[]{:S(2)}) %collective-permute-start.9) | collective-permute-done | bytes 245792 | tf_op jit(solution)/shard_map/ppermute | solution.py:51
  42.2 3.7 %collective-permute-done.2.refs_12_ = bf16[320,256]{1,0:T(8,128)(2,1)S(1)} collective-permute-done((bf16[320,256]{1,0:T(8,128)(2,1)}, bf16[320,256]{1,0:T(8,128)(2,1)S(1)}, u32[]{:S(2)}, u32[]{:S(2)}) %collective-permute-start.2) | collective-permute-done | bytes 163872 | tf_op jit(solution)/shard_map/ppermute | solution.py:51
  48.0 1.6 %collective-permute-start.12 = (bf16[320,384]{1,0:T(8,128)(2,1)S(1)}, bf16[320,384]{1,0:T(8,128)(2,1)}, u32[]{:S(2)}, u32[]{:S(2)}) collective-permute-start(bf16[320,384]{1,0:T(8,128)(2,1)S(1)} %collective-permute-done.refs_12_), channel_id=1, source_target_pairs={{0,1},{1,0},{2,3},{3,2},{4,5},{5,4},{6,7},{7,6},{8,9},{9,8},{10,11... | collective-permute-start | bytes 737288 | tf_op jit(solution)/shard_map/ppermute | solution.py:51
  50.9 5.5 %collective-permute-done.12.refs_14_ = bf16[320,384]{1,0:T(8,128)(2,1)} collective-permute-done((bf16[320,384]{1,0:T(8,128)(2,1)S(1)}, bf16[320,384]{1,0:T(8,128)(2,1)}, u32[]{:S(2)}, u32[]{:S(2)}) %collective-permute-start.12) | collective-permute-done | bytes 245792 | tf_op jit(solution)/shard_map/ppermute | solution.py:51
  57.8 1.6 %collective-permute-start.17 = (bf16[320,256]{1,0:T(8,128)(2,1)}, bf16[320,256]{1,0:T(8,128)(2,1)}, u32[]{:S(2)}, u32[]{:S(2)}) collective-permute-start(bf16[320,256]{1,0:T(8,128)(2,1)} %get-tuple-element.56), channel_id=1, source_target_pairs={{0,1},{1,0},{2,3},{3,2},{4,5},{5,4},{6,7},{7,6},{8,9},{9,8},{10,11... | collective-permute-start | bytes 491528 | tf_op jit(solution)/shard_map/ppermute | solution.py:51
  59.4 3.0 %cut.3 = (bf16[640,384]{1,0:T(8,128)(2,1)}, bf16[640,256]{1,0:T(8,128)(2,1)}, bf16[640,256]{1,0:T(8,128)(2,1)}) custom-call(s32[2]{0:T(128)} %get-tuple-element.100.refs_0_, bf16[640,2560]{1,0:T(8,128)(2,1)} %refs_1_.3, bf16[640,512]{1,0:T(8,128)(2,1)} %refs_2_.3, bf16[640,512]{1,0:T(8,128)(2,1)} %refs_3_.5), custom_call_target="tpu_custom_call" | custom-call | tf_op jit(solution)/shard_map/cut/pallas_call | solution.py:111
  63.7 1.5 %collective-permute-start.18 = (bf16[320,256]{1,0:T(8,128)(2,1)}, bf16[320,256]{1,0:T(8,128)(2,1)S(1)}, u32[]{:S(2)}, u32[]{:S(2)}) collective-permute-start(bf16[320,256]{1,0:T(8,128)(2,1)} %collective-permute-done.17.refs_10_), channel_id=1, source_target_pairs={{0,16},{4,20},{8,24},{12,28},{16,0},{20,4},{24,8},{28,12},{1,17},{... | collective-permute-start | bytes 491528 | tf_op jit(solution)/shard_map/ppermute | solution.py:51
  65.2 2.5 %collective-permute-start.22 = (bf16[320,256]{1,0:T(8,128)(2,1)}, bf16[320,256]{1,0:T(8,128)(2,1)S(1)}, u32[]{:S(2)}, u32[]{:S(2)}) collective-permute-start(bf16[320,256]{1,0:T(8,128)(2,1)} %get-tuple-element.58), channel_id=1, source_target_pairs={{0,2},{1,3},{2,0},{3,1},{4,6},{5,7},{6,4},{7,5},{8,10},{9,11},{10,... | collective-permute-start | bytes 491528 | tf_op jit(solution)/shard_map/ppermute | solution.py:51
  67.7 1.6 %collective-permute-start.20 = (bf16[320,256]{1,0:T(8,128)(2,1)S(1)}, bf16[320,256]{1,0:T(8,128)(2,1)S(1)}, u32[]{:S(2)}, u32[]{:S(2)}) collective-permute-start(bf16[320,256]{1,0:T(8,128)(2,1)S(1)} %collective-permute-done.2.refs_12_), channel_id=1, source_target_pairs={{0,1},{1,0},{2,3},{3,2},{4,5},{5,4},{6,7},{7,6},{8,9},{9,8},{10,11... | collective-permute-start | bytes 491528 | tf_op jit(solution)/shard_map/ppermute | solution.py:51
  74.4 8.4 %heads.3 = (f32[256,384]{1,0:T(8,128)S(1)}, bf16[256,384]{1,0:T(8,128)(2,1)S(1)}, bf16[256,384]{1,0:T(8,128)(2,1)S(1)}, bf16[256,384]{1,0:T(8,128)(2,1)S(1)}, bf...) custom-call(s32[8]{0:T(128)S(1)} %stack.48.refs_0_, ...), custom_call_target="tpu_custom_call" | custom-call | flops 2013265920 | bytes 7208960 | tf_op jit(solution)/shard_map/heads/pallas_call | solution.py:330
  83.8 1.6 %collective-permute-start.21 = (bf16[320,256]{1,0:T(8,128)(2,1)S(1)}, bf16[320,256]{1,0:T(8,128)(2,1)S(1)}, u32[]{:S(2)}, u32[]{:S(2)}) collective-permute-start(bf16[320,256]{1,0:T(8,128)(2,1)S(1)} %collective-permute-done.20.refs_14_), channel_id=1, source_target_pairs={{0,16},{4,20},{8,24},{12,28},{16,0},{20,4},{24,8},{28,12},{1,17},{... | collective-permute-start | bytes 491528 | tf_op jit(solution)/shard_map/ppermute | solution.py:51
  85.5 1.6 %collective-permute-start.28 = (bf16[320,256]{1,0:T(8,128)(2,1)S(1)}, bf16[320,256]{1,0:T(8,128)(2,1)S(1)}, u32[]{:S(2)}, u32[]{:S(2)}) collective-permute-start(bf16[320,256]{1,0:T(8,128)(2,1)S(1)} %collective-permute-done.22.refs_12_), channel_id=1, source_target_pairs={{0,1},{1,0},{2,3},{3,2},{4,5},{5,4},{6,7},{7,6},{8,9},{9,8},{10,11... | collective-permute-start | bytes 491528 | tf_op jit(solution)/shard_map/ppermute | solution.py:51
  87.1 2.9 %collective-permute-done.4.refs_10_ = bf16[320,256]{1,0:T(8,128)(2,1)S(1)} collective-permute-done((bf16[320,256]{1,0:T(8,128)(2,1)S(1)}, bf16[320,256]{1,0:T(8,128)(2,1)S(1)}, u32[]{:S(2)}, u32[]{:S(2)}) %collective-permute-start.4) | collective-permute-done | bytes 163872 | tf_op jit(solution)/shard_map/ppermute | solution.py:51
  90.5 1.6 %collective-permute-start.27 = (bf16[320,256]{1,0:T(8,128)(2,1)S(1)}, bf16[320,256]{1,0:T(8,128)(2,1)S(1)}, u32[]{:S(2)}, u32[]{:S(2)}) collective-permute-start(bf16[320,256]{1,0:T(8,128)(2,1)S(1)} %collective-permute-done.22.refs_12_), channel_id=1, source_target_pairs={{0,16},{4,20},{8,24},{12,28},{16,0},{20,4},{24,8},{28,12},{1,17},{... | collective-permute-start | bytes 491528 | tf_op jit(solution)/shard_map/ppermute | solution.py:51
  92.1 1.9 %collective-permute-done.21.refs_15_ = bf16[320,256]{1,0:T(8,128)(2,1)S(1)} collective-permute-done((bf16[320,256]{1,0:T(8,128)(2,1)S(1)}, bf16[320,256]{1,0:T(8,128)(2,1)S(1)}, u32[]{:S(2)}, u32[]{:S(2)}) %collective-permute-start.21) | collective-permute-done | bytes 163872 | tf_op jit(solution)/shard_map/ppermute | solution.py:51
  94.4 1.8 %collective-permute-start.29 = (bf16[320,256]{1,0:T(8,128)(2,1)S(1)}, bf16[320,256]{1,0:T(8,128)(2,1)S(1)}, u32[]{:S(2)}, u32[]{:S(2)}) collective-permute-start(bf16[320,256]{1,0:T(8,128)(2,1)S(1)} %collective-permute-done.28.refs_14_), channel_id=1, source_target_pairs={{0,16},{4,20},{8,24},{12,28},{16,0},{20,4},{24,8},{28,12},{1,17},{... | collective-permute-start | bytes 491528 | tf_op jit(solution)/shard_map/ppermute | solution.py:51
  96.2 6.9 %heads.4 = (f32[256,256]{1,0:T(8,128)S(1)}, bf16[256,256]{1,0:T(8,128)(2,1)S(1)}, bf16[256,256]{1,0:T(8,128)(2,1)S(1)}, bf16[256,256]{1,0:T(8,128)(2,1)S(1)}) custom-call(s32[8]{0:T(128)S(1)} %stack.48.refs_0_, s32[4,256]{1,0:T(4,128)S(1)} %bitcast.22, bf16[128,2560]{1,0:T(8,128)(2,1)S(1)} %get-tuple-element.54.refs_2_, ...), custom_call_target="tpu_custom_call" | custom-call | flops 1342177280 | bytes 6553600 | tf_op jit(solution)/shard_map/heads/pallas_call | solution.py:330
  103.2 1.7 %collective-permute-start.24 = (bf16[256,256]{1,0:T(8,128)(2,1)S(1)}, bf16[256,256]{1,0:T(8,128)(2,1)S(1)}, u32[]{:S(2)}, u32[]{:S(2)}) collective-permute-start(bf16[256,256]{1,0:T(8,128)(2,1)S(1)} %get-tuple-element.84), channel_id=1, source_target_pairs={{0,8},{4,12},{8,0},{12,4},{16,24},{20,28},{24,16},{28,20},{1,9},{5... | collective-permute-start | bytes 393224 | tf_op jit(solution)/shard_map/ppermute | solution.py:51
  105.2 6.9 %heads.5 = (f32[256,256]{1,0:T(8,128)S(1)}, bf16[256,256]{1,0:T(8,128)(2,1)S(1)}, bf16[256,256]{1,0:T(8,128)(2,1)S(1)}, bf16[256,256]{1,0:T(8,128)(2,1)S(1)}) custom-call(s32[8]{0:T(128)S(1)} %stack.48.refs_0_, s32[4,256]{1,0:T(4,128)S(1)} %bitcast.23, bf16[128,2560]{1,0:T(8,128)(2,1)S(1)} %get-tuple-element.54.refs_2_, ...), custom_call_target="tpu_custom_call" | custom-call | flops 1342177280 | bytes 6553600 | tf_op jit(solution)/shard_map/heads/pallas_call | solution.py:330
  112.4 1.7 %collective-permute-start.31 = (bf16[256,256]{1,0:T(8,128)(2,1)S(1)}, bf16[256,256]{1,0:T(8,128)(2,1)S(1)}, u32[]{:S(2)}, u32[]{:S(2)}) collective-permute-start(bf16[256,256]{1,0:T(8,128)(2,1)S(1)} %get-tuple-element.91), channel_id=1, source_target_pairs={{0,8},{4,12},{8,0},{12,4},{16,24},{20,28},{24,16},{28,20},{1,9},{5... | collective-permute-start | bytes 393224 | tf_op jit(solution)/shard_map/ppermute | solution.py:51
  114.1 4.6 %collective-permute-done.31.refs_10_ = bf16[256,256]{1,0:T(8,128)(2,1)S(1)} collective-permute-done((bf16[256,256]{1,0:T(8,128)(2,1)S(1)}, bf16[256,256]{1,0:T(8,128)(2,1)S(1)}, u32[]{:S(2)}, u32[]{:S(2)}) %collective-permute-start.31) | collective-permute-done | bytes 131104 | tf_op jit(solution)/shard_map/ppermute | solution.py:51
  118.7 1.5 %collective-permute-done.32.refs_11_ = bf16[256,256]{1,0:T(8,128)(2,1)S(1)} collective-permute-done((bf16[256,256]{1,0:T(8,128)(2,1)S(1)}, bf16[256,256]{1,0:T(8,128)(2,1)S(1)}, u32[]{:S(2)}, u32[]{:S(2)}) %collective-permute-start.32) | collective-permute-done | bytes 131104 | tf_op jit(solution)/shard_map/ppermute | solution.py:51
  120.2 2.7 %finish.1 = (f32[256,2560]{1,0:T(8,128)}, f32[256,512]{1,0:T(8,128)}, f32[256,512]{1,0:T(8,128)}) custom-call(s32[2]{0:T(128)S(1)} %copy-done.15, f32[256,384]{1,0:T(8,128)S(1)} %get-tuple-element.70.refs_0_, bf16[256,384]{1,0:T(8,128)(2,1)S(1)} %collective-permute-done.14.refs_1_, bf16[256,384]{1,0:T(8,128)(2,1)S(1)} %collective-permute-done.15.refs_2_, ...), custom_call_target="tpu_custom_call" | custom-call | tf_op jit(solution)/shard_map/finish/pallas_call | solution.py:364
  (111 shorter events, 21.4 us)
Async XLA Ops:
  7.1 25.3 %collective-permute-start.1 = (bf16[128,2560]{1,0:T(8,128)(2,1)S(1)}, bf16[128,2560]{1,0:T(8,128)(2,1)S(1)}, u32[]{:S(2)}, u32[]{:S(2)}) collective-permute-start(bf16[128,2560]{1,0:T(8,128)(2,1)S(1)} %get-tuple-element.54.refs_2_), channel_id=1, source_target_pairs={{0,8},{4,12},{8,0},{12,4},{16,24},{20,28},{24,16},{28,20},{1,9},{5... | collective-permute-start | bytes 1966088 | tf_op jit(solution)/shard_map/ppermute | solution.py:51
  10.2 22.3 %all-to-all-start = ((bf16[8,144,256]{2,1,0:T(8,128)(2,1)}), bf16[8,144,256]{2,1,0:T(8,128)(2,1)S(1)}, u32[]{:S(2)}, u32[]{:S(2)}) async-start(bf16[8,144,256]{2,1,0:T(8,128)(2,1)} %get-tuple-element.53), calls=%async_computation | async-start | bytes 1179648 | tf_op jit(solution)/shard_map/all_to_all | solution.py:432
  13.7 14.6 %collective-permute-start = (bf16[320,384]{1,0:T(8,128)(2,1)}, bf16[320,384]{1,0:T(8,128)(2,1)S(1)}, u32[]{:S(2)}, u32[]{:S(2)}) collective-permute-start(bf16[320,384]{1,0:T(8,128)(2,1)} %get-tuple-element.51), channel_id=1, source_target_pairs={{0,2},{1,3},{2,0},{3,1},{4,6},{5,7},{6,4},{7,5},{8,10},{9,11},{10,... | collective-permute-start | bytes 737288 | tf_op jit(solution)/shard_map/ppermute | solution.py:51
  32.4 14.8 %collective-permute-start.3 = (bf16[128,2560]{1,0:T(8,128)(2,1)S(1)}, bf16[128,2560]{1,0:T(8,128)(2,1)}, u32[]{:S(2)}, u32[]{:S(2)}) collective-permute-start(bf16[128,2560]{1,0:T(8,128)(2,1)S(1)} %get-tuple-element.57.refs_3_), channel_id=1, source_target_pairs={{0,8},{4,12},{8,0},{12,4},{16,24},{20,28},{24,16},{28,20},{1,9},{5... | collective-permute-start | bytes 1966088 | tf_op jit(solution)/shard_map/ppermute | solution.py:51
  33.1 7.0 %collective-permute-start.9 = (bf16[320,384]{1,0:T(8,128)(2,1)}, bf16[320,384]{1,0:T(8,128)(2,1)S(1)}, u32[]{:S(2)}, u32[]{:S(2)}) collective-permute-start(bf16[320,384]{1,0:T(8,128)(2,1)} %get-tuple-element.51), channel_id=1, source_target_pairs={{0,1},{1,0},{2,3},{3,2},{4,5},{5,4},{6,7},{7,6},{8,9},{9,8},{10,11... | collective-permute-start | bytes 737288 | tf_op jit(solution)/shard_map/ppermute | solution.py:51
  34.7 14.8 %collective-permute-start.5 = (bf16[128,2560]{1,0:T(8,128)(2,1)S(1)}, bf16[128,2560]{1,0:T(8,128)(2,1)S(1)}, u32[]{:S(2)}, u32[]{:S(2)}) collective-permute-start(bf16[128,2560]{1,0:T(8,128)(2,1)S(1)} %get-tuple-element.54.refs_2_), channel_id=1, source_target_pairs={{0,4},{4,0},{8,12},{12,8},{16,20},{20,16},{24,28},{28,24},{1,5},{5... | collective-permute-start | bytes 1966088 | tf_op jit(solution)/shard_map/ppermute | solution.py:51
  34.7 22.3 %collective-permute-start.6 = (bf16[128,2560]{1,0:T(8,128)(2,1)S(1)}, bf16[128,2560]{1,0:T(8,128)(2,1)S(1)}, u32[]{:S(2)}, u32[]{:S(2)}) collective-permute-start(bf16[128,2560]{1,0:T(8,128)(2,1)S(1)} %get-tuple-element.57.refs_3_), channel_id=1, source_target_pairs={{0,4},{4,0},{8,12},{12,8},{16,20},{20,16},{24,28},{28,24},{1,5},{5... | collective-permute-start | bytes 1966088 | tf_op jit(solution)/shard_map/ppermute | solution.py:51
  35.2 10.6 %collective-permute-start.2 = (bf16[320,256]{1,0:T(8,128)(2,1)}, bf16[320,256]{1,0:T(8,128)(2,1)S(1)}, u32[]{:S(2)}, u32[]{:S(2)}) collective-permute-start(bf16[320,256]{1,0:T(8,128)(2,1)} %get-tuple-element.56), channel_id=1, source_target_pairs={{0,2},{1,3},{2,0},{3,1},{4,6},{5,7},{6,4},{7,5},{8,10},{9,11},{10,... | collective-permute-start | bytes 491528 | tf_op jit(solution)/shard_map/ppermute | solution.py:51
  40.1 7.1 %collective-permute-start.10 = (bf16[320,384]{1,0:T(8,128)(2,1)S(1)}, bf16[320,384]{1,0:T(8,128)(2,1)S(1)}, u32[]{:S(2)}, u32[]{:S(2)}) collective-permute-start(bf16[320,384]{1,0:T(8,128)(2,1)S(1)} %collective-permute-done.9.refs_10_), channel_id=1, source_target_pairs={{0,16},{4,20},{8,24},{12,28},{16,0},{20,4},{24,8},{28,12},{1,17},{... | collective-permute-start | bytes 737288 | tf_op jit(solution)/shard_map/ppermute | solution.py:51
  45.8 23.5 %collective-permute-start.7 = (bf16[128,2560]{1,0:T(8,128)(2,1)S(1)}, bf16[128,2560]{1,0:T(8,128)(2,1)}, u32[]{:S(2)}, u32[]{:S(2)}) collective-permute-start(bf16[128,2560]{1,0:T(8,128)(2,1)S(1)} %collective-permute-done.1.refs_6_), channel_id=1, source_target_pairs={{0,4},{4,0},{8,12},{12,8},{16,20},{20,16},{24,28},{28,24},{1,5},{5... | collective-permute-start | bytes 1966088 | tf_op jit(solution)/shard_map/ppermute | solution.py:51
  47.3 22.1 %collective-permute-start.8 = (bf16[128,2560]{1,0:T(8,128)(2,1)}, bf16[128,2560]{1,0:T(8,128)(2,1)}, u32[]{:S(2)}, u32[]{:S(2)}) collective-permute-start(bf16[128,2560]{1,0:T(8,128)(2,1)} %collective-permute-done.3.refs_7_), channel_id=1, source_target_pairs={{0,4},{4,0},{8,12},{12,8},{16,20},{20,16},{24,28},{28,24},{1,5},{5... | collective-permute-start | bytes 1966088 | tf_op jit(solution)/shard_map/ppermute | solution.py:51
  48.0 8.5 %collective-permute-start.12 = (bf16[320,384]{1,0:T(8,128)(2,1)S(1)}, bf16[320,384]{1,0:T(8,128)(2,1)}, u32[]{:S(2)}, u32[]{:S(2)}) collective-permute-start(bf16[320,384]{1,0:T(8,128)(2,1)S(1)} %collective-permute-done.refs_12_), channel_id=1, source_target_pairs={{0,1},{1,0},{2,3},{3,2},{4,5},{5,4},{6,7},{7,6},{8,9},{9,8},{10,11... | collective-permute-start | bytes 737288 | tf_op jit(solution)/shard_map/ppermute | solution.py:51
  50.4 14.8 %collective-permute-start.11 = (bf16[320,384]{1,0:T(8,128)(2,1)S(1)}, bf16[320,384]{1,0:T(8,128)(2,1)}, u32[]{:S(2)}, u32[]{:S(2)}) collective-permute-start(bf16[320,384]{1,0:T(8,128)(2,1)S(1)} %collective-permute-done.refs_12_), channel_id=1, source_target_pairs={{0,16},{4,20},{8,24},{12,28},{16,0},{20,4},{24,8},{28,12},{1,17},{... | collective-permute-start | bytes 737288 | tf_op jit(solution)/shard_map/ppermute | solution.py:51
  56.4 11.2 %collective-permute-start.13 = (bf16[320,384]{1,0:T(8,128)(2,1)}, bf16[320,384]{1,0:T(8,128)(2,1)}, u32[]{:S(2)}, u32[]{:S(2)}) collective-permute-start(bf16[320,384]{1,0:T(8,128)(2,1)} %collective-permute-done.12.refs_14_), channel_id=1, source_target_pairs={{0,16},{4,20},{8,24},{12,28},{16,0},{20,4},{24,8},{28,12},{1,17},{... | collective-permute-start | bytes 737288 | tf_op jit(solution)/shard_map/ppermute | solution.py:51
  63.7 21.8 %collective-permute-start.18 = (bf16[320,256]{1,0:T(8,128)(2,1)}, bf16[320,256]{1,0:T(8,128)(2,1)S(1)}, u32[]{:S(2)}, u32[]{:S(2)}) collective-permute-start(bf16[320,256]{1,0:T(8,128)(2,1)} %collective-permute-done.17.refs_10_), channel_id=1, source_target_pairs={{0,16},{4,20},{8,24},{12,28},{16,0},{20,4},{24,8},{28,12},{1,17},{... | collective-permute-start | bytes 491528 | tf_op jit(solution)/shard_map/ppermute | solution.py:51
  65.2 18.3 %collective-permute-start.22 = (bf16[320,256]{1,0:T(8,128)(2,1)}, bf16[320,256]{1,0:T(8,128)(2,1)S(1)}, u32[]{:S(2)}, u32[]{:S(2)}) collective-permute-start(bf16[320,256]{1,0:T(8,128)(2,1)} %get-tuple-element.58), channel_id=1, source_target_pairs={{0,2},{1,3},{2,0},{3,1},{4,6},{5,7},{6,4},{7,5},{8,10},{9,11},{10,... | collective-permute-start | bytes 491528 | tf_op jit(solution)/shard_map/ppermute | solution.py:51
  67.7 16.1 %collective-permute-start.20 = (bf16[320,256]{1,0:T(8,128)(2,1)S(1)}, bf16[320,256]{1,0:T(8,128)(2,1)S(1)}, u32[]{:S(2)}, u32[]{:S(2)}) collective-permute-start(bf16[320,256]{1,0:T(8,128)(2,1)S(1)} %collective-permute-done.2.refs_12_), channel_id=1, source_target_pairs={{0,1},{1,0},{2,3},{3,2},{4,5},{5,4},{6,7},{7,6},{8,9},{9,8},{10,11... | collective-permute-start | bytes 491528 | tf_op jit(solution)/shard_map/ppermute | solution.py:51
  82.9 11.5 %collective-permute-start.14 = (bf16[256,384]{1,0:T(8,128)(2,1)S(1)}, bf16[256,384]{1,0:T(8,128)(2,1)S(1)}, u32[]{:S(2)}, u32[]{:S(2)}) collective-permute-start(bf16[256,384]{1,0:T(8,128)(2,1)S(1)} %get-tuple-element.67), channel_id=1, source_target_pairs={{0,4},{4,0},{8,12},{12,8},{16,20},{20,16},{24,28},{28,24},{1,5},{5... | collective-permute-start | bytes 589832 | tf_op jit(solution)/shard_map/ppermute | solution.py:51
  83.0 7.1 %collective-permute-start.4 = (bf16[320,256]{1,0:T(8,128)(2,1)S(1)}, bf16[320,256]{1,0:T(8,128)(2,1)S(1)}, u32[]{:S(2)}, u32[]{:S(2)}) collective-permute-start(bf16[320,256]{1,0:T(8,128)(2,1)S(1)} %copy-done.24), channel_id=1, source_target_pairs={{0,1},{1,0},{2,3},{3,2},{4,5},{5,4},{6,7},{7,6},{8,9},{9,8},{10,11... | collective-permute-start | bytes 491528 | tf_op jit(solution)/shard_map/ppermute | solution.py:51
  83.4 7.0 %collective-permute-start.19 = (bf16[320,256]{1,0:T(8,128)(2,1)S(1)}, bf16[320,256]{1,0:T(8,128)(2,1)S(1)}, u32[]{:S(2)}, u32[]{:S(2)}) collective-permute-start(bf16[320,256]{1,0:T(8,128)(2,1)S(1)} %collective-permute-done.2.refs_12_), channel_id=1, source_target_pairs={{0,16},{4,20},{8,24},{12,28},{16,0},{20,4},{24,8},{28,12},{1,17},{... | collective-permute-start | bytes 491528 | tf_op jit(solution)/shard_map/ppermute | solution.py:51
  83.8 10.2 %collective-permute-start.21 = (bf16[320,256]{1,0:T(8,128)(2,1)S(1)}, bf16[320,256]{1,0:T(8,128)(2,1)S(1)}, u32[]{:S(2)}, u32[]{:S(2)}) collective-permute-start(bf16[320,256]{1,0:T(8,128)(2,1)S(1)} %collective-permute-done.20.refs_14_), channel_id=1, source_target_pairs={{0,16},{4,20},{8,24},{12,28},{16,0},{20,4},{24,8},{28,12},{1,17},{... | collective-permute-start | bytes 491528 | tf_op jit(solution)/shard_map/ppermute | solution.py:51
  85.5 8.9 %collective-permute-start.28 = (bf16[320,256]{1,0:T(8,128)(2,1)S(1)}, bf16[320,256]{1,0:T(8,128)(2,1)S(1)}, u32[]{:S(2)}, u32[]{:S(2)}) collective-permute-start(bf16[320,256]{1,0:T(8,128)(2,1)S(1)} %collective-permute-done.22.refs_12_), channel_id=1, source_target_pairs={{0,1},{1,0},{2,3},{3,2},{4,5},{5,4},{6,7},{7,6},{8,9},{9,8},{10,11... | collective-permute-start | bytes 491528 | tf_op jit(solution)/shard_map/ppermute | solution.py:51
  90.0 14.9 %collective-permute-start.26 = (bf16[320,256]{1,0:T(8,128)(2,1)S(1)}, bf16[320,256]{1,0:T(8,128)(2,1)S(1)}, u32[]{:S(2)}, u32[]{:S(2)}) collective-permute-start(bf16[320,256]{1,0:T(8,128)(2,1)S(1)} %collective-permute-done.4.refs_10_), channel_id=1, source_target_pairs={{0,16},{4,20},{8,24},{12,28},{16,0},{20,4},{24,8},{28,12},{1,17},{... | collective-permute-start | bytes 491528 | tf_op jit(solution)/shard_map/ppermute | solution.py:51
  90.5 14.7 %collective-permute-start.27 = (bf16[320,256]{1,0:T(8,128)(2,1)S(1)}, bf16[320,256]{1,0:T(8,128)(2,1)S(1)}, u32[]{:S(2)}, u32[]{:S(2)}) collective-permute-start(bf16[320,256]{1,0:T(8,128)(2,1)S(1)} %collective-permute-done.22.refs_12_), channel_id=1, source_target_pairs={{0,16},{4,20},{8,24},{12,28},{16,0},{20,4},{24,8},{28,12},{1,17},{... | collective-permute-start | bytes 491528 | tf_op jit(solution)/shard_map/ppermute | solution.py:51
  94.0 9.1 %collective-permute-start.15 = (bf16[256,384]{1,0:T(8,128)(2,1)S(1)}, bf16[256,384]{1,0:T(8,128)(2,1)S(1)}, u32[]{:S(2)}, u32[]{:S(2)}) collective-permute-start(bf16[256,384]{1,0:T(8,128)(2,1)S(1)} %get-tuple-element.68), channel_id=1, source_target_pairs={{0,8},{4,12},{8,0},{12,4},{16,24},{20,28},{24,16},{28,20},{1,9},{5... | collective-permute-start | bytes 589832 | tf_op jit(solution)/shard_map/ppermute | solution.py:51
  94.4 8.8 %collective-permute-start.16 = (bf16[256,384]{1,0:T(8,128)(2,1)S(1)}, bf16[256,384]{1,0:T(8,128)(2,1)S(1)}, u32[]{:S(2)}, u32[]{:S(2)}) collective-permute-start(bf16[256,384]{1,0:T(8,128)(2,1)S(1)} %get-tuple-element.69), channel_id=1, source_target_pairs={{0,12},{4,8},{8,4},{12,0},{16,28},{20,24},{24,20},{28,16},{1,13},{... | collective-permute-start | bytes 589832 | tf_op jit(solution)/shard_map/ppermute | solution.py:51
  94.4 10.8 %collective-permute-start.29 = (bf16[320,256]{1,0:T(8,128)(2,1)S(1)}, bf16[320,256]{1,0:T(8,128)(2,1)S(1)}, u32[]{:S(2)}, u32[]{:S(2)}) collective-permute-start(bf16[320,256]{1,0:T(8,128)(2,1)S(1)} %collective-permute-done.28.refs_14_), channel_id=1, source_target_pairs={{0,16},{4,20},{8,24},{12,28},{16,0},{20,4},{24,8},{28,12},{1,17},{... | collective-permute-start | bytes 491528 | tf_op jit(solution)/shard_map/ppermute | solution.py:51
  103.1 11.0 %collective-permute-start.23 = (bf16[256,256]{1,0:T(8,128)(2,1)S(1)}, bf16[256,256]{1,0:T(8,128)(2,1)S(1)}, u32[]{:S(2)}, u32[]{:S(2)}) collective-permute-start(bf16[256,256]{1,0:T(8,128)(2,1)S(1)} %get-tuple-element.83), channel_id=1, source_target_pairs={{0,4},{4,0},{8,12},{12,8},{16,20},{20,16},{24,28},{28,24},{1,5},{5... | collective-permute-start | bytes 393224 | tf_op jit(solution)/shard_map/ppermute | solution.py:51
  103.2 10.9 %collective-permute-start.24 = (bf16[256,256]{1,0:T(8,128)(2,1)S(1)}, bf16[256,256]{1,0:T(8,128)(2,1)S(1)}, u32[]{:S(2)}, u32[]{:S(2)}) collective-permute-start(bf16[256,256]{1,0:T(8,128)(2,1)S(1)} %get-tuple-element.84), channel_id=1, source_target_pairs={{0,8},{4,12},{8,0},{12,4},{16,24},{20,28},{24,16},{28,20},{1,9},{5... | collective-permute-start | bytes 393224 | tf_op jit(solution)/shard_map/ppermute | solution.py:51
  104.9 9.2 %collective-permute-start.25 = (bf16[256,256]{1,0:T(8,128)(2,1)S(1)}, bf16[256,256]{1,0:T(8,128)(2,1)S(1)}, u32[]{:S(2)}, u32[]{:S(2)}) collective-permute-start(bf16[256,256]{1,0:T(8,128)(2,1)S(1)} %get-tuple-element.85), channel_id=1, source_target_pairs={{0,12},{4,8},{8,4},{12,0},{16,28},{20,24},{24,20},{28,16},{1,13},{... | collective-permute-start | bytes 393224 | tf_op jit(solution)/shard_map/ppermute | solution.py:51
  112.4 6.3 %collective-permute-start.31 = (bf16[256,256]{1,0:T(8,128)(2,1)S(1)}, bf16[256,256]{1,0:T(8,128)(2,1)S(1)}, u32[]{:S(2)}, u32[]{:S(2)}) collective-permute-start(bf16[256,256]{1,0:T(8,128)(2,1)S(1)} %get-tuple-element.91), channel_id=1, source_target_pairs={{0,8},{4,12},{8,0},{12,4},{16,24},{20,28},{24,16},{28,20},{1,9},{5... | collective-permute-start | bytes 393224 | tf_op jit(solution)/shard_map/ppermute | solution.py:51
  114.1 6.1 %collective-permute-start.32 = (bf16[256,256]{1,0:T(8,128)(2,1)S(1)}, bf16[256,256]{1,0:T(8,128)(2,1)S(1)}, u32[]{:S(2)}, u32[]{:S(2)}) collective-permute-start(bf16[256,256]{1,0:T(8,128)(2,1)S(1)} %get-tuple-element.92), channel_id=1, source_target_pairs={{0,12},{4,8},{8,4},{12,0},{16,28},{20,24},{24,20},{28,16},{1,13},{... | collective-permute-start | bytes 393224 | tf_op jit(solution)/shard_map/ppermute | solution.py:51
  (27 other events, 196.7 us)

commit v4 on v0

v4 whole, which is shorter than its diff:
```python
import functools

import jax
import jax.numpy as jnp
import numpy as np
from jax import lax
from jax.experimental import pallas as pl
from jax.experimental.pallas import tpu as pltpu
from jax.sharding import PartitionSpec as P

HD = 128
GROUP = 5
QBLK = 128
SEL = 4
TEAM = 4
FARS = (0, 2, 4, 6)

norm_eps = 1e-06
rope_base = 10000000.0

TILES = 2 + GROUP
WIDTH = TILES * HD
MIB = 1024 * 1024

SMEM = pl.BlockSpec(memory_space=pltpu.SMEM)
VMEM = pl.BlockSpec(memory_space=pltpu.VMEM)
ANY = pl.BlockSpec(memory_space=pl.ANY)
NOTE_ROWS = 16


def angle_tables(head_dim):
    half_dim = head_dim // 2
    frequency = rope_base ** (-2.0 * np.arange(half_dim) / head_dim)
    return np.stack(
        [np.mod(frequency * 32.0**digit_level, 2.0 * np.pi) for digit_level in range(4)]
    )


def rope_table(positions):
    tables = jnp.asarray(np.tile(angle_tables(HD), (1, 2)), jnp.float32)
    quarter = jnp.where(jnp.arange(HD) < HD // 2, 0.0, -np.pi / 2).astype(jnp.float32)
    angles = jnp.broadcast_to(quarter[None, :], (positions.shape[0], HD))
    remaining = positions
    for digit_level in range(4):
        digit_value = (remaining % 32).astype(jnp.float32)
        angles = angles + digit_value[:, None] * tables[digit_level][None, :]
        remaining = remaining // 32
    return jnp.cos(angles)


def swap(value, axis, bit):
    size = lax.axis_size(axis)
    return lax.ppermute(value, axis, [(i, i ^ bit) for i in range(size)])


def bits_of(size, low):
    bits = []
    bit = low
    while bit < size:
        bits.append(bit)
        bit *= 2
    return bits[::-1]


def tile_sources(group):
    return (group * HD, 1, 0), (group * HD, 1, 1), (group * GROUP * HD, GROUP, 2)


def start_all(copies, sem):
    copies = [
        pltpu.make_async_copy(source, target, sem.at[index])
        for index, (source, target) in enumerate(copies)
    ]
    for copy in copies:
        copy.start()
    return copies


def cut_kernel(place_ref, wk_ref, wv_ref, wq_ref, out_ref, sem):
    part = pl.ds(pl.multiple_of(place_ref[1], 16), out_ref.shape[0])
    copies = []
    for ref, (column, tiles, at) in zip((wk_ref, wv_ref, wq_ref), tile_sources(place_ref[0])):
        column = pl.ds(pl.multiple_of(column, HD), tiles * HD)
        copies.append((ref.at[part, column], out_ref.at[:, pl.ds(at * HD, tiles * HD)]))
    for copy in start_all(copies, sem):
        copy.wait()


def cut(place, piece_rows, weights, limit):
    return pl.pallas_call(
        cut_kernel,
        out_shape=jax.ShapeDtypeStruct((piece_rows, WIDTH), jnp.bfloat16),
        in_specs=[SMEM] + [ANY] * 3,
        out_specs=VMEM,
        scratch_shapes=[pltpu.SemaphoreType.DMA((3,))],
        compiler_params=pltpu.CompilerParams(vmem_limit_bytes=limit * MIB),
        name="cut",
    )(place, *weights)


def normed_rows(tokens, gain):
    widened = tokens.astype(jnp.float32)
    return (
        widened
        * lax.rsqrt(jnp.mean(widened * widened, axis=-1, keepdims=True) + norm_eps)
        * gain.astype(jnp.float32)
    ).astype(jnp.bfloat16)


def pack_kernel(team_count, *refs):
    lists_ref, ck_ref, cv_ref, payload_ref = refs
    prefix = ck_ref.shape[0]
    for target in range(team_count):
        column = pl.ds(target // 2 % TEAM * HD, HD)
        payload_ref[target, pl.ds(0, prefix), pl.ds(0, HD)] = ck_ref[:, column]
        payload_ref[target, pl.ds(0, prefix), pl.ds(HD, HD)] = cv_ref[:, column]
        payload_ref[target, pl.ds(prefix, NOTE_ROWS), :] = lists_ref[...]


def pack(team_count, lists, caches):
    prefix = caches[0].shape[0]
    note = jnp.pad(lists.astype(jnp.bfloat16)[None, :], ((0, NOTE_ROWS - 1), (0, 2 * HD - lists.shape[0])))
    return pl.pallas_call(
        functools.partial(pack_kernel, team_count),
        out_shape=jax.ShapeDtypeStruct(
            (team_count, prefix + NOTE_ROWS, 2 * HD), jnp.bfloat16
        ),
        in_specs=[VMEM] * 3,
        out_specs=VMEM,
        compiler_params=pltpu.CompilerParams(vmem_limit_bytes=14 * MIB),
        name="pack",
    )(note, *caches)


def turned(value, cosine, sine):
    return value * cosine + pltpu.roll(value, HD // 2, 1) * sine


def heads_kernel(far, x_count, piece_count, *refs):
    refs = list(refs)

    def take(count):
        taken = refs[:count]
        del refs[:count]
        return taken

    place_ref, lists_ref = take(2)
    x_refs = take(x_count)
    gain_ref, bias_ref, table_ref, cache_ref = take(4)
    if piece_count:
        piece_refs = take(piece_count)
        out_ref, w_ref, cache_value_t_ref = take(3)
    else:
        w_ref, cache_value_t_ref, out_ref = take(3)
    q_buf, key_buf, value_t_buf, sem = take(4)

    rows = sum(x_ref.shape[0] for x_ref in x_refs)
    group = place_ref[0]
    copies = []
    if piece_count:
        for index, piece in enumerate(piece_refs):
            start = pl.multiple_of(place_ref[2 + index], 16)
            copies.append((piece, w_ref.at[pl.ds(start, piece.shape[0]), :]))
        copies = start_all(copies, sem)
    blocks_each = (cache_ref.shape[1] - NOTE_ROWS) // QBLK

    def cached(place):
        if blocks_each == 1:
            return place, pl.ds(0, QBLK)
        return place // blocks_each, pl.ds(pl.multiple_of(place % blocks_each * QBLK, QBLK), QBLK)

    if piece_count:
        for place in range(blocks_each * cache_ref.shape[0]):
            owner, part = cached(place)
            cache_value_t_ref[place] = cache_ref[owner, part, pl.ds(HD, HD)].T
    x = [normed_rows(x_ref[...], gain_ref[...]) for x_ref in x_refs]
    x = jnp.concatenate(x, axis=0) if x_count > 1 else x[0]
    for copy in copies:
        copy.wait()

    factor = HD ** (-0.5) * float(np.log2(np.e))
    causal = lax.broadcasted_iota(jnp.int32, (QBLK, QBLK), 0) <= lax.broadcasted_iota(
        jnp.int32, (QBLK, QBLK), 1
    )
    contract_last = (((1,), (1,)), ((), ()))
    blocks = rows // QBLK

    lin = jnp.dot(x, w_ref[...], preferred_element_type=jnp.float32) + bias_ref[...]
    low_half = lax.broadcasted_iota(jnp.int32, (rows, HD), 1) < HD // 2
    table = table_ref[...]
    swapped = pltpu.roll(table, HD // 2, 1)
    cosine = jnp.where(low_half, table, swapped)
    sine = jnp.where(low_half, -swapped, table)
    for tile in range(TILES):
        value = lin[:, tile * HD : (tile + 1) * HD]
        if tile != 1:
            value = turned(value, cosine, sine)
        if tile >= 2:
            q_buf[:, pl.ds((tile - 2) * HD, HD)] = value.astype(jnp.bfloat16)
            continue
        out_ref[:, pl.ds(tile * HD, HD)] = value.astype(out_ref.dtype)
        if tile == 0:
            key_buf[...] = value.astype(jnp.bfloat16)
        else:
            value_t_buf[...] = value.astype(jnp.bfloat16).T

    owner_list = place_ref[place_ref.shape[0] - 1] ^ far
    for block in range(blocks):
        span = pl.ds(block * QBLK, QBLK)
        for head in range(GROUP):
            query = q_buf[span, pl.ds(head * HD, HD)]
            at = ((group * GROUP + head) * blocks + block) * SEL
            slots = [lists_ref[owner_list, at + j] for j in range(SEL)]
            keys = [key_buf[span, :]]
            values = [value_t_buf[:, span]]
            for slot in slots:
                place = jnp.maximum(slot, 0)
                owner, part = cached(place)
                keys.append(cache_ref[owner, part, pl.ds(0, HD)])
                values.append(cache_value_t_ref[place])
            scores = lax.dot_general(
                jnp.concatenate(keys, axis=0),
                query,
                contract_last,
                preferred_element_type=jnp.float32,
            )
            parts = [jnp.where(causal, scores[:QBLK], -jnp.inf)]
            for j in range(SEL):
                part = scores[(j + 1) * QBLK : (j + 2) * QBLK]
                parts.append(part + jnp.where(slots[j] >= 0, 0.0, -jnp.inf))
            top = functools.reduce(jnp.maximum, parts)
            top = jnp.max(top, axis=0, keepdims=True) * factor
            parts = [jnp.exp2(part * factor - top) for part in parts]
            total = jnp.sum(functools.reduce(jnp.add, parts), axis=0, keepdims=True)
            weights = jnp.concatenate([part.astype(jnp.bfloat16) for part in parts], axis=0)
            mixed = jnp.dot(
                jnp.concatenate(values, axis=1), weights, preferred_element_type=jnp.float32
            )
            out_ref[span, pl.ds((2 + head) * HD, HD)] = (mixed / total).T.astype(out_ref.dtype)


def heads(far, place, lists, x_parts, gain, bias, table, cache, pieces, kept):
    depth = x_parts[0].shape[1]
    rows = sum(part.shape[0] for part in x_parts)
    operands = [place, lists, *x_parts, gain, bias, table, cache]
    specs = [SMEM] * 2 + [VMEM] * (len(x_parts) + 4)
    shapes = [jax.ShapeDtypeStruct((rows, WIDTH), jnp.bfloat16 if far else jnp.float32)]
    if pieces:
        operands += pieces
        specs += [ANY] * len(pieces)
        total_blocks = cache.shape[0] * (cache.shape[1] - NOTE_ROWS) // QBLK
        shapes.append(jax.ShapeDtypeStruct((depth, WIDTH), jnp.bfloat16))
        shapes.append(jax.ShapeDtypeStruct((total_blocks, HD, QBLK), jnp.bfloat16))
    else:
        operands += kept
        specs += [VMEM] * 2
    return pl.pallas_call(
        functools.partial(heads_kernel, far, len(x_parts), len(pieces)),
        out_shape=shapes,
        in_specs=specs,
        out_specs=[VMEM] * len(shapes),
        scratch_shapes=[
            pltpu.VMEM((rows, GROUP * HD), jnp.bfloat16),
            pltpu.VMEM((rows, HD), jnp.bfloat16),
            pltpu.VMEM((HD, rows), jnp.bfloat16),
            pltpu.SemaphoreType.DMA((max(len(pieces), 1),)),
        ],
        compiler_params=pltpu.CompilerParams(vmem_limit_bytes=16 * MIB),
        cost_estimate=pl.CostEstimate(
            flops=2 * rows * depth * WIDTH,
            bytes_accessed=2 * depth * (rows + WIDTH),
            transcendentals=rows * GROUP * (SEL + 1) * QBLK,
        ),
        name="heads",
    )(*operands)


def finish_kernel(place_ref, *refs):
    context_ref, keys_ref, values_ref = refs[len(FARS) :]
    for far, part in zip(FARS, refs):
        sources = tile_sources(place_ref[0] ^ (far // 2))
        for target, (column, tiles, at) in zip((keys_ref, values_ref, context_ref), sources):
            target[:, pl.ds(pl.multiple_of(column, HD), tiles * HD)] = part[
                :, pl.ds(at * HD, tiles * HD)
            ].astype(jnp.float32)


def finish(place, parts):
    rows = parts[0].shape[0]
    return pl.pallas_call(
        finish_kernel,
        out_shape=[
            jax.ShapeDtypeStruct((rows, TEAM * GROUP * HD), jnp.float32),
            jax.ShapeDtypeStruct((rows, TEAM * HD), jnp.float32),
            jax.ShapeDtypeStruct((rows, TEAM * HD), jnp.float32),
        ],
        in_specs=[SMEM] + [VMEM] * len(parts),
        out_specs=[VMEM] * 3,
        compiler_params=pltpu.CompilerParams(vmem_limit_bytes=16 * MIB),
        name="finish",
    )(place, *parts)


tie = lax.optimization_barrier


def on_device(
    tokens,
    norm_gain,
    w_query,
    w_key,
    w_value,
    b_query,
    b_key,
    b_value,
    cache_keys,
    cache_values,
    block_lists,
    start_position,
):
    rows = tokens.shape[0]
    shard = w_query.shape[0]
    ctx_size, grp_size = lax.axis_size("ctx"), lax.axis_size("grp")
    me, layer = lax.axis_index("ctx"), lax.axis_index("grp")
    group = me // 2 % TEAM
    core = me % 2
    piece_rows = shard // 2

    tokens_2 = swap(tokens, "ctx", 2)
    tokens_4 = swap(tokens, "ctx", 4)

    grp_order = [0]
    for bit in bits_of(grp_size, 1):
        grp_order += [far ^ bit for far in grp_order]
    piece_places = [(far, over) for far in sorted(grp_order) if far for over in (0, 1)]
    place = jnp.stack(
        [group, core * piece_rows, layer * shard]
        + [(layer ^ far) * shard + (core ^ over) * piece_rows for far, over in piece_places]
        + [me]
    ).astype(jnp.int32)
    weights = (w_key, w_value, w_query)
    half = cut(jnp.stack([group, core * piece_rows]).astype(jnp.int32), piece_rows, weights, 60)

    payload = pack(ctx_size, block_lists.reshape(-1), (cache_keys, cache_values))
    cache = lax.all_to_all(payload, "ctx", 0, 0)
    row_ids = jnp.arange(rows, dtype=jnp.int32)
    tables = [
        rope_table(start_position[0] + ((me ^ far) * grp_size + layer) * rows + row_ids)
        for far in FARS
    ]
    bias = jnp.concatenate(
        [
            lax.dynamic_slice_in_dim(b_key, group * HD, HD),
            lax.dynamic_slice_in_dim(b_value, group * HD, HD),
            lax.dynamic_slice_in_dim(b_query, group * GROUP * HD, GROUP * HD),
        ]
    ).astype(jnp.float32)[None, :]

    held = {0: half}
    for index, bit in enumerate(bits_of(grp_size, 1)):
        for far in sorted(held):
            held[far ^ bit] = swap(held[far], "grp", bit)
        if index == 0:
            held[bit], tables, bias = tie((held[bit], tables, bias))
    whole = cut(jnp.stack([group, 0]).astype(jnp.int32), shard, weights, 14)
    pieces = [whole]
    for far, over in piece_places:
        pieces.append(swap(held[far], "ctx", 1) if over else held[far])

    half_rows = rows // 2
    tokens_6 = [
        swap(tokens_2[:half_rows], "ctx", 4),
        swap(tokens_4[half_rows:], "ctx", 2),
    ]

    lists = cache[:, cache_keys.shape[0], :].astype(jnp.int32)

    x_parts = {0: [tokens], 2: [tokens_2], 4: [tokens_4], 6: tokens_6}
    kept, parts = None, {}
    for far in (2, 4, 6, 0):
        out, *rest = heads(
            far,
            place,
            lists,
            x_parts[far],
            norm_gain[None, :],
            bias,
            tables[FARS.index(far)],
            cache,
            [] if kept else pieces,
            kept,
        )
        kept = kept or rest
        parts[far] = swap(out, "ctx", far) if far else out
    return tuple(finish(place, [parts[far] for far in FARS]))


def solution(mesh):
    in_specs = (
        P(("ctx", "grp"), None),
        P(),
        P("grp", None),
        P("grp", None),
        P("grp", None),
        P(),
        P(),
        P(),
        P("ctx", None),
        P("ctx", None),
        P(None, ("ctx", "grp"), None),
        P(),
    )
    out_specs = (P(("ctx", "grp"), None), P(("ctx", "grp"), None), P(("ctx", "grp"), None))
    return jax.shard_map(
        on_device, mesh=mesh, in_specs=in_specs, out_specs=out_specs, check_vma=False
    )
```

time: 458 us -> 97.1 us (0.21)
  waiting for transfers between devices: 359 us -> 33 us
  matrix products: 45.9 us -> 0 us
  Pallas kernels: 0 us -> 28.1 us
  starting transfers between devices: 0.19 us -> 20.1 us
  local copies, waits for them, and re-layouts: 25 us -> 9.1 us
  between operations: 14.8 us -> 1.65 us
  other arithmetic: 11.8 us -> 4.46 us
    all_gather x5 -> x0, waiting for transfers between devices: 357 us -> none  [the longest x1 224 us: on_device(): lax.all_gather(w_query, 'grp', axis=0, tiled=True)]
    dot_general x21 -> x0, matrix products: 45.9 us -> none  [the longest x8 15.3 us: one_key_block(): jnp.einsum('rkgd,pkd->kgrp', query_heads, block_keys) * score_scale]
    ppermute x0 -> x13, waiting for transfers between devices: none -> 33 us  [swap(): return lax.ppermute(value, axis, [(i, i ^ bit) for i in range(size)])]
    pallas_call x0 -> x8, Pallas kernels: none -> 28.1 us  [the longest x4 21.2 us: heads(): pl.pallas_call(functools.partial(heads_kernel, far, len(x_parts), len(pie...]
    ppermute x0 -> x13, starting transfers between devices: none -> 16.4 us  [swap(): return lax.ppermute(value, axis, [(i, i ^ bit) for i in range(size)])]
    reduce_sum x10 -> x0, other arithmetic: 7.52 us -> none  [the longest x8 4.87 us: one_key_block(): new_total = old_total * factor + jnp.sum(weights, axis=-1)]
    dynamic_slice x8 -> x1, local copies, waits for them, and re-layouts: 7.96 us -> 0.77 us  [on_device(): lax.dynamic_slice_in_dim(b_query, group * GROUP * HD, GROUP * HD)]
    while x10 -> x0, local copies, waits for them, and re-layouts: 4.58 us -> none  [the longest x2 4.55 us: on_device(): lax.fori_loop(0, key_count // QBLK, one_key_block, initial_state)]
  transfers between devices with their start and end apart: 5 -> 14, of which waited for: 5 -> 3; matrix products, arithmetic and copies ran while one was open for 6% -> 8% of each run, Pallas kernels for 0% -> 24%
where the time goes in v4:
time: 97.1 us; the launch traced here: 96.5 us
  waiting for transfers between devices  33 us (34%)
  Pallas kernels  28.1 us (29%)
  starting transfers between devices  20.1 us (21%)
  local copies, waits for them, and re-layouts  9.1 us (9%)
  other arithmetic  4.46 us (5%)
  between operations  1.65 us (2%)
    ppermute x13, waiting for transfers between devices, swap(): return lax.ppermute(value, axis, [(i, i ^ bit) for i in range(size)])  33 us
    pallas_call x4, Pallas kernels, heads(): pl.pallas_call(functools.partial(heads_kernel, far, len(x_parts), len(pie...  21.2 us
    ppermute x13, starting transfers between devices, swap(): return lax.ppermute(value, axis, [(i, i ^ bit) for i in range(size)])  16.4 us
    unnamed x29, local copies, waits for them, and re-layouts  5.05 us
    all_to_all x1, starting transfers between devices, on_device(): cache = lax.all_to_all(payload, 'ctx', 0, 0)  3.73 us
    cos x2, other arithmetic, rope_table(): return jnp.cos(angles)  3.56 us
    pallas_call x2, Pallas kernels, cut(): pl.pallas_call(cut_kernel, out_shape=jax.ShapeDtypeStruct((piece_rows, WI...  3.44 us
    pallas_call x1, Pallas kernels, finish(): pl.pallas_call(finish_kernel, out_shape=[jax.ShapeDtypeStruct((rows, TEAM...  2.63 us
  transfers between devices with their start and end apart: 14, of which 3 were waited for; matrix products, arithmetic and copies ran while one was open for 8% of the time, Pallas kernels for 24%

profile of v4, /device:TPU:0, one launch (start us, length us, event | category | flops | bytes accessed | tf_op | source)
XLA Modules:
  0.0 96.5 jit_solution(3304221086963354482)
XLA Ops:
  0.7 0.6 pad_add_fusion.place_ref
  1.3 2.7 %cut.2 = bf16[320,896]{1,0:T(8,128)(2,1)} custom-call(s32[2]{0:T(128)} %pad_add_fusion.place_ref, bf16[640,512]{1,0:T(8,128)(2,1)} %wk_ref.3, bf16[640,512]{1,0:T(8,128)(2,1)} %wv_ref.3, bf16[640,2560]{1,0:T(8,128)(2,1)} %wq_ref.3), custom_call_target="tpu_custom_call" | custom-call | tf_op jit(solution)/shard_map/cut/pallas_call | solution.py:90
  4.1 3.1 %collective-permute-start.2 = (bf16[320,896]{1,0:T(8,128)(2,1)}, bf16[320,896]{1,0:T(8,128)(2,1)}, u32[]{:S(2)}, u32[]{:S(2)}) collective-permute-start(bf16[320,896]{1,0:T(8,128)(2,1)} %cut.2), channel_id=1, source_target_pairs={{0,1},{1,0},{2,3},{3,2},{4,5},{5,4},{6,7},{7,6},{8,9},{9,8},{10,11... | collective-permute-start | bytes 1720328 | tf_op jit(solution)/shard_map/ppermute | solution.py:53
  7.2 2.6 %collective-permute-start = (bf16[320,896]{1,0:T(8,128)(2,1)}, bf16[320,896]{1,0:T(8,128)(2,1)}, u32[]{:S(2)}, u32[]{:S(2)}) collective-permute-start(bf16[320,896]{1,0:T(8,128)(2,1)} %cut.2), channel_id=1, source_target_pairs={{0,2},{1,3},{2,0},{3,1},{4,6},{5,7},{6,4},{7,5},{8,10},{9,11},{10,... | collective-permute-start | bytes 1720328 | tf_op jit(solution)/shard_map/ppermute | solution.py:53
  9.7 1.5 %collective-permute-start.1 = (bf16[256,2560]{1,0:T(8,128)(2,1)}, bf16[256,2560]{1,0:T(8,128)(2,1)S(1)}, u32[]{:S(2)}, u32[]{:S(2)}) collective-permute-start(bf16[256,2560]{1,0:T(8,128)(2,1)} %refs_2_.3), channel_id=1, source_target_pairs={{0,8},{4,12},{8,0},{12,4},{16,24},{20,28},{24,16},{28,20},{1,9},{5... | collective-permute-start | bytes 3932168 | tf_op jit(solution)/shard_map/ppermute | solution.py:53
  11.2 1.5 %collective-permute-start.8 = (bf16[256,2560]{1,0:T(8,128)(2,1)}, bf16[256,2560]{1,0:T(8,128)(2,1)}, u32[]{:S(2)}, u32[]{:S(2)}) collective-permute-start(bf16[256,2560]{1,0:T(8,128)(2,1)} %refs_2_.3), channel_id=1, source_target_pairs={{0,16},{4,20},{8,24},{12,28},{16,0},{20,4},{24,8},{28,12},{1,17},{... | collective-permute-start | bytes 3932168 | tf_op jit(solution)/shard_map/ppermute | solution.py:53
  13.6 0.8 dynamic_slice.11
  14.6 0.5 add_cosine_fusion.3.refs_5_
  15.2 3.0 %add_cosine_fusion = (f32[256,128]{1,0:T(8,128)S(1)}, f32[256,128]{1,0:T(8,128)}, f32[256,128]{1,0:T(8,128)S(1)}) fusion(f32[256]{0:T(256)S(1)} %get-tuple-element.31, f32[256]{0:T(256)S(1)} %get-tuple-element.30, f32[256]{0:T(256)S(1)} %get-tuple-element.29, f32[256]{0:T(256)S(1)} %get-tuple-element.28, f32[128]{0:T(128)S(1)} %copy-done.8, ...), kind=kLoop, calls=%fused_computation | loop fusion | flops 786432 | bytes 408064 | tf_op jit(solution)/shard_map/cos | solution.py:48
  18.2 17.0 %collective-permute-done.refs_10_ = bf16[320,896]{1,0:T(8,128)(2,1)} collective-permute-done((bf16[320,896]{1,0:T(8,128)(2,1)}, bf16[320,896]{1,0:T(8,128)(2,1)}, u32[]{:S(2)}, u32[]{:S(2)}) %collective-permute-start) | collective-permute-done | bytes 573472 | tf_op jit(solution)/shard_map/ppermute | solution.py:53
  35.9 0.9 pack.1
  36.8 3.7 %all-to-all-start = ((bf16[8,144,256]{2,1,0:T(8,128)(2,1)}), bf16[8,144,256]{2,1,0:T(8,128)(2,1)S(1)}, u32[]{:S(2)}, u32[]{:S(2)}) async-start(bf16[8,144,256]{2,1,0:T(8,128)(2,1)} %pack.1), calls=%async_computation | async-start | bytes 1179648 | tf_op jit(solution)/shard_map/all_to_all | solution.py:345
  40.5 0.5 collective-permute-start.4
  41.1 6.9 %collective-permute-done.5.refs_12_ = bf16[320,896]{1,0:T(8,128)(2,1)} collective-permute-done((bf16[320,896]{1,0:T(8,128)(2,1)}, bf16[320,896]{1,0:T(8,128)(2,1)}, u32[]{:S(2)}, u32[]{:S(2)}) %collective-permute-start.5) | collective-permute-done | bytes 573472 | tf_op jit(solution)/shard_map/ppermute | solution.py:53
  48.0 0.9 slice.77
  48.8 1.5 %collective-permute-start.10 = (bf16[128,2560]{1,0:T(8,128)(2,1)}, bf16[128,2560]{1,0:T(8,128)(2,1)}, u32[]{:S(2)}, u32[]{:S(2)}) collective-permute-start(bf16[128,2560]{1,0:T(8,128)(2,1)} %slice.77), channel_id=1, source_target_pairs={{0,16},{4,20},{8,24},{12,28},{16,0},{20,4},{24,8},{28,12},{1,17},{... | collective-permute-start | bytes 1966088 | tf_op jit(solution)/shard_map/ppermute | solution.py:53
  50.4 2.0 %slice.78 = bf16[128,2560]{1,0:T(8,128)(2,1)} slice(bf16[256,2560]{1,0:T(8,128)(2,1)} %collective-permute-done.8.refs_2_), slice={[128:256], [0:2560]} | slice | bytes 1310720 | tf_op jit(solution)/shard_map/slice | solution.py:373
  52.3 1.5 %collective-permute-start.11 = (bf16[128,2560]{1,0:T(8,128)(2,1)}, bf16[128,2560]{1,0:T(8,128)(2,1)}, u32[]{:S(2)}, u32[]{:S(2)}) collective-permute-start(bf16[128,2560]{1,0:T(8,128)(2,1)} %slice.78), channel_id=1, source_target_pairs={{0,8},{4,12},{8,0},{12,4},{16,24},{20,28},{24,16},{28,20},{1,9},{5... | collective-permute-start | bytes 1966088 | tf_op jit(solution)/shard_map/ppermute | solution.py:53
  53.9 1.9 %copy-done = bf16[640,2560]{1,0:T(8,128)(2,1)S(1)} copy-done((bf16[640,2560]{1,0:T(8,128)(2,1)S(1)}, bf16[640,2560]{1,0:T(8,128)(2,1)}, u32[]{:S(2)}) %copy-start) | copy-done | bytes 3276824
  55.8 1.1 %copy-done.1 = bf16[640,512]{1,0:T(8,128)(2,1)S(1)} copy-done((bf16[640,512]{1,0:T(8,128)(2,1)S(1)}, bf16[640,512]{1,0:T(8,128)(2,1)}, u32[]{:S(2)}) %copy-start.1) | copy-done | bytes 655384
  56.9 1.1 %copy-done.2 = bf16[640,512]{1,0:T(8,128)(2,1)S(1)} copy-done((bf16[640,512]{1,0:T(8,128)(2,1)S(1)}, bf16[640,512]{1,0:T(8,128)(2,1)}, u32[]{:S(2)}) %copy-start.2) | copy-done | bytes 655384
  58.0 0.7 cut.3.refs_7_
  58.9 0.9 copy-done.3
  59.8 6.5 %heads.4 = (bf16[256,896]{1,0:T(8,128)(2,1)S(1)}, bf16[2560,896]{1,0:T(8,128)(2,1)S(1)}, bf16[8,128,128]{2,1,0:T(8,128)(2,1)S(1)}) custom-call(s32[10]{0:T(128)S(1)} %stack.52.refs_0_.place_ref, s32[8,256]{1,0:T(8,128)S(1)} %bitcast.22, bf16[256,2560]{1,0:T(8,128)(2,1)S(1)} %collective-permute-done.1.refs_2_, ...), custom_call_target="tpu_custom_call" | custom-call | flops 1174405120 | bytes 5898240 | tf_op jit(solution)/shard_map/heads/pallas_call | solution.py:257
  66.3 0.6 collective-permute-start.7
  66.9 4.9 %heads.6 = bf16[256,896]{1,0:T(8,128)(2,1)S(1)} custom-call(s32[10]{0:T(128)S(1)} %stack.52.refs_0_.place_ref, s32[8,256]{1,0:T(8,128)S(1)} %bitcast.23, bf16[256,2560]{1,0:T(8,128)(2,1)} %collective-permute-done.8.refs_2_, bf16[1,2560]{1,0:T(2,128)(2,1)S(1)} %broadcast_in_dim.24.refs_3_.refs_4_, f32[1,896]{1,0:T(1,128)S(1)} %maximum_convert_fusion.refs_4_.refs_5_, ...), custom_call_target="tpu_custom_call" | custom-call | flops 1174405120 | bytes 5898240 | tf_op jit(solution)/shard_map/heads/pallas_call | solution.py:257
  71.9 0.6 collective-permute-start.9
  72.4 4.9 %heads.7 = bf16[256,896]{1,0:T(8,128)(2,1)S(1)} custom-call(s32[10]{0:T(128)S(1)} %stack.52.refs_0_.place_ref, s32[8,256]{1,0:T(8,128)S(1)} %bitcast.24, bf16[128,2560]{1,0:T(8,128)(2,1)} %collective-permute-done.10.refs_2_, bf16[128,2560]{1,0:T(8,128)(2,1)} %collective-permute-done.11.refs_3_, bf16[1,2560]{1,0:T(2,128)(2,1)S(1)} %broadcast_in_dim.24.refs_3_.refs_4_, ...), custom_call_target="tpu_custom_call" | custom-call | flops 1174405120 | bytes 5898240 | tf_op jit(solution)/shard_map/heads/pallas_call | solution.py:257
  77.3 2.5 %collective-permute-start.12 = (bf16[256,896]{1,0:T(8,128)(2,1)S(1)}, bf16[256,896]{1,0:T(8,128)(2,1)S(1)}, u32[]{:S(2)}, u32[]{:S(2)}) collective-permute-start(bf16[256,896]{1,0:T(8,128)(2,1)S(1)} %heads.7), channel_id=1, source_target_pairs={{0,24},{4,28},{8,16},{12,20},{16,8},{20,12},{24,0},{28,4},{1,25},{... | collective-permute-start | bytes 1376264 | tf_op jit(solution)/shard_map/ppermute | solution.py:53
  79.8 4.9 %heads.5.refs_0_ = f32[256,896]{1,0:T(8,128)S(1)} custom-call(s32[10]{0:T(128)S(1)} %stack.52.refs_0_.place_ref, s32[8,256]{1,0:T(8,128)S(1)} %bitcast.25, bf16[256,2560]{1,0:T(8,128)(2,1)} %refs_2_.3, bf16[1,2560]{1,0:T(2,128)(2,1)S(1)} %broadcast_in_dim.24.refs_3_.refs_4_, f32[1,896]{1,0:T(1,128)S(1)} %maximum_convert_fusion.refs_4_.refs_5_, ...), custom_call_target="tpu_custom_call" | custom-call | flops 1174405120 | bytes 5898240 | tf_op jit(solution)/shard_map/heads/pallas_call | solution.py:257
  84.7 9.1 %collective-permute-done.9.refs_2_ = bf16[256,896]{1,0:T(8,128)(2,1)S(1)} collective-permute-done((bf16[256,896]{1,0:T(8,128)(2,1)S(1)}, bf16[256,896]{1,0:T(8,128)(2,1)S(1)}, u32[]{:S(2)}, u32[]{:S(2)}) %collective-permute-start.9) | collective-permute-done | bytes 458784 | tf_op jit(solution)/shard_map/ppermute | solution.py:53
  93.8 2.6 %finish.1 = (f32[256,2560]{1,0:T(8,128)}, f32[256,512]{1,0:T(8,128)}, f32[256,512]{1,0:T(8,128)}) custom-call(s32[10]{0:T(128)S(1)} %stack.52.refs_0_.place_ref, f32[256,896]{1,0:T(8,128)S(1)} %heads.5.refs_0_, bf16[256,896]{1,0:T(8,128)(2,1)S(1)} %collective-permute-done.7.refs_1_, bf16[256,896]{1,0:T(8,128)(2,1)S(1)} %collective-permute-done.9.refs_2_, ...), custom_call_target="tpu_custom_call" | custom-call | tf_op jit(solution)/shard_map/finish/pallas_call | solution.py:290
  (59 shorter events, 1.3 us)
Async XLA Ops:
  1.3 13.2 %copy-start.12 = (bf16[512]{0:T(512)(128)(2,1)S(1)}, bf16[512]{0:T(512)(128)(2,1)}, u32[]{:S(2)}) copy-start(bf16[512]{0:T(512)(128)(2,1)} %param.23) | copy-start | bytes 3076
  1.3 13.2 %copy-start.13 = (bf16[512]{0:T(512)(128)(2,1)S(1)}, bf16[512]{0:T(512)(128)(2,1)}, u32[]{:S(2)}) copy-start(bf16[512]{0:T(512)(128)(2,1)} %param.22) | copy-start | bytes 3076
  1.3 13.3 %copy-start.8 = (f32[128]{0:T(128)S(1)}, f32[128]{0:T(128)}, u32[]{:S(2)}) copy-start(f32[128]{0:T(128)} %constant.262) | copy-start | bytes 1540
  1.3 13.3 %copy-start.9 = (f32[128]{0:T(128)S(1)}, f32[128]{0:T(128)}, u32[]{:S(2)}) copy-start(f32[128]{0:T(128)} %constant.260) | copy-start | bytes 1540
  1.3 13.3 %copy-start.10 = (f32[128]{0:T(128)S(1)}, f32[128]{0:T(128)}, u32[]{:S(2)}) copy-start(f32[128]{0:T(128)} %constant.258) | copy-start | bytes 1540
  1.3 13.3 %copy-start.11 = (f32[128]{0:T(128)S(1)}, f32[128]{0:T(128)}, u32[]{:S(2)}) copy-start(f32[128]{0:T(128)} %constant.256) | copy-start | bytes 1540
  1.3 34.3 %copy-start.7 = (s32[20,2,4]{0,2,1:T(4,128)S(1)}, s32[20,2,4]{0,2,1:T(4,128)}, u32[]{:S(2)}) copy-start(s32[20,2,4]{0,2,1:T(4,128)} %param.26) | copy-start | bytes 1924
  1.3 34.5 %copy-start.4 = (bf16[128,512]{1,0:T(8,128)(2,1)S(1)}, bf16[128,512]{1,0:T(8,128)(2,1)}, u32[]{:S(2)}) copy-start(bf16[128,512]{1,0:T(8,128)(2,1)} %refs_1_.1) | copy-start | bytes 393220
  1.3 34.5 %copy-start.5 = (bf16[128,512]{1,0:T(8,128)(2,1)S(1)}, bf16[128,512]{1,0:T(8,128)(2,1)}, u32[]{:S(2)}) copy-start(bf16[128,512]{1,0:T(8,128)(2,1)} %refs_2_.2) | copy-start | bytes 393220
  4.1 36.9 %collective-permute-start.2 = (bf16[320,896]{1,0:T(8,128)(2,1)}, bf16[320,896]{1,0:T(8,128)(2,1)}, u32[]{:S(2)}, u32[]{:S(2)}) collective-permute-start(bf16[320,896]{1,0:T(8,128)(2,1)} %cut.2), channel_id=1, source_target_pairs={{0,1},{1,0},{2,3},{3,2},{4,5},{5,4},{6,7},{7,6},{8,9},{9,8},{10,11... | collective-permute-start | bytes 1720328 | tf_op jit(solution)/shard_map/ppermute | solution.py:53
  7.2 28.0 %collective-permute-start = (bf16[320,896]{1,0:T(8,128)(2,1)}, bf16[320,896]{1,0:T(8,128)(2,1)}, u32[]{:S(2)}, u32[]{:S(2)}) collective-permute-start(bf16[320,896]{1,0:T(8,128)(2,1)} %cut.2), channel_id=1, source_target_pairs={{0,2},{1,3},{2,0},{3,1},{4,6},{5,7},{6,4},{7,5},{8,10},{9,11},{10,... | collective-permute-start | bytes 1720328 | tf_op jit(solution)/shard_map/ppermute | solution.py:53
  9.7 38.2 %collective-permute-start.1 = (bf16[256,2560]{1,0:T(8,128)(2,1)}, bf16[256,2560]{1,0:T(8,128)(2,1)S(1)}, u32[]{:S(2)}, u32[]{:S(2)}) collective-permute-start(bf16[256,2560]{1,0:T(8,128)(2,1)} %refs_2_.3), channel_id=1, source_target_pairs={{0,8},{4,12},{8,0},{12,4},{16,24},{20,28},{24,16},{28,20},{1,9},{5... | collective-permute-start | bytes 3932168 | tf_op jit(solution)/shard_map/ppermute | solution.py:53
  11.2 39.1 %collective-permute-start.8 = (bf16[256,2560]{1,0:T(8,128)(2,1)}, bf16[256,2560]{1,0:T(8,128)(2,1)}, u32[]{:S(2)}, u32[]{:S(2)}) collective-permute-start(bf16[256,2560]{1,0:T(8,128)(2,1)} %refs_2_.3), channel_id=1, source_target_pairs={{0,16},{4,20},{8,24},{12,28},{16,0},{20,4},{24,8},{28,12},{1,17},{... | collective-permute-start | bytes 3932168 | tf_op jit(solution)/shard_map/ppermute | solution.py:53
  35.2 12.8 %collective-permute-start.5 = (bf16[320,896]{1,0:T(8,128)(2,1)}, bf16[320,896]{1,0:T(8,128)(2,1)}, u32[]{:S(2)}, u32[]{:S(2)}) collective-permute-start(bf16[320,896]{1,0:T(8,128)(2,1)} %collective-permute-done.refs_10_), channel_id=1, source_target_pairs={{0,1},{1,0},{2,3},{3,2},{4,5},{5,4},{6,7},{7,6},{8,9},{9,8},{10,11... | collective-permute-start | bytes 1720328 | tf_op jit(solution)/shard_map/ppermute | solution.py:53
  36.8 22.1 %all-to-all-start = ((bf16[8,144,256]{2,1,0:T(8,128)(2,1)}), bf16[8,144,256]{2,1,0:T(8,128)(2,1)S(1)}, u32[]{:S(2)}, u32[]{:S(2)}) async-start(bf16[8,144,256]{2,1,0:T(8,128)(2,1)} %pack.1), calls=%async_computation | async-start | bytes 1179648 | tf_op jit(solution)/shard_map/all_to_all | solution.py:345
  40.5 13.3 %copy-start.6 = (bf16[2560]{0:T(1024)(128)(2,1)S(1)}, bf16[2560]{0:T(1024)(128)(2,1)}, u32[]{:S(2)}) copy-start(bf16[2560]{0:T(1024)(128)(2,1)} %param.17) | copy-start | bytes 15364
  40.5 18.4 %collective-permute-start.4 = (bf16[320,896]{1,0:T(8,128)(2,1)}, bf16[320,896]{1,0:T(8,128)(2,1)}, u32[]{:S(2)}, u32[]{:S(2)}) collective-permute-start(bf16[320,896]{1,0:T(8,128)(2,1)} %collective-permute-done.refs_10_), channel_id=1, source_target_pairs={{0,4},{4,0},{8,12},{12,8},{16,20},{20,16},{24,28},{28,24},{1,5},{5... | collective-permute-start | bytes 1720328 | tf_op jit(solution)/shard_map/ppermute | solution.py:53
  41.0 17.9 %collective-permute-start.3 = (bf16[320,896]{1,0:T(8,128)(2,1)}, bf16[320,896]{1,0:T(8,128)(2,1)}, u32[]{:S(2)}, u32[]{:S(2)}) collective-permute-start(bf16[320,896]{1,0:T(8,128)(2,1)} %collective-permute-done.2.refs_8_), channel_id=1, source_target_pairs={{0,4},{4,0},{8,12},{12,8},{16,20},{20,16},{24,28},{28,24},{1,5},{5... | collective-permute-start | bytes 1720328 | tf_op jit(solution)/shard_map/ppermute | solution.py:53
  47.9 10.9 %collective-permute-start.6 = (bf16[320,896]{1,0:T(8,128)(2,1)}, bf16[320,896]{1,0:T(8,128)(2,1)}, u32[]{:S(2)}, u32[]{:S(2)}) collective-permute-start(bf16[320,896]{1,0:T(8,128)(2,1)} %collective-permute-done.5.refs_12_), channel_id=1, source_target_pairs={{0,4},{4,0},{8,12},{12,8},{16,20},{20,16},{24,28},{28,24},{1,5},{5... | collective-permute-start | bytes 1720328 | tf_op jit(solution)/shard_map/ppermute | solution.py:53
  48.8 23.6 %collective-permute-start.10 = (bf16[128,2560]{1,0:T(8,128)(2,1)}, bf16[128,2560]{1,0:T(8,128)(2,1)}, u32[]{:S(2)}, u32[]{:S(2)}) collective-permute-start(bf16[128,2560]{1,0:T(8,128)(2,1)} %slice.77), channel_id=1, source_target_pairs={{0,16},{4,20},{8,24},{12,28},{16,0},{20,4},{24,8},{28,12},{1,17},{... | collective-permute-start | bytes 1966088 | tf_op jit(solution)/shard_map/ppermute | solution.py:53
  52.3 20.1 %collective-permute-start.11 = (bf16[128,2560]{1,0:T(8,128)(2,1)}, bf16[128,2560]{1,0:T(8,128)(2,1)}, u32[]{:S(2)}, u32[]{:S(2)}) collective-permute-start(bf16[128,2560]{1,0:T(8,128)(2,1)} %slice.78), channel_id=1, source_target_pairs={{0,8},{4,12},{8,0},{12,4},{16,24},{20,28},{24,16},{28,20},{1,9},{5... | collective-permute-start | bytes 1966088 | tf_op jit(solution)/shard_map/ppermute | solution.py:53
  53.9 1.9 %copy-start = (bf16[640,2560]{1,0:T(8,128)(2,1)S(1)}, bf16[640,2560]{1,0:T(8,128)(2,1)}, u32[]{:S(2)}) copy-start(bf16[640,2560]{1,0:T(8,128)(2,1)} %wq_ref.3) | copy-start | bytes 9830404
  55.8 1.1 %copy-start.1 = (bf16[640,512]{1,0:T(8,128)(2,1)S(1)}, bf16[640,512]{1,0:T(8,128)(2,1)}, u32[]{:S(2)}) copy-start(bf16[640,512]{1,0:T(8,128)(2,1)} %wk_ref.3) | copy-start | bytes 1966084
  56.9 1.1 %copy-start.2 = (bf16[640,512]{1,0:T(8,128)(2,1)S(1)}, bf16[640,512]{1,0:T(8,128)(2,1)}, u32[]{:S(2)}) copy-start(bf16[640,512]{1,0:T(8,128)(2,1)} %wv_ref.3) | copy-start | bytes 1966084
  58.9 0.9 copy-start.3
  66.3 18.4 %collective-permute-start.7 = (bf16[256,896]{1,0:T(8,128)(2,1)S(1)}, bf16[256,896]{1,0:T(8,128)(2,1)S(1)}, u32[]{:S(2)}, u32[]{:S(2)}) collective-permute-start(bf16[256,896]{1,0:T(8,128)(2,1)S(1)} %get-tuple-element.18), channel_id=1, source_target_pairs={{0,8},{4,12},{8,0},{12,4},{16,24},{20,28},{24,16},{28,20},{1,9},{5... | collective-permute-start | bytes 1376264 | tf_op jit(solution)/shard_map/ppermute | solution.py:53
  71.9 22.0 %collective-permute-start.9 = (bf16[256,896]{1,0:T(8,128)(2,1)S(1)}, bf16[256,896]{1,0:T(8,128)(2,1)S(1)}, u32[]{:S(2)}, u32[]{:S(2)}) collective-permute-start(bf16[256,896]{1,0:T(8,128)(2,1)S(1)} %heads.6), channel_id=1, source_target_pairs={{0,16},{4,20},{8,24},{12,28},{16,0},{20,4},{24,8},{28,12},{1,17},{... | collective-permute-start | bytes 1376264 | tf_op jit(solution)/shard_map/ppermute | solution.py:53
  77.3 16.5 %collective-permute-start.12 = (bf16[256,896]{1,0:T(8,128)(2,1)S(1)}, bf16[256,896]{1,0:T(8,128)(2,1)S(1)}, u32[]{:S(2)}, u32[]{:S(2)}) collective-permute-start(bf16[256,896]{1,0:T(8,128)(2,1)S(1)} %heads.7), channel_id=1, source_target_pairs={{0,24},{4,28},{8,16},{12,20},{16,8},{20,12},{24,0},{28,4},{1,25},{... | collective-permute-start | bytes 1376264 | tf_op jit(solution)/shard_map/ppermute | solution.py:53

commit v5 on v4

--- a/solution.py
+++ b/solution.py
@@ -20,6 +20,7 @@
 
 TILES = 2 + GROUP
 WIDTH = TILES * HD
+ORDER = (6, 2, 4, 0)
 MIB = 1024 * 1024
 
 SMEM = pl.BlockSpec(memory_space=pltpu.SMEM)
@@ -76,26 +77,66 @@
     return copies
 
 
-def cut_kernel(place_ref, wk_ref, wv_ref, wq_ref, out_ref, sem):
-    part = pl.ds(pl.multiple_of(place_ref[1], 16), out_ref.shape[0])
+def cut_kernel(wk_ref, wv_ref, wq_ref, half_ref, whole_ref, sem):
+    me = lax.axis_index("ctx")
+    rows = half_ref.shape[0]
+    part = pl.ds(pl.multiple_of(me % 2 * rows, 16), rows)
     copies = []
-    for ref, (column, tiles, at) in zip((wk_ref, wv_ref, wq_ref), tile_sources(place_ref[0])):
-        column = pl.ds(pl.multiple_of(column, HD), tiles * HD)
-        copies.append((ref.at[part, column], out_ref.at[:, pl.ds(at * HD, tiles * HD)]))
+    for target, run in ((half_ref, part), (whole_ref, slice(None))):
+        for ref, (column, tiles, at) in zip(
+            (wk_ref, wv_ref, wq_ref), tile_sources(me // 2 % TEAM)
+        ):
+            column = pl.ds(pl.multiple_of(column, HD), tiles * HD)
+            copies.append((ref.at[run, column], target.at[:, pl.ds(at * HD, tiles * HD)]))
     for copy in start_all(copies, sem):
         copy.wait()
 
 
-def cut(place, piece_rows, weights, limit):
+def cut(weights):
+    shard = weights[0].shape[0]
     return pl.pallas_call(
         cut_kernel,
-        out_shape=jax.ShapeDtypeStruct((piece_rows, WIDTH), jnp.bfloat16),
-        in_specs=[SMEM] + [ANY] * 3,
-        out_specs=VMEM,
-        scratch_shapes=[pltpu.SemaphoreType.DMA((3,))],
-        compiler_params=pltpu.CompilerParams(vmem_limit_bytes=limit * MIB),
+        out_shape=[
+            jax.ShapeDtypeStruct((rows, WIDTH), jnp.bfloat16) for rows in (shard // 2, shard)
+        ],
+        in_specs=[ANY] * 3,
+        out_specs=[VMEM] * 2,
+        scratch_shapes=[pltpu.SemaphoreType.DMA((6,))],
+        compiler_params=pltpu.CompilerParams(vmem_limit_bytes=60 * MIB),
         name="cut",
-    )(place, *weights)
+    )(*weights)
+
+
+def gather_kernel(count, place_ref, cache_ref, *refs):
+    piece_refs = refs[:count]
+    w_ref, cache_value_t_ref, sem = refs[count:]
+    copies = []
+    for index, piece in enumerate(piece_refs):
+        start = pl.multiple_of(place_ref[1 + index], 16)
+        copies.append((piece, w_ref.at[pl.ds(start, piece.shape[0]), :]))
+    copies = start_all(copies, sem)
+    blocks_each = (cache_ref.shape[1] - NOTE_ROWS) // QBLK
+    for place in range(blocks_each * cache_ref.shape[0]):
+        part = pl.ds(place % blocks_each * QBLK, QBLK)
+        cache_value_t_ref[place] = cache_ref[place // blocks_each, part, pl.ds(HD, HD)].T
+    for copy in copies:
+        copy.wait()
+
+
+def gather(place, depth, cache, pieces):
+    total_blocks = cache.shape[0] * (cache.shape[1] - NOTE_ROWS) // QBLK
+    return pl.pallas_call(
+        functools.partial(gather_kernel, len(pieces)),
+        out_shape=[
+            jax.ShapeDtypeStruct((depth, WIDTH), jnp.bfloat16),
+            jax.ShapeDtypeStruct((total_blocks, HD, QBLK), jnp.bfloat16),
+        ],
+        in_specs=[SMEM, VMEM] + [ANY] * len(pieces),
+        out_specs=[VMEM] * 2,
+        scratch_shapes=[pltpu.SemaphoreType.DMA((len(pieces),))],
+        compiler_params=pltpu.CompilerParams(vmem_limit_bytes=16 * MIB),
+        name="gather",
+    )(place, cache, *pieces)
 
 
 def normed_rows(tokens, gain):
@@ -111,7 +152,7 @@
     lists_ref, ck_ref, cv_ref, payload_ref = refs
     prefix = ck_ref.shape[0]
     for target in range(team_count):
-        column = pl.ds(target // 2 % TEAM * HD, HD)
+        column = pl.ds(target % TEAM * HD, HD)
         payload_ref[target, pl.ds(0, prefix), pl.ds(0, HD)] = ck_ref[:, column]
         payload_ref[target, pl.ds(0, prefix), pl.ds(HD, HD)] = cv_ref[:, column]
         payload_ref[target, pl.ds(prefix, NOTE_ROWS), :] = lists_ref[...]
@@ -147,11 +188,11 @@
     place_ref, lists_ref = take(2)
     x_refs = take(x_count)
     gain_ref, bias_ref, table_ref, cache_ref = take(4)
+    cache_value_t_ref, w_ref = take(2)
+    piece_refs = take(piece_count)
+    (out_ref,) = take(1)
     if piece_count:
-        piece_refs = take(piece_count)
-        out_ref, w_ref, cache_value_t_ref = take(3)
-    else:
-        w_ref, cache_value_t_ref, out_ref = take(3)
+        (w_ref,) = take(1)
     q_buf, key_buf, value_t_buf, sem = take(4)
 
     rows = sum(x_ref.shape[0] for x_ref in x_refs)
@@ -159,7 +200,7 @@
     copies = []
     if piece_count:
         for index, piece in enumerate(piece_refs):
-            start = pl.multiple_of(place_ref[2 + index], 16)
+            start = pl.multiple_of(place_ref[place_ref.shape[0] - 3 + index], 16)
             copies.append((piece, w_ref.at[pl.ds(start, piece.shape[0]), :]))
         copies = start_all(copies, sem)
     blocks_each = (cache_ref.shape[1] - NOTE_ROWS) // QBLK
@@ -169,10 +210,6 @@
             return place, pl.ds(0, QBLK)
         return place // blocks_each, pl.ds(pl.multiple_of(place % blocks_each * QBLK, QBLK), QBLK)
 
-    if piece_count:
-        for place in range(blocks_each * cache_ref.shape[0]):
-            owner, part = cached(place)
-            cache_value_t_ref[place] = cache_ref[owner, part, pl.ds(HD, HD)].T
     x = [normed_rows(x_ref[...], gain_ref[...]) for x_ref in x_refs]
     x = jnp.concatenate(x, axis=0) if x_count > 1 else x[0]
     for copy in copies:
@@ -187,7 +224,7 @@
 
     lin = jnp.dot(x, w_ref[...], preferred_element_type=jnp.float32) + bias_ref[...]
     low_half = lax.broadcasted_iota(jnp.int32, (rows, HD), 1) < HD // 2
-    table = table_ref[...]
+    table = table_ref[pl.ds(FARS.index(far) * rows, rows), :]
     swapped = pltpu.roll(table, HD // 2, 1)
     cosine = jnp.where(low_half, table, swapped)
     sine = jnp.where(low_half, -swapped, table)
@@ -204,7 +241,7 @@
         else:
             value_t_buf[...] = value.astype(jnp.bfloat16).T
 
-    owner_list = place_ref[place_ref.shape[0] - 1] ^ far
+    owner_list = (place_ref[place_ref.shape[0] - 1] ^ far) // 2
     for block in range(blocks):
         span = pl.ds(block * QBLK, QBLK)
         for head in range(GROUP):
@@ -245,20 +282,20 @@
     operands = [place, lists, *x_parts, gain, bias, table, cache]
     specs = [SMEM] * 2 + [VMEM] * (len(x_parts) + 4)
     shapes = [jax.ShapeDtypeStruct((rows, WIDTH), jnp.bfloat16 if far else jnp.float32)]
+    operands += kept
+    specs += [VMEM] * 2
+    aliases = {}
     if pieces:
+        aliases = {len(operands) - 1: 1}
         operands += pieces
         specs += [ANY] * len(pieces)
-        total_blocks = cache.shape[0] * (cache.shape[1] - NOTE_ROWS) // QBLK
         shapes.append(jax.ShapeDtypeStruct((depth, WIDTH), jnp.bfloat16))
-        shapes.append(jax.ShapeDtypeStruct((total_blocks, HD, QBLK), jnp.bfloat16))
-    else:
-        operands += kept
-        specs += [VMEM] * 2
     return pl.pallas_call(
         functools.partial(heads_kernel, far, len(x_parts), len(pieces)),
         out_shape=shapes,
         in_specs=specs,
         out_specs=[VMEM] * len(shapes),
+        input_output_aliases=aliases,
         scratch_shapes=[
             pltpu.VMEM((rows, GROUP * HD), jnp.bfloat16),
             pltpu.VMEM((rows, HD), jnp.bfloat16),
@@ -266,18 +303,14 @@
             pltpu.SemaphoreType.DMA((max(len(pieces), 1),)),
         ],
         compiler_params=pltpu.CompilerParams(vmem_limit_bytes=16 * MIB),
-        cost_estimate=pl.CostEstimate(
-            flops=2 * rows * depth * WIDTH,
-            bytes_accessed=2 * depth * (rows + WIDTH),
-            transcendentals=rows * GROUP * (SEL + 1) * QBLK,
-        ),
+        cost_estimate=pl.CostEstimate(flops=1, bytes_accessed=1, transcendentals=0),
         name="heads",
     )(*operands)
 
 
-def finish_kernel(place_ref, *refs):
-    context_ref, keys_ref, values_ref = refs[len(FARS) :]
-    for far, part in zip(FARS, refs):
+def finish_kernel(fars, place_ref, *refs):
+    context_ref, keys_ref, values_ref = refs[-3:]
+    for far, part in zip(fars, refs):
         sources = tile_sources(place_ref[0] ^ (far // 2))
         for target, (column, tiles, at) in zip((keys_ref, values_ref, context_ref), sources):
             target[:, pl.ds(pl.multiple_of(column, HD), tiles * HD)] = part[
@@ -286,19 +319,51 @@
 
 
 def finish(place, parts):
-    rows = parts[0].shape[0]
-    return pl.pallas_call(
-        finish_kernel,
+    fars = tuple(parts)
+    rows = parts[fars[0]].shape[0]
+    return pl.pallas_call(
+        functools.partial(finish_kernel, fars),
         out_shape=[
-            jax.ShapeDtypeStruct((rows, TEAM * GROUP * HD), jnp.float32),
-            jax.ShapeDtypeStruct((rows, TEAM * HD), jnp.float32),
-            jax.ShapeDtypeStruct((rows, TEAM * HD), jnp.float32),
+            jax.ShapeDtypeStruct((rows, TEAM * width), jnp.float32)
+            for width in (GROUP * HD, HD, HD)
         ],
-        in_specs=[SMEM] + [VMEM] * len(parts),
+        in_specs=[SMEM] + [VMEM] * len(fars),
         out_specs=[VMEM] * 3,
         compiler_params=pltpu.CompilerParams(vmem_limit_bytes=16 * MIB),
         name="finish",
-    )(place, *parts)
+    )(place, *parts.values())
+
+
+def last_kernel(fars, place_ref, *refs):
+    count = len(fars)
+    outs, wides, sem = refs[count + 3 : count + 6], refs[count + 6 : -1], refs[-1]
+    copies = []
+    for far, part_ref, wide in zip(fars, refs, wides):
+        wide[...] = part_ref[...].astype(jnp.float32)
+        for index, (column, tiles, at) in enumerate(tile_sources(place_ref[0] ^ (far // 2))):
+            column = pl.ds(pl.multiple_of(column, HD), tiles * HD)
+            copies.append(
+                (wide.at[:, pl.ds(at * HD, tiles * HD)], outs[(1, 2, 0)[index]].at[:, column])
+            )
+    for copy in start_all(copies, sem):
+        copy.wait()
+
+
+def finish_last(place, parts, outs):
+    fars = tuple(parts)
+    count = len(fars)
+    shape = parts[fars[0]].shape
+    return pl.pallas_call(
+        functools.partial(last_kernel, fars),
+        out_shape=[jax.ShapeDtypeStruct(out.shape, out.dtype) for out in outs],
+        in_specs=[SMEM] + [VMEM] * count + [ANY] * 3,
+        out_specs=[ANY] * 3,
+        input_output_aliases={1 + count + index: index for index in range(3)},
+        scratch_shapes=[pltpu.VMEM(shape, jnp.float32)] * count
+        + [pltpu.SemaphoreType.DMA((3 * count,))],
+        compiler_params=pltpu.CompilerParams(vmem_limit_bytes=16 * MIB),
+        name="finish_last",
+    )(place, *parts.values(), *outs)
 
 
 tie = lax.optimization_barrier
@@ -328,26 +393,28 @@
 
     tokens_2 = swap(tokens, "ctx", 2)
     tokens_4 = swap(tokens, "ctx", 4)
+    low, high = tokens_2[: rows // 2], tokens_4[rows // 2 :]
 
     grp_order = [0]
     for bit in bits_of(grp_size, 1):
         grp_order += [far ^ bit for far in grp_order]
     piece_places = [(far, over) for far in sorted(grp_order) if far for over in (0, 1)]
     place = jnp.stack(
-        [group, core * piece_rows, layer * shard]
+        [group, layer * shard]
         + [(layer ^ far) * shard + (core ^ over) * piece_rows for far, over in piece_places]
         + [me]
     ).astype(jnp.int32)
     weights = (w_key, w_value, w_query)
-    half = cut(jnp.stack([group, core * piece_rows]).astype(jnp.int32), piece_rows, weights, 60)
-
-    payload = pack(ctx_size, block_lists.reshape(-1), (cache_keys, cache_values))
-    cache = lax.all_to_all(payload, "ctx", 0, 0)
+    half, whole = cut(weights)
+
+    payload = pack(ctx_size // 2, block_lists.reshape(-1), (cache_keys, cache_values))
+    same_core = [list(range(c, ctx_size, 2)) for c in range(2)]
+    cache = lax.all_to_all(payload, "ctx", 0, 0, axis_index_groups=same_core)
     row_ids = jnp.arange(rows, dtype=jnp.int32)
-    tables = [
-        rope_table(start_position[0] + ((me ^ far) * grp_size + layer) * rows + row_ids)
-        for far in FARS
-    ]
+    tables = rope_table(
+        start_position[0]
+        + jnp.concatenate([((me ^ far) * grp_size + layer) * rows + row_ids for far in FARS])
+    )
     bias = jnp.concatenate(
         [
             lax.dynamic_slice_in_dim(b_key, group * HD, HD),
@@ -361,23 +428,25 @@
         for far in sorted(held):
             held[far ^ bit] = swap(held[far], "grp", bit)
         if index == 0:
-            held[bit], tables, bias = tie((held[bit], tables, bias))
-    whole = cut(jnp.stack([group, 0]).astype(jnp.int32), shard, weights, 14)
+            held[bit], tables, bias, cache, *_ = tie((held[bit], tables, bias, cache, low, high))
     pieces = [whole]
     for far, over in piece_places:
         pieces.append(swap(held[far], "ctx", 1) if over else held[far])
 
-    half_rows = rows // 2
-    tokens_6 = [
-        swap(tokens_2[:half_rows], "ctx", 4),
-        swap(tokens_4[half_rows:], "ctx", 2),
-    ]
-
+    tokens_6 = [swap(low, "ctx", 4), swap(high, "ctx", 2)]
     lists = cache[:, cache_keys.shape[0], :].astype(jnp.int32)
+    blocks_each = cache_keys.shape[0] // QBLK
+    owner = jnp.maximum(lists, 0) // blocks_each
+    owner = ((owner ^ me) & 1) * (ctx_size // 2) + owner // 2
+    lists = jnp.where(lists < 0, -1, owner * blocks_each + jnp.maximum(lists, 0) % blocks_each)
+    cache = jnp.concatenate([cache, swap(cache, "ctx", 1)], axis=0)
 
     x_parts = {0: [tokens], 2: [tokens_2], 4: [tokens_4], 6: tokens_6}
-    kept, parts = None, {}
-    for far in (2, 4, 6, 0):
+    early, late = pieces[:-2], pieces[-2:]
+    w_part, cache_value_t = gather(place, tokens.shape[1], cache, early)
+    late[0], x_parts[6] = tie((late[0], tokens_6))
+    kept, parts = [cache_value_t, w_part], {}
+    for far in ORDER:
         out, *rest = heads(
             far,
             place,
@@ -385,14 +454,17 @@
             x_parts[far],
             norm_gain[None, :],
             bias,
-            tables[FARS.index(far)],
+            tables,
             cache,
-            [] if kept else pieces,
+            late,
             kept,
         )
-        kept = kept or rest
+        if rest:
+            late, kept = [], [cache_value_t, rest[0]]
         parts[far] = swap(out, "ctx", far) if far else out
-    return tuple(finish(place, [parts[far] for far in FARS]))
+    early, late = ORDER[-1:] + ORDER[:-3], ORDER[-3:-1]
+    outs = finish(place, {far: parts[far] for far in early})
+    return tuple(finish_last(place, {far: parts[far] for far in late}, outs))
 
 
 def solution(mesh):

time: 97.1 us -> 88.2 us (0.908)
  local copies, waits for them, and re-layouts: 9.1 us -> 5.31 us
  other arithmetic: 4.46 us -> 1.96 us
  waiting for transfers between devices: 33 us -> 31.4 us
    pallas_call x4, Pallas kernels: 21.2 us -> 17.3 us  [heads(): pl.pallas_call(functools.partial(heads_kernel, far, len(x_parts), len(pie...]
    unnamed x29 -> x25, local copies, waits for them, and re-layouts: 5.05 us -> 1.34 us
    pallas_call x3 -> x4, Pallas kernels: 6.07 us -> 9.15 us  [the longest x1 2.72 us: cut(): pl.pallas_call(cut_kernel, out_shape=[jax.ShapeDtypeStruct((rows, WIDTH),...]
    cos x2 -> x1, other arithmetic: 3.56 us -> 1.86 us  [rope_table(): return jnp.cos(angles)]
    ppermute x13 -> x14, waiting for transfers between devices: 33 us -> 31.4 us  [swap(): return lax.ppermute(value, axis, [(i, i ^ bit) for i in range(size)])]
    slice x2, local copies, waits for them, and re-layouts: 2.85 us -> 1.8 us  [on_device(): low, high = (tokens_2[:rows // 2], tokens_4[rows // 2:])]
    concatenate x0 -> x1, local copies, waits for them, and re-layouts: none -> 0.98 us  [on_device(): cache = jnp.concatenate([cache, swap(cache, 'ctx', 1)], axis=0)]
    ppermute x13 -> x14, starting transfers between devices: 16.4 us -> 16.6 us  [swap(): return lax.ppermute(value, axis, [(i, i ^ bit) for i in range(size)])]
  transfers between devices with their start and end apart: 14 -> 15, of which waited for: 3 -> 7; matrix products, arithmetic and copies ran while one was open for 8% -> 7% of each run, Pallas kernels for 24% -> 23%
where the time goes in v5:
time: 88.2 us; the launch traced here: 87.8 us
  waiting for transfers between devices  31.4 us (36%)
  Pallas kernels  27.2 us (31%)
  starting transfers between devices  20 us (23%)
  local copies, waits for them, and re-layouts  5.31 us (6%)
  other arithmetic  1.96 us (2%)
  between operations  1.81 us (2%)
    ppermute x14, waiting for transfers between devices, swap(): return lax.ppermute(value, axis, [(i, i ^ bit) for i in range(size)])  31.4 us
    pallas_call x4, Pallas kernels, heads(): pl.pallas_call(functools.partial(heads_kernel, far, len(x_parts), len(pie...  17.3 us
    ppermute x14, starting transfers between devices, swap(): return lax.ppermute(value, axis, [(i, i ^ bit) for i in range(size)])  16.6 us
    all_to_all x1, starting transfers between devices, on_device(): cache = lax.all_to_all(payload, 'ctx', 0, 0, axis_index_groups=same_core)  3.45 us
    pallas_call x1, Pallas kernels, cut(): pl.pallas_call(cut_kernel, out_shape=[jax.ShapeDtypeStruct((rows, WIDTH),...  2.72 us
    pallas_call x1, Pallas kernels, finish(): pl.pallas_call(functools.partial(finish_kernel, fars), out_shape=[jax.Sha...  2.52 us
    pallas_call x1, Pallas kernels, gather(): pl.pallas_call(functools.partial(gather_kernel, len(pieces)), out_shape=[...  2.05 us
    pallas_call x1, Pallas kernels, finish_last(): pl.pallas_call(functools.partial(last_kernel, fars), out_shape=[jax.Shape...  1.87 us
  transfers between devices with their start and end apart: 15, of which 7 were waited for; matrix products, arithmetic and copies ran while one was open for 7% of the time, Pallas kernels for 23%

profile of v5, /device:TPU:0, one launch (start us, length us, event | category | flops | bytes accessed | tf_op | source)
XLA Modules:
  0.0 87.8 jit_solution(1109006313440971486)
XLA Ops:
  0.7 3.0 %collective-permute-start.1 = (bf16[256,2560]{1,0:T(8,128)(2,1)}, bf16[256,2560]{1,0:T(8,128)(2,1)S(1)}, u32[]{:S(2)}, u32[]{:S(2)}) collective-permute-start(bf16[256,2560]{1,0:T(8,128)(2,1)} %refs_2_.3), channel_id=1, source_target_pairs={{0,8},{4,12},{8,0},{12,4},{16,24},{20,28},{24,16},{28,20},{1,9},{5... | collective-permute-start | bytes 3932168 | tf_op jit(solution)/shard_map/ppermute | solution.py:54
  3.7 1.5 %collective-permute-start.2 = (bf16[256,2560]{1,0:T(8,128)(2,1)}, bf16[256,2560]{1,0:T(8,128)(2,1)S(1)}, u32[]{:S(2)}, u32[]{:S(2)}) collective-permute-start(bf16[256,2560]{1,0:T(8,128)(2,1)} %refs_2_.3), channel_id=1, source_target_pairs={{0,16},{4,20},{8,24},{12,28},{16,0},{20,4},{24,8},{28,12},{1,17},{... | collective-permute-start | bytes 3932168 | tf_op jit(solution)/shard_map/ppermute | solution.py:54
  5.3 2.7 %cut.1 = (bf16[320,896]{1,0:T(8,128)(2,1)}, bf16[640,896]{1,0:T(8,128)(2,1)}) custom-call(bf16[640,512]{1,0:T(8,128)(2,1)} %wk_ref.1, bf16[640,512]{1,0:T(8,128)(2,1)} %wv_ref.1, bf16[640,2560]{1,0:T(8,128)(2,1)} %wq_ref.1), custom_call_target="tpu_custom_call" | custom-call | tf_op jit(solution)/shard_map/cut/pallas_call | solution.py:97
  8.0 1.6 %collective-permute-start.4 = (bf16[320,896]{1,0:T(8,128)(2,1)}, bf16[320,896]{1,0:T(8,128)(2,1)}, u32[]{:S(2)}, u32[]{:S(2)}) collective-permute-start(bf16[320,896]{1,0:T(8,128)(2,1)} %get-tuple-element.19), channel_id=1, source_target_pairs={{0,1},{1,0},{2,3},{3,2},{4,5},{5,4},{6,7},{7,6},{8,9},{9,8},{10,11... | collective-permute-start | bytes 1720328 | tf_op jit(solution)/shard_map/ppermute | solution.py:54
  9.6 2.6 %collective-permute-start = (bf16[320,896]{1,0:T(8,128)(2,1)}, bf16[320,896]{1,0:T(8,128)(2,1)}, u32[]{:S(2)}, u32[]{:S(2)}) collective-permute-start(bf16[320,896]{1,0:T(8,128)(2,1)} %get-tuple-element.19), channel_id=1, source_target_pairs={{0,2},{1,3},{2,0},{3,1},{4,6},{5,7},{6,4},{7,5},{8,10},{9,11},{10,... | collective-permute-start | bytes 1720328 | tf_op jit(solution)/shard_map/ppermute | solution.py:54
  12.5 0.8 pack.1
  13.3 3.5 %all-to-all-start = ((bf16[4,144,256]{2,1,0:T(8,128)(2,1)}), bf16[4,144,256]{2,1,0:T(8,128)(2,1)S(1)}, u32[]{:S(2)}, u32[]{:S(2)}) async-start(bf16[4,144,256]{2,1,0:T(8,128)(2,1)} %pack.1), calls=%async_computation | async-start | bytes 589824 | tf_op jit(solution)/shard_map/all_to_all | solution.py:412
  17.4 0.8 dynamic_slice.11
  18.4 1.9 %add_cosine_fusion.refs_6_.refs_5_ = f32[1024,128]{1,0:T(8,128)S(1)} fusion(f32[128]{0:T(128)S(1)} %copy-done.6, f32[1024]{0:T(1024)S(1)} %get-tuple-element.41, f32[128]{0:T(128)S(1)} %copy-done.7, f32[1024]{0:T(1024)S(1)} %get-tuple-element.40, f32[128]{0:T(128)S(1)} %copy-done.8, f32[1024]{0:T(1024)S(1)} %get-tuple-element.35, f32[128]{0:T(128)S(1)} %copy-done.9, ...), kind=kLoop, calls=%fused_computation | loop fusion | flops 1048576 | bytes 543232 | tf_op jit(solution)/shard_map/cos | solution.py:49
  20.3 13.3 %collective-permute-done.1.refs_2_ = bf16[256,2560]{1,0:T(8,128)(2,1)S(1)} collective-permute-done((bf16[256,2560]{1,0:T(8,128)(2,1)}, bf16[256,2560]{1,0:T(8,128)(2,1)S(1)}, u32[]{:S(2)}, u32[]{:S(2)}) %collective-permute-start.1) | collective-permute-done | bytes 1310752 | tf_op jit(solution)/shard_map/ppermute | solution.py:54
  33.6 0.9 %slice.28 = bf16[128,2560]{1,0:T(8,128)(2,1)} slice(bf16[256,2560]{1,0:T(8,128)(2,1)S(1)} %collective-permute-done.1.refs_2_), slice={[0:128], [0:2560]} | slice | bytes 1310720 | tf_op jit(solution)/shard_map/slice | solution.py:396
  34.4 2.1 %collective-permute-done.2.refs_2_ = bf16[256,2560]{1,0:T(8,128)(2,1)S(1)} collective-permute-done((bf16[256,2560]{1,0:T(8,128)(2,1)}, bf16[256,2560]{1,0:T(8,128)(2,1)S(1)}, u32[]{:S(2)}, u32[]{:S(2)}) %collective-permute-start.2) | collective-permute-done | bytes 1310752 | tf_op jit(solution)/shard_map/ppermute | solution.py:54
  36.6 0.9 %slice.29 = bf16[128,2560]{1,0:T(8,128)(2,1)} slice(bf16[256,2560]{1,0:T(8,128)(2,1)S(1)} %collective-permute-done.2.refs_2_), slice={[128:256], [0:2560]} | slice | bytes 1310720 | tf_op jit(solution)/shard_map/slice | solution.py:396
  37.5 1.6 %collective-permute-start.7 = (bf16[320,896]{1,0:T(8,128)(2,1)}, bf16[320,896]{1,0:T(8,128)(2,1)}, u32[]{:S(2)}, u32[]{:S(2)}) collective-permute-start(bf16[320,896]{1,0:T(8,128)(2,1)} %collective-permute-done.refs_3_), channel_id=1, source_target_pairs={{0,1},{1,0},{2,3},{3,2},{4,5},{5,4},{6,7},{7,6},{8,9},{9,8},{10,11... | collective-permute-start | bytes 1720328 | tf_op jit(solution)/shard_map/ppermute | solution.py:54
  39.7 1.5 %collective-permute-start.8 = (bf16[128,2560]{1,0:T(8,128)(2,1)}, bf16[128,2560]{1,0:T(8,128)(2,1)S(1)}, u32[]{:S(2)}, u32[]{:S(2)}) collective-permute-start(bf16[128,2560]{1,0:T(8,128)(2,1)} %slice.28), channel_id=1, source_target_pairs={{0,16},{4,20},{8,24},{12,28},{16,0},{20,4},{24,8},{28,12},{1,17},{... | collective-permute-start | bytes 1966088 | tf_op jit(solution)/shard_map/ppermute | solution.py:54
  41.8 8.7 %collective-permute-done.7.refs_10_ = bf16[320,896]{1,0:T(8,128)(2,1)} collective-permute-done((bf16[320,896]{1,0:T(8,128)(2,1)}, bf16[320,896]{1,0:T(8,128)(2,1)}, u32[]{:S(2)}, u32[]{:S(2)}) %collective-permute-start.7) | collective-permute-done | bytes 573472 | tf_op jit(solution)/shard_map/ppermute | solution.py:54
  50.6 1.0 %constant_dynamic-update-slice_fusion.cache_ref.refs_7_.refs_6_ = bf16[8,144,256]{2,1,0:T(8,128)(2,1)S(1)} fusion(bf16[8,144,256]{2,1,0:T(8,128)(2,1)S(1)} %constant_dynamic-update-slice_fusion.1, bf16[4,144,256]{2,1,0:T(8,128)(2,1)} %collective-permute-done.3), kind=kLoop, calls=%fused_computation.1 | loop fusion | bytes 589824 | tf_op jit(solution)/shard_map/concatenate | solution.py:442
  51.6 1.2 %copy-done.1 = bf16[640,896]{1,0:T(8,128)(2,1)S(1)} copy-done((bf16[640,896]{1,0:T(8,128)(2,1)S(1)}, bf16[640,896]{1,0:T(8,128)(2,1)}, u32[]{:S(2)}) %copy-start.1) | copy-done | bytes 1146904
  52.8 2.0 %gather.1 = (bf16[2560,896]{1,0:T(8,128)(2,1)S(1)}, bf16[8,128,128]{2,1,0:T(8,128)(2,1)S(1)}) custom-call(s32[9]{0:T(128)S(1)} %stack.39.place_ref.refs_0_, bf16[8,144,256]{2,1,0:T(8,128)(2,1)S(1)} %constant_dynamic-update-slice_fusion.cache_ref.refs_7_.refs_6_, bf16[640,896]{1,0:T(8,128)(2,1)S(1)} %copy-done.1, ...), custom_call_target="tpu_custom_call" | custom-call | tf_op jit(solution)/shard_map/gather/pallas_call | solution.py:128
  54.9 1.8 %collective-permute-done.8.refs_2_ = bf16[128,2560]{1,0:T(8,128)(2,1)S(1)} collective-permute-done((bf16[128,2560]{1,0:T(8,128)(2,1)}, bf16[128,2560]{1,0:T(8,128)(2,1)S(1)}, u32[]{:S(2)}, u32[]{:S(2)}) %collective-permute-start.8) | collective-permute-done | bytes 655392 | tf_op jit(solution)/shard_map/ppermute | solution.py:54
  56.7 1.2 %collective-permute-done.9.refs_3_ = bf16[128,2560]{1,0:T(8,128)(2,1)S(1)} collective-permute-done((bf16[128,2560]{1,0:T(8,128)(2,1)}, bf16[128,2560]{1,0:T(8,128)(2,1)S(1)}, u32[]{:S(2)}, u32[]{:S(2)}) %collective-permute-start.9) | collective-permute-done | bytes 655392 | tf_op jit(solution)/shard_map/ppermute | solution.py:54
  57.9 4.9 %heads.4 = (bf16[256,896]{1,0:T(8,128)(2,1)S(1)}, bf16[2560,896]{1,0:T(8,128)(2,1)S(1)}) custom-call(s32[9]{0:T(128)S(1)} %stack.39.place_ref.refs_0_, s32[4,256]{1,0:T(4,128)S(1)} %fusion.6.refs_1_, bf16[128,2560]{1,0:T(8,128)(2,1)S(1)} %collective-permute-done.8.refs_2_, ...), custom_call_target="tpu_custom_call", output_to_operand_aliasing={{1}: (9, {})} | custom-call | flops 1 | bytes 1 | tf_op jit(solution)/shard_map/heads/pallas_call | solution.py:293
  62.8 1.1 %collective-permute-start.13 = (bf16[256,896]{1,0:T(8,128)(2,1)S(1)}, bf16[256,896]{1,0:T(8,128)(2,1)S(1)}, u32[]{:S(2)}, u32[]{:S(2)}) collective-permute-start(bf16[256,896]{1,0:T(8,128)(2,1)S(1)} %get-tuple-element.31), channel_id=1, source_target_pairs={{0,24},{4,28},{8,16},{12,20},{16,8},{20,12},{24,0},{28,4},{1,25},{... | collective-permute-start | bytes 1376264 | tf_op jit(solution)/shard_map/ppermute | solution.py:54
  63.9 4.2 %heads.5 = bf16[256,896]{1,0:T(8,128)(2,1)S(1)} custom-call(s32[9]{0:T(128)S(1)} %stack.39.place_ref.refs_0_, s32[4,256]{1,0:T(4,128)S(1)} %fusion.6.refs_1_, bf16[256,2560]{1,0:T(8,128)(2,1)S(1)} %collective-permute-done.1.refs_2_, bf16[1,2560]{1,0:T(2,128)(2,1)S(1)} %broadcast_in_dim.34.refs_4_.refs_3_, f32[1,896]{1,0:T(1,128)S(1)} %maximum_convert_fusion.refs_5_.refs_4_, ...), custom_call_target="tpu_custom_call" | custom-call | flops 1 | bytes 1 | tf_op jit(solution)/shard_map/heads/pallas_call | solution.py:293
  68.1 1.0 %collective-permute-start.11 = (bf16[256,896]{1,0:T(8,128)(2,1)S(1)}, bf16[256,896]{1,0:T(8,128)(2,1)S(1)}, u32[]{:S(2)}, u32[]{:S(2)}) collective-permute-start(bf16[256,896]{1,0:T(8,128)(2,1)S(1)} %heads.5), channel_id=1, source_target_pairs={{0,8},{4,12},{8,0},{12,4},{16,24},{20,28},{24,16},{28,20},{1,9},{5... | collective-permute-start | bytes 1376264 | tf_op jit(solution)/shard_map/ppermute | solution.py:54
  69.1 4.2 %heads.6 = bf16[256,896]{1,0:T(8,128)(2,1)S(1)} custom-call(s32[9]{0:T(128)S(1)} %stack.39.place_ref.refs_0_, s32[4,256]{1,0:T(4,128)S(1)} %fusion.6.refs_1_, bf16[256,2560]{1,0:T(8,128)(2,1)S(1)} %collective-permute-done.2.refs_2_, bf16[1,2560]{1,0:T(2,128)(2,1)S(1)} %broadcast_in_dim.34.refs_4_.refs_3_, f32[1,896]{1,0:T(1,128)S(1)} %maximum_convert_fusion.refs_5_.refs_4_, ...), custom_call_target="tpu_custom_call" | custom-call | flops 1 | bytes 1 | tf_op jit(solution)/shard_map/heads/pallas_call | solution.py:293
  73.2 1.6 %collective-permute-start.12 = (bf16[256,896]{1,0:T(8,128)(2,1)S(1)}, bf16[256,896]{1,0:T(8,128)(2,1)S(1)}, u32[]{:S(2)}, u32[]{:S(2)}) collective-permute-start(bf16[256,896]{1,0:T(8,128)(2,1)S(1)} %heads.6), channel_id=1, source_target_pairs={{0,16},{4,20},{8,24},{12,28},{16,0},{20,4},{24,8},{28,12},{1,17},{... | collective-permute-start | bytes 1376264 | tf_op jit(solution)/shard_map/ppermute | solution.py:54
  74.8 4.1 %heads.7.refs_0_ = f32[256,896]{1,0:T(8,128)S(1)} custom-call(s32[9]{0:T(128)S(1)} %stack.39.place_ref.refs_0_, s32[4,256]{1,0:T(4,128)S(1)} %fusion.6.refs_1_, bf16[256,2560]{1,0:T(8,128)(2,1)S(1)} %copy-done, bf16[1,2560]{1,0:T(2,128)(2,1)S(1)} %broadcast_in_dim.34.refs_4_.refs_3_, f32[1,896]{1,0:T(1,128)S(1)} %maximum_convert_fusion.refs_5_.refs_4_, ...), custom_call_target="tpu_custom_call" | custom-call | flops 1 | bytes 1 | tf_op jit(solution)/shard_map/heads/pallas_call | solution.py:293
  79.0 2.5 %finish.1 = (f32[256,2560]{1,0:T(8,128)}, f32[256,512]{1,0:T(8,128)}, f32[256,512]{1,0:T(8,128)}) custom-call(s32[9]{0:T(128)S(1)} %stack.39.place_ref.refs_0_, f32[256,896]{1,0:T(8,128)S(1)} %heads.7.refs_0_, bf16[256,896]{1,0:T(8,128)(2,1)S(1)} %collective-permute-done.13.refs_1_), custom_call_target="tpu_custom_call" | custom-call | tf_op jit(solution)/shard_map/finish/pallas_call | solution.py:324
  81.5 2.9 %collective-permute-done.11.refs_0_ = bf16[256,896]{1,0:T(8,128)(2,1)S(1)} collective-permute-done((bf16[256,896]{1,0:T(8,128)(2,1)S(1)}, bf16[256,896]{1,0:T(8,128)(2,1)S(1)}, u32[]{:S(2)}, u32[]{:S(2)}) %collective-permute-start.11) | collective-permute-done | bytes 458784 | tf_op jit(solution)/shard_map/ppermute | solution.py:54
  84.4 1.4 %collective-permute-done.12.refs_1_ = bf16[256,896]{1,0:T(8,128)(2,1)S(1)} collective-permute-done((bf16[256,896]{1,0:T(8,128)(2,1)S(1)}, bf16[256,896]{1,0:T(8,128)(2,1)S(1)}, u32[]{:S(2)}, u32[]{:S(2)}) %collective-permute-start.12) | collective-permute-done | bytes 458784 | tf_op jit(solution)/shard_map/ppermute | solution.py:54
  85.8 1.9 %finish_last.1 = (f32[256,2560]{1,0:T(8,128)}, f32[256,512]{1,0:T(8,128)}, f32[256,512]{1,0:T(8,128)}) custom-call(s32[9]{0:T(128)S(1)} %stack.39.place_ref.refs_0_, bf16[256,896]{1,0:T(8,128)(2,1)S(1)} %collective-permute-done.11.refs_0_, ...), custom_call_target="tpu_custom_call", output_to_operand_aliasing={{0}: (3, {}), {1}: (4, {}), {2}: (5, {})} | custom-call | tf_op jit(solution)/shard_map/finish_last/pallas_call | solution.py:356
  (54 shorter events, 1.7 us)
Async XLA Ops:
  0.6 17.7 %copy-start.6 = (f32[128]{0:T(128)S(1)}, f32[128]{0:T(128)}, u32[]{:S(2)}) copy-start(f32[128]{0:T(128)} %constant.171) | copy-start | bytes 1540
  0.6 17.7 %copy-start.7 = (f32[128]{0:T(128)S(1)}, f32[128]{0:T(128)}, u32[]{:S(2)}) copy-start(f32[128]{0:T(128)} %constant.169) | copy-start | bytes 1540
  0.7 17.7 %copy-start.8 = (f32[128]{0:T(128)S(1)}, f32[128]{0:T(128)}, u32[]{:S(2)}) copy-start(f32[128]{0:T(128)} %constant.167) | copy-start | bytes 1540
  0.7 17.7 %copy-start.9 = (f32[128]{0:T(128)S(1)}, f32[128]{0:T(128)}, u32[]{:S(2)}) copy-start(f32[128]{0:T(128)} %constant.165) | copy-start | bytes 1540
  0.7 11.5 %copy-start.5 = (s32[20,2,4]{0,2,1:T(4,128)S(1)}, s32[20,2,4]{0,2,1:T(4,128)}, u32[]{:S(2)}) copy-start(s32[20,2,4]{0,2,1:T(4,128)} %param.23) | copy-start | bytes 1924
  0.7 11.8 %copy-start.3 = (bf16[128,512]{1,0:T(8,128)(2,1)S(1)}, bf16[128,512]{1,0:T(8,128)(2,1)}, u32[]{:S(2)}) copy-start(bf16[128,512]{1,0:T(8,128)(2,1)} %refs_2_.2) | copy-start | bytes 393220
  0.7 11.8 %copy-start.2 = (bf16[128,512]{1,0:T(8,128)(2,1)S(1)}, bf16[128,512]{1,0:T(8,128)(2,1)}, u32[]{:S(2)}) copy-start(bf16[128,512]{1,0:T(8,128)(2,1)} %refs_1_.1) | copy-start | bytes 393220
  0.7 17.5 %copy-start.10 = (bf16[512]{0:T(512)(128)(2,1)S(1)}, bf16[512]{0:T(512)(128)(2,1)}, u32[]{:S(2)}) copy-start(bf16[512]{0:T(512)(128)(2,1)} %param.20) | copy-start | bytes 3076
  0.7 17.5 %copy-start.11 = (bf16[512]{0:T(512)(128)(2,1)S(1)}, bf16[512]{0:T(512)(128)(2,1)}, u32[]{:S(2)}) copy-start(bf16[512]{0:T(512)(128)(2,1)} %param.19) | copy-start | bytes 3076
  0.7 32.8 %collective-permute-start.1 = (bf16[256,2560]{1,0:T(8,128)(2,1)}, bf16[256,2560]{1,0:T(8,128)(2,1)S(1)}, u32[]{:S(2)}, u32[]{:S(2)}) collective-permute-start(bf16[256,2560]{1,0:T(8,128)(2,1)} %refs_2_.3), channel_id=1, source_target_pairs={{0,8},{4,12},{8,0},{12,4},{16,24},{20,28},{24,16},{28,20},{1,9},{5... | collective-permute-start | bytes 3932168 | tf_op jit(solution)/shard_map/ppermute | solution.py:54
  3.7 32.8 %collective-permute-start.2 = (bf16[256,2560]{1,0:T(8,128)(2,1)}, bf16[256,2560]{1,0:T(8,128)(2,1)S(1)}, u32[]{:S(2)}, u32[]{:S(2)}) collective-permute-start(bf16[256,2560]{1,0:T(8,128)(2,1)} %refs_2_.3), channel_id=1, source_target_pairs={{0,16},{4,20},{8,24},{12,28},{16,0},{20,4},{24,8},{28,12},{1,17},{... | collective-permute-start | bytes 3932168 | tf_op jit(solution)/shard_map/ppermute | solution.py:54
  8.0 31.1 %copy-start.4 = (bf16[2560]{0:T(1024)(128)(2,1)S(1)}, bf16[2560]{0:T(1024)(128)(2,1)}, u32[]{:S(2)}) copy-start(bf16[2560]{0:T(1024)(128)(2,1)} %param.14) | copy-start | bytes 15364
  8.0 31.2 %collective-permute-start.4 = (bf16[320,896]{1,0:T(8,128)(2,1)}, bf16[320,896]{1,0:T(8,128)(2,1)}, u32[]{:S(2)}, u32[]{:S(2)}) collective-permute-start(bf16[320,896]{1,0:T(8,128)(2,1)} %get-tuple-element.19), channel_id=1, source_target_pairs={{0,1},{1,0},{2,3},{3,2},{4,5},{5,4},{6,7},{7,6},{8,9},{9,8},{10,11... | collective-permute-start | bytes 1720328 | tf_op jit(solution)/shard_map/ppermute | solution.py:54
  9.6 27.8 %collective-permute-start = (bf16[320,896]{1,0:T(8,128)(2,1)}, bf16[320,896]{1,0:T(8,128)(2,1)}, u32[]{:S(2)}, u32[]{:S(2)}) collective-permute-start(bf16[320,896]{1,0:T(8,128)(2,1)} %get-tuple-element.19), channel_id=1, source_target_pairs={{0,2},{1,3},{2,0},{3,1},{4,6},{5,7},{6,4},{7,5},{8,10},{9,11},{10,... | collective-permute-start | bytes 1720328 | tf_op jit(solution)/shard_map/ppermute | solution.py:54
  13.3 24.2 %all-to-all-start = ((bf16[4,144,256]{2,1,0:T(8,128)(2,1)}), bf16[4,144,256]{2,1,0:T(8,128)(2,1)S(1)}, u32[]{:S(2)}, u32[]{:S(2)}) async-start(bf16[4,144,256]{2,1,0:T(8,128)(2,1)} %pack.1), calls=%async_computation | async-start | bytes 589824 | tf_op jit(solution)/shard_map/all_to_all | solution.py:412
  37.5 13.0 %collective-permute-start.7 = (bf16[320,896]{1,0:T(8,128)(2,1)}, bf16[320,896]{1,0:T(8,128)(2,1)}, u32[]{:S(2)}, u32[]{:S(2)}) collective-permute-start(bf16[320,896]{1,0:T(8,128)(2,1)} %collective-permute-done.refs_3_), channel_id=1, source_target_pairs={{0,1},{1,0},{2,3},{3,2},{4,5},{5,4},{6,7},{7,6},{8,9},{9,8},{10,11... | collective-permute-start | bytes 1720328 | tf_op jit(solution)/shard_map/ppermute | solution.py:54
  39.0 2.6 %collective-permute-start.3 = (bf16[4,144,256]{2,1,0:T(8,128)(2,1)S(1)}, bf16[4,144,256]{2,1,0:T(8,128)(2,1)}, u32[]{:S(2)}, u32[]{:S(2)}) collective-permute-start(bf16[4,144,256]{2,1,0:T(8,128)(2,1)S(1)} %all-to-all-done), channel_id=1, source_target_pairs={{0,4},{4,0},{8,12},{12,8},{16,20},{20,16},{24,28},{28,24},{1,5},{5... | collective-permute-start | bytes 884744 | tf_op jit(solution)/shard_map/ppermute | solution.py:54
  39.2 12.4 %collective-permute-start.5 = (bf16[320,896]{1,0:T(8,128)(2,1)}, bf16[320,896]{1,0:T(8,128)(2,1)S(1)}, u32[]{:S(2)}, u32[]{:S(2)}) collective-permute-start(bf16[320,896]{1,0:T(8,128)(2,1)} %collective-permute-done.4.refs_1_), channel_id=1, source_target_pairs={{0,4},{4,0},{8,12},{12,8},{16,20},{20,16},{24,28},{28,24},{1,5},{5... | collective-permute-start | bytes 1720328 | tf_op jit(solution)/shard_map/ppermute | solution.py:54
  39.7 16.9 %collective-permute-start.8 = (bf16[128,2560]{1,0:T(8,128)(2,1)}, bf16[128,2560]{1,0:T(8,128)(2,1)S(1)}, u32[]{:S(2)}, u32[]{:S(2)}) collective-permute-start(bf16[128,2560]{1,0:T(8,128)(2,1)} %slice.28), channel_id=1, source_target_pairs={{0,16},{4,20},{8,24},{12,28},{16,0},{20,4},{24,8},{28,12},{1,17},{... | collective-permute-start | bytes 1966088 | tf_op jit(solution)/shard_map/ppermute | solution.py:54
  41.3 16.6 %collective-permute-start.9 = (bf16[128,2560]{1,0:T(8,128)(2,1)}, bf16[128,2560]{1,0:T(8,128)(2,1)S(1)}, u32[]{:S(2)}, u32[]{:S(2)}) collective-permute-start(bf16[128,2560]{1,0:T(8,128)(2,1)} %slice.29), channel_id=1, source_target_pairs={{0,8},{4,12},{8,0},{12,4},{16,24},{20,28},{24,16},{28,20},{1,9},{5... | collective-permute-start | bytes 1966088 | tf_op jit(solution)/shard_map/ppermute | solution.py:54
  41.7 9.9 %collective-permute-start.6 = (bf16[320,896]{1,0:T(8,128)(2,1)}, bf16[320,896]{1,0:T(8,128)(2,1)S(1)}, u32[]{:S(2)}, u32[]{:S(2)}) collective-permute-start(bf16[320,896]{1,0:T(8,128)(2,1)} %collective-permute-done.refs_3_), channel_id=1, source_target_pairs={{0,4},{4,0},{8,12},{12,8},{16,20},{20,16},{24,28},{28,24},{1,5},{5... | collective-permute-start | bytes 1720328 | tf_op jit(solution)/shard_map/ppermute | solution.py:54
  50.5 7.4 %collective-permute-start.10 = (bf16[320,896]{1,0:T(8,128)(2,1)}, bf16[320,896]{1,0:T(8,128)(2,1)S(1)}, u32[]{:S(2)}, u32[]{:S(2)}) collective-permute-start(bf16[320,896]{1,0:T(8,128)(2,1)} %collective-permute-done.7.refs_10_), channel_id=1, source_target_pairs={{0,4},{4,0},{8,12},{12,8},{16,20},{20,16},{24,28},{28,24},{1,5},{5... | collective-permute-start | bytes 1720328 | tf_op jit(solution)/shard_map/ppermute | solution.py:54
  51.6 1.3 %copy-start.1 = (bf16[640,896]{1,0:T(8,128)(2,1)S(1)}, bf16[640,896]{1,0:T(8,128)(2,1)}, u32[]{:S(2)}) copy-start(bf16[640,896]{1,0:T(8,128)(2,1)} %get-tuple-element.23.refs_0_) | copy-start | bytes 3440644
  62.8 16.2 %collective-permute-start.13 = (bf16[256,896]{1,0:T(8,128)(2,1)S(1)}, bf16[256,896]{1,0:T(8,128)(2,1)S(1)}, u32[]{:S(2)}, u32[]{:S(2)}) collective-permute-start(bf16[256,896]{1,0:T(8,128)(2,1)S(1)} %get-tuple-element.31), channel_id=1, source_target_pairs={{0,24},{4,28},{8,16},{12,20},{16,8},{20,12},{24,0},{28,4},{1,25},{... | collective-permute-start | bytes 1376264 | tf_op jit(solution)/shard_map/ppermute | solution.py:54
  68.1 6.7 %copy-start = (bf16[256,2560]{1,0:T(8,128)(2,1)S(1)}, bf16[256,2560]{1,0:T(8,128)(2,1)}, u32[]{:S(2)}) copy-start(bf16[256,2560]{1,0:T(8,128)(2,1)} %refs_2_.3) | copy-start | bytes 3932164
  68.1 16.3 %collective-permute-start.11 = (bf16[256,896]{1,0:T(8,128)(2,1)S(1)}, bf16[256,896]{1,0:T(8,128)(2,1)S(1)}, u32[]{:S(2)}, u32[]{:S(2)}) collective-permute-start(bf16[256,896]{1,0:T(8,128)(2,1)S(1)} %heads.5), channel_id=1, source_target_pairs={{0,8},{4,12},{8,0},{12,4},{16,24},{20,28},{24,16},{28,20},{1,9},{5... | collective-permute-start | bytes 1376264 | tf_op jit(solution)/shard_map/ppermute | solution.py:54
  73.2 12.6 %collective-permute-start.12 = (bf16[256,896]{1,0:T(8,128)(2,1)S(1)}, bf16[256,896]{1,0:T(8,128)(2,1)S(1)}, u32[]{:S(2)}, u32[]{:S(2)}) collective-permute-start(bf16[256,896]{1,0:T(8,128)(2,1)S(1)} %heads.6), channel_id=1, source_target_pairs={{0,16},{4,20},{8,24},{12,28},{16,0},{20,4},{24,8},{28,12},{1,17},{... | collective-permute-start | bytes 1376264 | tf_op jit(solution)/shard_map/ppermute | solution.py:54

commit v6 on v5

--- a/solution.py
+++ b/solution.py
@@ -20,7 +20,6 @@
 
 TILES = 2 + GROUP
 WIDTH = TILES * HD
-ORDER = (6, 2, 4, 0)
 MIB = 1024 * 1024
 
 SMEM = pl.BlockSpec(memory_space=pltpu.SMEM)
@@ -148,6 +147,23 @@
     ).astype(jnp.bfloat16)
 
 
+def norm_kernel(gain_ref, *refs):
+    count = len(refs) // 2
+    for token_ref, normed_ref in zip(refs[:count], refs[count:]):
+        normed_ref[...] = normed_rows(token_ref[...], gain_ref[...])
+
+
+def norm(gain, parts):
+    return pl.pallas_call(
+        norm_kernel,
+        out_shape=[jax.ShapeDtypeStruct(part.shape, part.dtype) for part in parts],
+        in_specs=[VMEM] * (1 + len(parts)),
+        out_specs=[VMEM] * len(parts),
+        compiler_params=pltpu.CompilerParams(vmem_limit_bytes=20 * MIB),
+        name="norm",
+    )(gain, *parts)
+
+
 def pack_kernel(team_count, *refs):
     lists_ref, ck_ref, cv_ref, payload_ref = refs
     prefix = ck_ref.shape[0]
@@ -177,7 +193,7 @@
     return value * cosine + pltpu.roll(value, HD // 2, 1) * sine
 
 
-def heads_kernel(far, x_count, piece_count, *refs):
+def heads_kernel(far, first_row, x_count, piece_count, *refs):
     refs = list(refs)
 
     def take(count):
@@ -210,7 +226,10 @@
             return place, pl.ds(0, QBLK)
         return place // blocks_each, pl.ds(pl.multiple_of(place % blocks_each * QBLK, QBLK), QBLK)
 
-    x = [normed_rows(x_ref[...], gain_ref[...]) for x_ref in x_refs]
+    if far == FARS[-1]:
+        x = [normed_rows(x_ref[...], gain_ref[...]) for x_ref in x_refs]
+    else:
+        x = [x_ref[...] for x_ref in x_refs]
     x = jnp.concatenate(x, axis=0) if x_count > 1 else x[0]
     for copy in copies:
         copy.wait()
@@ -224,7 +243,8 @@
 
     lin = jnp.dot(x, w_ref[...], preferred_element_type=jnp.float32) + bias_ref[...]
     low_half = lax.broadcasted_iota(jnp.int32, (rows, HD), 1) < HD // 2
-    table = table_ref[pl.ds(FARS.index(far) * rows, rows), :]
+    all_rows = table_ref.shape[0] // len(FARS)
+    table = table_ref[pl.ds(FARS.index(far) * all_rows + first_row, rows), :]
     swapped = pltpu.roll(table, HD // 2, 1)
     cosine = jnp.where(low_half, table, swapped)
     sine = jnp.where(low_half, -swapped, table)
@@ -246,7 +266,8 @@
         span = pl.ds(block * QBLK, QBLK)
         for head in range(GROUP):
             query = q_buf[span, pl.ds(head * HD, HD)]
-            at = ((group * GROUP + head) * blocks + block) * SEL
+            listed = (group * GROUP + head) * (all_rows // QBLK) + first_row // QBLK + block
+            at = listed * SEL
             slots = [lists_ref[owner_list, at + j] for j in range(SEL)]
             keys = [key_buf[span, :]]
             values = [value_t_buf[:, span]]
@@ -276,7 +297,7 @@
             out_ref[span, pl.ds((2 + head) * HD, HD)] = (mixed / total).T.astype(out_ref.dtype)
 
 
-def heads(far, place, lists, x_parts, gain, bias, table, cache, pieces, kept):
+def heads(far, first_row, place, lists, x_parts, gain, bias, table, cache, pieces, kept):
     depth = x_parts[0].shape[1]
     rows = sum(part.shape[0] for part in x_parts)
     operands = [place, lists, *x_parts, gain, bias, table, cache]
@@ -291,7 +312,7 @@
         specs += [ANY] * len(pieces)
         shapes.append(jax.ShapeDtypeStruct((depth, WIDTH), jnp.bfloat16))
     return pl.pallas_call(
-        functools.partial(heads_kernel, far, len(x_parts), len(pieces)),
+        functools.partial(heads_kernel, far, first_row, len(x_parts), len(pieces)),
         out_shape=shapes,
         in_specs=specs,
         out_specs=[VMEM] * len(shapes),
@@ -308,58 +329,59 @@
     )(*operands)
 
 
-def finish_kernel(fars, place_ref, *refs):
+def finish_kernel(runs, place_ref, *refs):
     context_ref, keys_ref, values_ref = refs[-3:]
-    for far, part in zip(fars, refs):
+    for (far, first_row), part in zip(runs, refs):
+        rows = pl.ds(first_row, part.shape[0])
         sources = tile_sources(place_ref[0] ^ (far // 2))
         for target, (column, tiles, at) in zip((keys_ref, values_ref, context_ref), sources):
-            target[:, pl.ds(pl.multiple_of(column, HD), tiles * HD)] = part[
+            target[rows, pl.ds(pl.multiple_of(column, HD), tiles * HD)] = part[
                 :, pl.ds(at * HD, tiles * HD)
             ].astype(jnp.float32)
 
 
-def finish(place, parts):
-    fars = tuple(parts)
-    rows = parts[fars[0]].shape[0]
-    return pl.pallas_call(
-        functools.partial(finish_kernel, fars),
+def finish(place, rows, parts):
+    return pl.pallas_call(
+        functools.partial(finish_kernel, tuple(parts)),
         out_shape=[
             jax.ShapeDtypeStruct((rows, TEAM * width), jnp.float32)
             for width in (GROUP * HD, HD, HD)
         ],
-        in_specs=[SMEM] + [VMEM] * len(fars),
+        in_specs=[SMEM] + [VMEM] * len(parts),
         out_specs=[VMEM] * 3,
         compiler_params=pltpu.CompilerParams(vmem_limit_bytes=16 * MIB),
         name="finish",
     )(place, *parts.values())
 
 
-def last_kernel(fars, place_ref, *refs):
-    count = len(fars)
+def last_kernel(runs, place_ref, *refs):
+    count = len(runs)
     outs, wides, sem = refs[count + 3 : count + 6], refs[count + 6 : -1], refs[-1]
     copies = []
-    for far, part_ref, wide in zip(fars, refs, wides):
-        wide[...] = part_ref[...].astype(jnp.float32)
+    for (far, first_row), part_ref, wide in zip(runs, refs, wides):
+        rows = pl.ds(first_row, part_ref.shape[0])
         for index, (column, tiles, at) in enumerate(tile_sources(place_ref[0] ^ (far // 2))):
+            span = pl.ds(at * HD, tiles * HD)
+            wide[:, span] = part_ref[:, span].astype(jnp.float32)
             column = pl.ds(pl.multiple_of(column, HD), tiles * HD)
-            copies.append(
-                (wide.at[:, pl.ds(at * HD, tiles * HD)], outs[(1, 2, 0)[index]].at[:, column])
+            copy = pltpu.make_async_copy(
+                wide.at[:, span], outs[(1, 2, 0)[index]].at[rows, column], sem.at[len(copies)]
             )
-    for copy in start_all(copies, sem):
+            copy.start()
+            copies.append(copy)
+    for copy in copies:
         copy.wait()
 
 
 def finish_last(place, parts, outs):
-    fars = tuple(parts)
-    count = len(fars)
-    shape = parts[fars[0]].shape
-    return pl.pallas_call(
-        functools.partial(last_kernel, fars),
+    count = len(parts)
+    return pl.pallas_call(
+        functools.partial(last_kernel, tuple(parts)),
         out_shape=[jax.ShapeDtypeStruct(out.shape, out.dtype) for out in outs],
         in_specs=[SMEM] + [VMEM] * count + [ANY] * 3,
         out_specs=[ANY] * 3,
         input_output_aliases={1 + count + index: index for index in range(3)},
-        scratch_shapes=[pltpu.VMEM(shape, jnp.float32)] * count
+        scratch_shapes=[pltpu.VMEM(part.shape, jnp.float32) for part in parts.values()]
         + [pltpu.SemaphoreType.DMA((3 * count,))],
         compiler_params=pltpu.CompilerParams(vmem_limit_bytes=16 * MIB),
         name="finish_last",
@@ -423,35 +445,44 @@
         ]
     ).astype(jnp.float32)[None, :]
 
+    tokens_6 = [swap(low, "ctx", 4), swap(high, "ctx", 2)]
     held = {0: half}
     for index, bit in enumerate(bits_of(grp_size, 1)):
         for far in sorted(held):
             held[far ^ bit] = swap(held[far], "grp", bit)
         if index == 0:
             held[bit], tables, bias, cache, *_ = tie((held[bit], tables, bias, cache, low, high))
-    pieces = [whole]
-    for far, over in piece_places:
-        pieces.append(swap(held[far], "ctx", 1) if over else held[far])
-
-    tokens_6 = [swap(low, "ctx", 4), swap(high, "ctx", 2)]
     lists = cache[:, cache_keys.shape[0], :].astype(jnp.int32)
     blocks_each = cache_keys.shape[0] // QBLK
     owner = jnp.maximum(lists, 0) // blocks_each
     owner = ((owner ^ me) & 1) * (ctx_size // 2) + owner // 2
     lists = jnp.where(lists < 0, -1, owner * blocks_each + jnp.maximum(lists, 0) % blocks_each)
     cache = jnp.concatenate([cache, swap(cache, "ctx", 1)], axis=0)
-
-    x_parts = {0: [tokens], 2: [tokens_2], 4: [tokens_4], 6: tokens_6}
+    last_far = max(held)
+    normed = norm(norm_gain[None, :], [tokens_2, tokens_4, tokens])
+    held[last_far], *_ = tie((held[last_far], *tokens_6, cache, *normed))
+    pieces = [whole]
+    for far, over in piece_places:
+        pieces.append(swap(held[far], "ctx", 1) if over else held[far])
+
+
     early, late = pieces[:-2], pieces[-2:]
     w_part, cache_value_t = gather(place, tokens.shape[1], cache, early)
-    late[0], x_parts[6] = tie((late[0], tokens_6))
+    late[0], tokens_6 = tie((late[0], tokens_6))
+    runs = {
+        (6, 0): tokens_6,
+        (2, 0): normed[0],
+        (4, 0): normed[1],
+        (0, 0): normed[2],
+    }
     kept, parts = [cache_value_t, w_part], {}
-    for far in ORDER:
+    for (far, first_row), x in runs.items():
         out, *rest = heads(
             far,
+            first_row,
             place,
             lists,
-            x_parts[far],
+            x if far == 6 else [x],
             norm_gain[None, :],
             bias,
             tables,
@@ -461,10 +492,10 @@
         )
         if rest:
             late, kept = [], [cache_value_t, rest[0]]
-        parts[far] = swap(out, "ctx", far) if far else out
-    early, late = ORDER[-1:] + ORDER[:-3], ORDER[-3:-1]
-    outs = finish(place, {far: parts[far] for far in early})
-    return tuple(finish_last(place, {far: parts[far] for far in late}, outs))
+        parts[(far, first_row)] = swap(out, "ctx", far) if far else out
+    first = {run: parts[run] for run in parts if run[0] in (0, 6)}
+    last = {run: parts[run] for run in parts if run[0] in (2, 4)}
+    return tuple(finish_last(place, last, finish(place, rows, first)))
 
 
 def solution(mesh):

time: 88.2 us -> 85.9 us (0.974)
  waiting for transfers between devices: 31.4 us -> 25.7 us
  Pallas kernels: 27.2 us -> 29.1 us
  starting transfers between devices: 20 us -> 21.5 us
    ppermute x14, waiting for transfers between devices: 31.4 us -> 25.7 us  [swap(): return lax.ppermute(value, axis, [(i, i ^ bit) for i in range(size)])]
    pallas_call x6 -> x7, Pallas kernels: 21.7 us -> 23.5 us  [the longest x4 17 us: heads(): pl.pallas_call(functools.partial(heads_kernel, far, first_row, len(x_part...]
    ppermute x14, starting transfers between devices: 16.6 us -> 18 us  [swap(): return lax.ppermute(value, axis, [(i, i ^ bit) for i in range(size)])]
  transfers between devices with their start and end apart: 15 -> 15, of which waited for: 7 -> 7; matrix products, arithmetic and copies ran while one was open for 7% -> 7% of each run, Pallas kernels for 23% -> 25%
where the time goes in v6:
time: 85.9 us; the launch traced here: 85.4 us
  Pallas kernels  29.1 us (34%)
  waiting for transfers between devices  25.7 us (30%)
  starting transfers between devices  21.5 us (25%)
  local copies, waits for them, and re-layouts  5.42 us (6%)
  other arithmetic  1.96 us (2%)
  between operations  1.83 us (2%)
    ppermute x14, waiting for transfers between devices, swap(): return lax.ppermute(value, axis, [(i, i ^ bit) for i in range(size)])  25.7 us
    ppermute x14, starting transfers between devices, swap(): return lax.ppermute(value, axis, [(i, i ^ bit) for i in range(size)])  18 us
    pallas_call x4, Pallas kernels, heads(): pl.pallas_call(functools.partial(heads_kernel, far, first_row, len(x_part...  17 us
    all_to_all x1, starting transfers between devices, on_device(): cache = lax.all_to_all(payload, 'ctx', 0, 0, axis_index_groups=same_core)  3.45 us
    pallas_call x1, Pallas kernels, cut(): pl.pallas_call(cut_kernel, out_shape=[jax.ShapeDtypeStruct((rows, WIDTH),...  2.72 us
    pallas_call x1, Pallas kernels, finish(): pl.pallas_call(functools.partial(finish_kernel, tuple(parts)), out_shape=...  2.52 us
    pallas_call x1, Pallas kernels, norm(): pl.pallas_call(norm_kernel, out_shape=[jax.ShapeDtypeStruct(part.shape, p...  2.2 us
    pallas_call x1, Pallas kernels, gather(): pl.pallas_call(functools.partial(gather_kernel, len(pieces)), out_shape=[...  2.05 us
  transfers between devices with their start and end apart: 15, of which 7 were waited for; matrix products, arithmetic and copies ran while one was open for 7% of the time, Pallas kernels for 25%

profile of v6, /device:TPU:0, one launch (start us, length us, event | category | flops | bytes accessed | tf_op | source)
XLA Modules:
  0.0 85.4 jit_solution(10774965580425202803)
XLA Ops:
  0.7 3.0 %collective-permute-start.1 = (bf16[256,2560]{1,0:T(8,128)(2,1)}, bf16[256,2560]{1,0:T(8,128)(2,1)S(1)}, u32[]{:S(2)}, u32[]{:S(2)}) collective-permute-start(bf16[256,2560]{1,0:T(8,128)(2,1)} %refs_2_.3), channel_id=1, source_target_pairs={{0,8},{4,12},{8,0},{12,4},{16,24},{20,28},{24,16},{28,20},{1,9},{5... | collective-permute-start | bytes 3932168 | tf_op jit(solution)/shard_map/ppermute | solution.py:53
  3.7 1.5 %collective-permute-start.2 = (bf16[256,2560]{1,0:T(8,128)(2,1)}, bf16[256,2560]{1,0:T(8,128)(2,1)S(1)}, u32[]{:S(2)}, u32[]{:S(2)}) collective-permute-start(bf16[256,2560]{1,0:T(8,128)(2,1)} %refs_2_.3), channel_id=1, source_target_pairs={{0,16},{4,20},{8,24},{12,28},{16,0},{20,4},{24,8},{28,12},{1,17},{... | collective-permute-start | bytes 3932168 | tf_op jit(solution)/shard_map/ppermute | solution.py:53
  5.2 2.7 %cut.1 = (bf16[320,896]{1,0:T(8,128)(2,1)}, bf16[640,896]{1,0:T(8,128)(2,1)}) custom-call(bf16[640,512]{1,0:T(8,128)(2,1)} %wk_ref.1, bf16[640,512]{1,0:T(8,128)(2,1)} %wv_ref.1, bf16[640,2560]{1,0:T(8,128)(2,1)} %wq_ref.1), custom_call_target="tpu_custom_call" | custom-call | tf_op jit(solution)/shard_map/cut/pallas_call | solution.py:96
  8.0 1.6 %collective-permute-start.4 = (bf16[320,896]{1,0:T(8,128)(2,1)}, bf16[320,896]{1,0:T(8,128)(2,1)}, u32[]{:S(2)}, u32[]{:S(2)}) collective-permute-start(bf16[320,896]{1,0:T(8,128)(2,1)} %get-tuple-element.23), channel_id=1, source_target_pairs={{0,1},{1,0},{2,3},{3,2},{4,5},{5,4},{6,7},{7,6},{8,9},{9,8},{10,11... | collective-permute-start | bytes 1720328 | tf_op jit(solution)/shard_map/ppermute | solution.py:53
  9.6 2.6 %collective-permute-start = (bf16[320,896]{1,0:T(8,128)(2,1)}, bf16[320,896]{1,0:T(8,128)(2,1)}, u32[]{:S(2)}, u32[]{:S(2)}) collective-permute-start(bf16[320,896]{1,0:T(8,128)(2,1)} %get-tuple-element.23), channel_id=1, source_target_pairs={{0,2},{1,3},{2,0},{3,1},{4,6},{5,7},{6,4},{7,5},{8,10},{9,11},{10,... | collective-permute-start | bytes 1720328 | tf_op jit(solution)/shard_map/ppermute | solution.py:53
  12.5 0.8 pack.1
  13.3 3.5 %all-to-all-start = ((bf16[4,144,256]{2,1,0:T(8,128)(2,1)}), bf16[4,144,256]{2,1,0:T(8,128)(2,1)S(1)}, u32[]{:S(2)}, u32[]{:S(2)}) async-start(bf16[4,144,256]{2,1,0:T(8,128)(2,1)} %pack.1), calls=%async_computation | async-start | bytes 589824 | tf_op jit(solution)/shard_map/all_to_all | solution.py:434
  17.5 1.9 %add_cosine_fusion.refs_6_.refs_5_ = f32[1024,128]{1,0:T(8,128)S(1)} fusion(f32[128]{0:T(128)S(1)} %copy-done.6, f32[1024]{0:T(1024)S(1)} %get-tuple-element.49, f32[128]{0:T(128)S(1)} %copy-done.7, f32[1024]{0:T(1024)S(1)} %get-tuple-element.48, f32[128]{0:T(128)S(1)} %copy-done.8, f32[1024]{0:T(1024)S(1)} %get-tuple-element.43, f32[128]{0:T(128)S(1)} %copy-done.9, ...), kind=kLoop, calls=%fused_computation | loop fusion | flops 1048576 | bytes 543232 | tf_op jit(solution)/shard_map/cos | solution.py:48
  19.4 0.8 dynamic_slice.11
  20.3 13.3 %collective-permute-done.1.refs_0_ = bf16[256,2560]{1,0:T(8,128)(2,1)S(1)} collective-permute-done((bf16[256,2560]{1,0:T(8,128)(2,1)}, bf16[256,2560]{1,0:T(8,128)(2,1)S(1)}, u32[]{:S(2)}, u32[]{:S(2)}) %collective-permute-start.1) | collective-permute-done | bytes 1310752 | tf_op jit(solution)/shard_map/ppermute | solution.py:53
  33.5 0.9 %slice.28 = bf16[128,2560]{1,0:T(8,128)(2,1)} slice(bf16[256,2560]{1,0:T(8,128)(2,1)S(1)} %collective-permute-done.1.refs_0_), slice={[0:128], [0:2560]} | slice | bytes 1310720 | tf_op jit(solution)/shard_map/slice | solution.py:418
  34.4 2.1 %collective-permute-start.8 = (bf16[128,2560]{1,0:T(8,128)(2,1)}, bf16[128,2560]{1,0:T(8,128)(2,1)}, u32[]{:S(2)}, u32[]{:S(2)}) collective-permute-start(bf16[128,2560]{1,0:T(8,128)(2,1)} %slice.28), channel_id=1, source_target_pairs={{0,16},{4,20},{8,24},{12,28},{16,0},{20,4},{24,8},{28,12},{1,17},{... | collective-permute-start | bytes 1966088 | tf_op jit(solution)/shard_map/ppermute | solution.py:53
  36.8 0.9 %slice.29 = bf16[128,2560]{1,0:T(8,128)(2,1)} slice(bf16[256,2560]{1,0:T(8,128)(2,1)S(1)} %collective-permute-done.2.refs_1_), slice={[128:256], [0:2560]} | slice | bytes 1310720 | tf_op jit(solution)/shard_map/slice | solution.py:418
  37.7 1.2 %collective-permute-start.9 = (bf16[128,2560]{1,0:T(8,128)(2,1)}, bf16[128,2560]{1,0:T(8,128)(2,1)}, u32[]{:S(2)}, u32[]{:S(2)}) collective-permute-start(bf16[128,2560]{1,0:T(8,128)(2,1)} %slice.29), channel_id=1, source_target_pairs={{0,8},{4,12},{8,0},{12,4},{16,24},{20,28},{24,16},{28,20},{1,9},{5... | collective-permute-start | bytes 1966088 | tf_op jit(solution)/shard_map/ppermute | solution.py:53
  38.9 1.6 %collective-permute-start.7 = (bf16[320,896]{1,0:T(8,128)(2,1)}, bf16[320,896]{1,0:T(8,128)(2,1)}, u32[]{:S(2)}, u32[]{:S(2)}) collective-permute-start(bf16[320,896]{1,0:T(8,128)(2,1)} %collective-permute-done.refs_3_), channel_id=1, source_target_pairs={{0,1},{1,0},{2,3},{3,2},{4,5},{5,4},{6,7},{7,6},{8,9},{9,8},{10,11... | collective-permute-start | bytes 1720328 | tf_op jit(solution)/shard_map/ppermute | solution.py:53
  40.7 0.6 collective-permute-start.5
  41.2 1.3 %copy-done = bf16[256,2560]{1,0:T(8,128)(2,1)S(1)} copy-done((bf16[256,2560]{1,0:T(8,128)(2,1)S(1)}, bf16[256,2560]{1,0:T(8,128)(2,1)}, u32[]{:S(2)}) %copy-start) | copy-done | bytes 1310744
  42.6 2.2 %norm.1 = (bf16[256,2560]{1,0:T(8,128)(2,1)S(1)}, bf16[256,2560]{1,0:T(8,128)(2,1)S(1)}, bf16[256,2560]{1,0:T(8,128)(2,1)S(1)}) custom-call(bf16[1,2560]{1,0:T(2,128)(2,1)S(1)} %broadcast_in_dim.20.gain_ref.refs_4_.refs_3_, bf16[256,2560]{1,0:T(8,128)(2,1)S(1)} %collective-permute-done.1.refs_0_, bf16[256,2560]{1,0:T(8,128)(2,1)S(1)} %collective-permute-done.2.refs_1_, ...), custom_call_target="tpu_custom_call" | custom-call | tf_op jit(solution)/shard_map/norm/pallas_call | solution.py:157
  44.9 1.1 %constant_dynamic-update-slice_fusion.cache_ref.refs_7_.refs_6_ = bf16[8,144,256]{2,1,0:T(8,128)(2,1)S(1)} fusion(bf16[8,144,256]{2,1,0:T(8,128)(2,1)S(1)} %constant_dynamic-update-slice_fusion.1, bf16[4,144,256]{2,1,0:T(8,128)(2,1)} %collective-permute-done.3), kind=kLoop, calls=%fused_computation.1 | loop fusion | bytes 589824 | tf_op jit(solution)/shard_map/concatenate | solution.py:460
  45.9 5.6 %collective-permute-done.7.refs_10_ = bf16[320,896]{1,0:T(8,128)(2,1)} collective-permute-done((bf16[320,896]{1,0:T(8,128)(2,1)}, bf16[320,896]{1,0:T(8,128)(2,1)}, u32[]{:S(2)}, u32[]{:S(2)}) %collective-permute-start.7) | collective-permute-done | bytes 573472 | tf_op jit(solution)/shard_map/ppermute | solution.py:53
  51.5 0.5 collective-permute-done.9.refs_3_
  52.1 2.0 %gather.1 = (bf16[2560,896]{1,0:T(8,128)(2,1)S(1)}, bf16[8,128,128]{2,1,0:T(8,128)(2,1)S(1)}) custom-call(s32[9]{0:T(128)S(1)} %stack.39.place_ref.refs_0_, bf16[8,144,256]{2,1,0:T(8,128)(2,1)S(1)} %constant_dynamic-update-slice_fusion.cache_ref.refs_7_.refs_6_, bf16[640,896]{1,0:T(8,128)(2,1)S(1)} %copy-done.1, ...), custom_call_target="tpu_custom_call" | custom-call | tf_op jit(solution)/shard_map/gather/pallas_call | solution.py:127
  54.2 5.6 %heads.4 = (bf16[256,896]{1,0:T(8,128)(2,1)S(1)}, bf16[2560,896]{1,0:T(8,128)(2,1)S(1)}) custom-call(s32[9]{0:T(128)S(1)} %stack.39.place_ref.refs_0_, s32[4,256]{1,0:T(4,128)S(1)} %fusion.6.refs_1_, bf16[128,2560]{1,0:T(8,128)(2,1)} %collective-permute-done.8.refs_2_, ...), custom_call_target="tpu_custom_call", output_to_operand_aliasing={{1}: (9, {})} | custom-call | flops 1 | bytes 1 | tf_op jit(solution)/shard_map/heads/pallas_call | solution.py:314
  59.8 1.5 %collective-permute-start.13 = (bf16[256,896]{1,0:T(8,128)(2,1)S(1)}, bf16[256,896]{1,0:T(8,128)(2,1)S(1)}, u32[]{:S(2)}, u32[]{:S(2)}) collective-permute-start(bf16[256,896]{1,0:T(8,128)(2,1)S(1)} %get-tuple-element.39), channel_id=1, source_target_pairs={{0,24},{4,28},{8,16},{12,20},{16,8},{20,12},{24,0},{28,4},{1,25},{... | collective-permute-start | bytes 1376264 | tf_op jit(solution)/shard_map/ppermute | solution.py:53
  61.3 3.8 %heads.5 = bf16[256,896]{1,0:T(8,128)(2,1)S(1)} custom-call(s32[9]{0:T(128)S(1)} %stack.39.place_ref.refs_0_, s32[4,256]{1,0:T(4,128)S(1)} %fusion.6.refs_1_, bf16[256,2560]{1,0:T(8,128)(2,1)S(1)} %get-tuple-element.25.refs_2_, bf16[1,2560]{1,0:T(2,128)(2,1)S(1)} %broadcast_in_dim.20.gain_ref.refs_4_.refs_3_, ...), custom_call_target="tpu_custom_call" | custom-call | flops 1 | bytes 1 | tf_op jit(solution)/shard_map/heads/pallas_call | solution.py:314
  65.1 1.2 %collective-permute-start.11 = (bf16[256,896]{1,0:T(8,128)(2,1)S(1)}, bf16[256,896]{1,0:T(8,128)(2,1)S(1)}, u32[]{:S(2)}, u32[]{:S(2)}) collective-permute-start(bf16[256,896]{1,0:T(8,128)(2,1)S(1)} %heads.5), channel_id=1, source_target_pairs={{0,8},{4,12},{8,0},{12,4},{16,24},{20,28},{24,16},{28,20},{1,9},{5... | collective-permute-start | bytes 1376264 | tf_op jit(solution)/shard_map/ppermute | solution.py:53
  66.3 3.8 %heads.6 = bf16[256,896]{1,0:T(8,128)(2,1)S(1)} custom-call(s32[9]{0:T(128)S(1)} %stack.39.place_ref.refs_0_, s32[4,256]{1,0:T(4,128)S(1)} %fusion.6.refs_1_, bf16[256,2560]{1,0:T(8,128)(2,1)S(1)} %get-tuple-element.31.refs_2_, bf16[1,2560]{1,0:T(2,128)(2,1)S(1)} %broadcast_in_dim.20.gain_ref.refs_4_.refs_3_, ...), custom_call_target="tpu_custom_call" | custom-call | flops 1 | bytes 1 | tf_op jit(solution)/shard_map/heads/pallas_call | solution.py:314
  70.1 1.0 %collective-permute-start.12 = (bf16[256,896]{1,0:T(8,128)(2,1)S(1)}, bf16[256,896]{1,0:T(8,128)(2,1)S(1)}, u32[]{:S(2)}, u32[]{:S(2)}) collective-permute-start(bf16[256,896]{1,0:T(8,128)(2,1)S(1)} %heads.6), channel_id=1, source_target_pairs={{0,16},{4,20},{8,24},{12,28},{16,0},{20,4},{24,8},{28,12},{1,17},{... | collective-permute-start | bytes 1376264 | tf_op jit(solution)/shard_map/ppermute | solution.py:53
  71.1 3.8 %heads.7.refs_1_ = f32[256,896]{1,0:T(8,128)S(1)} custom-call(s32[9]{0:T(128)S(1)} %stack.39.place_ref.refs_0_, s32[4,256]{1,0:T(4,128)S(1)} %fusion.6.refs_1_, bf16[256,2560]{1,0:T(8,128)(2,1)S(1)} %get-tuple-element.32.refs_2_, bf16[1,2560]{1,0:T(2,128)(2,1)S(1)} %broadcast_in_dim.20.gain_ref.refs_4_.refs_3_, ...), custom_call_target="tpu_custom_call" | custom-call | flops 1 | bytes 1 | tf_op jit(solution)/shard_map/heads/pallas_call | solution.py:314
  74.9 2.5 %finish.1 = (f32[256,2560]{1,0:T(8,128)}, f32[256,512]{1,0:T(8,128)}, f32[256,512]{1,0:T(8,128)}) custom-call(s32[9]{0:T(128)S(1)} %stack.39.place_ref.refs_0_, bf16[256,896]{1,0:T(8,128)(2,1)S(1)} %collective-permute-done.13.refs_0_, f32[256,896]{1,0:T(8,128)S(1)} %heads.7.refs_1_), custom_call_target="tpu_custom_call" | custom-call | tf_op jit(solution)/shard_map/finish/pallas_call | solution.py:344
  77.4 5.7 %collective-permute-done.11.refs_0_ = bf16[256,896]{1,0:T(8,128)(2,1)S(1)} collective-permute-done((bf16[256,896]{1,0:T(8,128)(2,1)S(1)}, bf16[256,896]{1,0:T(8,128)(2,1)S(1)}, u32[]{:S(2)}, u32[]{:S(2)}) %collective-permute-start.11) | collective-permute-done | bytes 458784 | tf_op jit(solution)/shard_map/ppermute | solution.py:53
  83.5 1.8 %finish_last.1 = (f32[256,2560]{1,0:T(8,128)}, f32[256,512]{1,0:T(8,128)}, f32[256,512]{1,0:T(8,128)}) custom-call(s32[9]{0:T(128)S(1)} %stack.39.place_ref.refs_0_, bf16[256,896]{1,0:T(8,128)(2,1)S(1)} %collective-permute-done.11.refs_0_, ...), custom_call_target="tpu_custom_call", output_to_operand_aliasing={{0}: (3, {}), {1}: (4, {}), {2}: (5, {})} | custom-call | tf_op jit(solution)/shard_map/finish_last/pallas_call | solution.py:378
  (55 shorter events, 1.5 us)
Async XLA Ops:
  0.6 16.8 %copy-start.6 = (f32[128]{0:T(128)S(1)}, f32[128]{0:T(128)}, u32[]{:S(2)}) copy-start(f32[128]{0:T(128)} %constant.171) | copy-start | bytes 1540
  0.6 16.8 %copy-start.7 = (f32[128]{0:T(128)S(1)}, f32[128]{0:T(128)}, u32[]{:S(2)}) copy-start(f32[128]{0:T(128)} %constant.169) | copy-start | bytes 1540
  0.7 16.8 %copy-start.8 = (f32[128]{0:T(128)S(1)}, f32[128]{0:T(128)}, u32[]{:S(2)}) copy-start(f32[128]{0:T(128)} %constant.167) | copy-start | bytes 1540
  0.7 16.8 %copy-start.9 = (f32[128]{0:T(128)S(1)}, f32[128]{0:T(128)}, u32[]{:S(2)}) copy-start(f32[128]{0:T(128)} %constant.165) | copy-start | bytes 1540
  0.7 11.5 %copy-start.5 = (s32[20,2,4]{0,2,1:T(4,128)S(1)}, s32[20,2,4]{0,2,1:T(4,128)}, u32[]{:S(2)}) copy-start(s32[20,2,4]{0,2,1:T(4,128)} %param.23) | copy-start | bytes 1924
  0.7 11.8 %copy-start.3 = (bf16[128,512]{1,0:T(8,128)(2,1)S(1)}, bf16[128,512]{1,0:T(8,128)(2,1)}, u32[]{:S(2)}) copy-start(bf16[128,512]{1,0:T(8,128)(2,1)} %refs_2_.2) | copy-start | bytes 393220
  0.7 11.8 %copy-start.2 = (bf16[128,512]{1,0:T(8,128)(2,1)S(1)}, bf16[128,512]{1,0:T(8,128)(2,1)}, u32[]{:S(2)}) copy-start(bf16[128,512]{1,0:T(8,128)(2,1)} %refs_1_.1) | copy-start | bytes 393220
  0.7 32.8 %collective-permute-start.1 = (bf16[256,2560]{1,0:T(8,128)(2,1)}, bf16[256,2560]{1,0:T(8,128)(2,1)S(1)}, u32[]{:S(2)}, u32[]{:S(2)}) collective-permute-start(bf16[256,2560]{1,0:T(8,128)(2,1)} %refs_2_.3), channel_id=1, source_target_pairs={{0,8},{4,12},{8,0},{12,4},{16,24},{20,28},{24,16},{28,20},{1,9},{5... | collective-permute-start | bytes 3932168 | tf_op jit(solution)/shard_map/ppermute | solution.py:53
  3.7 33.1 %collective-permute-start.2 = (bf16[256,2560]{1,0:T(8,128)(2,1)}, bf16[256,2560]{1,0:T(8,128)(2,1)S(1)}, u32[]{:S(2)}, u32[]{:S(2)}) collective-permute-start(bf16[256,2560]{1,0:T(8,128)(2,1)} %refs_2_.3), channel_id=1, source_target_pairs={{0,16},{4,20},{8,24},{12,28},{16,0},{20,4},{24,8},{28,12},{1,17},{... | collective-permute-start | bytes 3932168 | tf_op jit(solution)/shard_map/ppermute | solution.py:53
  8.0 12.2 %copy-start.10 = (bf16[512]{0:T(512)(128)(2,1)S(1)}, bf16[512]{0:T(512)(128)(2,1)}, u32[]{:S(2)}) copy-start(bf16[512]{0:T(512)(128)(2,1)} %param.20) | copy-start | bytes 3076
  8.0 12.2 %copy-start.11 = (bf16[512]{0:T(512)(128)(2,1)S(1)}, bf16[512]{0:T(512)(128)(2,1)}, u32[]{:S(2)}) copy-start(bf16[512]{0:T(512)(128)(2,1)} %param.19) | copy-start | bytes 3076
  8.0 32.7 %collective-permute-start.4 = (bf16[320,896]{1,0:T(8,128)(2,1)}, bf16[320,896]{1,0:T(8,128)(2,1)}, u32[]{:S(2)}, u32[]{:S(2)}) collective-permute-start(bf16[320,896]{1,0:T(8,128)(2,1)} %get-tuple-element.23), channel_id=1, source_target_pairs={{0,1},{1,0},{2,3},{3,2},{4,5},{5,4},{6,7},{7,6},{8,9},{9,8},{10,11... | collective-permute-start | bytes 1720328 | tf_op jit(solution)/shard_map/ppermute | solution.py:53
  9.6 29.3 %collective-permute-start = (bf16[320,896]{1,0:T(8,128)(2,1)}, bf16[320,896]{1,0:T(8,128)(2,1)}, u32[]{:S(2)}, u32[]{:S(2)}) collective-permute-start(bf16[320,896]{1,0:T(8,128)(2,1)} %get-tuple-element.23), channel_id=1, source_target_pairs={{0,2},{1,3},{2,0},{3,1},{4,6},{5,7},{6,4},{7,5},{8,10},{9,11},{10,... | collective-permute-start | bytes 1720328 | tf_op jit(solution)/shard_map/ppermute | solution.py:53
  13.3 25.6 %all-to-all-start = ((bf16[4,144,256]{2,1,0:T(8,128)(2,1)}), bf16[4,144,256]{2,1,0:T(8,128)(2,1)S(1)}, u32[]{:S(2)}, u32[]{:S(2)}) async-start(bf16[4,144,256]{2,1,0:T(8,128)(2,1)} %pack.1), calls=%async_computation | async-start | bytes 589824 | tf_op jit(solution)/shard_map/all_to_all | solution.py:434
  20.3 20.3 %copy-start.4 = (bf16[2560]{0:T(1024)(128)(2,1)S(1)}, bf16[2560]{0:T(1024)(128)(2,1)}, u32[]{:S(2)}) copy-start(bf16[2560]{0:T(1024)(128)(2,1)} %param.14) | copy-start | bytes 15364
  34.4 17.1 %collective-permute-start.8 = (bf16[128,2560]{1,0:T(8,128)(2,1)}, bf16[128,2560]{1,0:T(8,128)(2,1)}, u32[]{:S(2)}, u32[]{:S(2)}) collective-permute-start(bf16[128,2560]{1,0:T(8,128)(2,1)} %slice.28), channel_id=1, source_target_pairs={{0,16},{4,20},{8,24},{12,28},{16,0},{20,4},{24,8},{28,12},{1,17},{... | collective-permute-start | bytes 1966088 | tf_op jit(solution)/shard_map/ppermute | solution.py:53
  37.7 14.3 %collective-permute-start.9 = (bf16[128,2560]{1,0:T(8,128)(2,1)}, bf16[128,2560]{1,0:T(8,128)(2,1)}, u32[]{:S(2)}, u32[]{:S(2)}) collective-permute-start(bf16[128,2560]{1,0:T(8,128)(2,1)} %slice.29), channel_id=1, source_target_pairs={{0,8},{4,12},{8,0},{12,4},{16,24},{20,28},{24,16},{28,20},{1,9},{5... | collective-permute-start | bytes 1966088 | tf_op jit(solution)/shard_map/ppermute | solution.py:53
  38.9 12.6 %collective-permute-start.7 = (bf16[320,896]{1,0:T(8,128)(2,1)}, bf16[320,896]{1,0:T(8,128)(2,1)}, u32[]{:S(2)}, u32[]{:S(2)}) collective-permute-start(bf16[320,896]{1,0:T(8,128)(2,1)} %collective-permute-done.refs_3_), channel_id=1, source_target_pairs={{0,1},{1,0},{2,3},{3,2},{4,5},{5,4},{6,7},{7,6},{8,9},{9,8},{10,11... | collective-permute-start | bytes 1720328 | tf_op jit(solution)/shard_map/ppermute | solution.py:53
  40.5 4.2 %collective-permute-start.3 = (bf16[4,144,256]{2,1,0:T(8,128)(2,1)S(1)}, bf16[4,144,256]{2,1,0:T(8,128)(2,1)}, u32[]{:S(2)}, u32[]{:S(2)}) collective-permute-start(bf16[4,144,256]{2,1,0:T(8,128)(2,1)S(1)} %all-to-all-done), channel_id=1, source_target_pairs={{0,4},{4,0},{8,12},{12,8},{16,20},{20,16},{24,28},{28,24},{1,5},{5... | collective-permute-start | bytes 884744 | tf_op jit(solution)/shard_map/ppermute | solution.py:53
  40.7 11.4 %collective-permute-start.5 = (bf16[320,896]{1,0:T(8,128)(2,1)}, bf16[320,896]{1,0:T(8,128)(2,1)S(1)}, u32[]{:S(2)}, u32[]{:S(2)}) collective-permute-start(bf16[320,896]{1,0:T(8,128)(2,1)} %collective-permute-done.4.refs_1_), channel_id=1, source_target_pairs={{0,4},{4,0},{8,12},{12,8},{16,20},{20,16},{24,28},{28,24},{1,5},{5... | collective-permute-start | bytes 1720328 | tf_op jit(solution)/shard_map/ppermute | solution.py:53
  41.2 1.3 %copy-start = (bf16[256,2560]{1,0:T(8,128)(2,1)S(1)}, bf16[256,2560]{1,0:T(8,128)(2,1)}, u32[]{:S(2)}) copy-start(bf16[256,2560]{1,0:T(8,128)(2,1)} %refs_2_.3) | copy-start | bytes 3932164
  44.8 7.3 %copy-start.1 = (bf16[640,896]{1,0:T(8,128)(2,1)S(1)}, bf16[640,896]{1,0:T(8,128)(2,1)}, u32[]{:S(2)}) copy-start(bf16[640,896]{1,0:T(8,128)(2,1)} %get-tuple-element.28.refs_0_) | copy-start | bytes 3440644
  44.8 7.3 %collective-permute-start.6 = (bf16[320,896]{1,0:T(8,128)(2,1)}, bf16[320,896]{1,0:T(8,128)(2,1)S(1)}, u32[]{:S(2)}, u32[]{:S(2)}) collective-permute-start(bf16[320,896]{1,0:T(8,128)(2,1)} %collective-permute-done.refs_3_), channel_id=1, source_target_pairs={{0,4},{4,0},{8,12},{12,8},{16,20},{20,16},{24,28},{28,24},{1,5},{5... | collective-permute-start | bytes 1720328 | tf_op jit(solution)/shard_map/ppermute | solution.py:53
  52.0 2.2 %collective-permute-start.10 = (bf16[320,896]{1,0:T(8,128)(2,1)}, bf16[320,896]{1,0:T(8,128)(2,1)S(1)}, u32[]{:S(2)}, u32[]{:S(2)}) collective-permute-start(bf16[320,896]{1,0:T(8,128)(2,1)} %collective-permute-done.7.refs_10_), channel_id=1, source_target_pairs={{0,4},{4,0},{8,12},{12,8},{16,20},{20,16},{24,28},{28,24},{1,5},{5... | collective-permute-start | bytes 1720328 | tf_op jit(solution)/shard_map/ppermute | solution.py:53
  59.8 15.1 %collective-permute-start.13 = (bf16[256,896]{1,0:T(8,128)(2,1)S(1)}, bf16[256,896]{1,0:T(8,128)(2,1)S(1)}, u32[]{:S(2)}, u32[]{:S(2)}) collective-permute-start(bf16[256,896]{1,0:T(8,128)(2,1)S(1)} %get-tuple-element.39), channel_id=1, source_target_pairs={{0,24},{4,28},{8,16},{12,20},{16,8},{20,12},{24,0},{28,4},{1,25},{... | collective-permute-start | bytes 1376264 | tf_op jit(solution)/shard_map/ppermute | solution.py:53
  65.1 18.0 %collective-permute-start.11 = (bf16[256,896]{1,0:T(8,128)(2,1)S(1)}, bf16[256,896]{1,0:T(8,128)(2,1)S(1)}, u32[]{:S(2)}, u32[]{:S(2)}) collective-permute-start(bf16[256,896]{1,0:T(8,128)(2,1)S(1)} %heads.5), channel_id=1, source_target_pairs={{0,8},{4,12},{8,0},{12,4},{16,24},{20,28},{24,16},{28,20},{1,9},{5... | collective-permute-start | bytes 1376264 | tf_op jit(solution)/shard_map/ppermute | solution.py:53
  70.1 13.4 %collective-permute-start.12 = (bf16[256,896]{1,0:T(8,128)(2,1)S(1)}, bf16[256,896]{1,0:T(8,128)(2,1)S(1)}, u32[]{:S(2)}, u32[]{:S(2)}) collective-permute-start(bf16[256,896]{1,0:T(8,128)(2,1)S(1)} %heads.6), channel_id=1, source_target_pairs={{0,16},{4,20},{8,24},{12,28},{16,0},{20,4},{24,8},{28,12},{1,17},{... | collective-permute-start | bytes 1376264 | tf_op jit(solution)/shard_map/ppermute | solution.py:53

commit v7 on v6

--- a/solution.py
+++ b/solution.py
@@ -106,10 +106,14 @@
     )(*weights)
 
 
-def gather_kernel(count, place_ref, cache_ref, *refs):
+def gather_kernel(count, place_ref, cache_ref, gain_ref, *refs):
     piece_refs = refs[:count]
-    w_ref, cache_value_t_ref, sem = refs[count:]
-    copies = []
+    x_refs = refs[count:-5]
+    w_ref, cache_value_t_ref, normed_ref, x_buf, sem = refs[-5:]
+    copies, first_row = [], 0
+    for x_ref in x_refs:
+        copies.append((x_ref, x_buf.at[pl.ds(first_row, x_ref.shape[0]), :]))
+        first_row += x_ref.shape[0]
     for index, piece in enumerate(piece_refs):
         start = pl.multiple_of(place_ref[1 + index], 16)
         copies.append((piece, w_ref.at[pl.ds(start, piece.shape[0]), :]))
@@ -118,24 +122,33 @@
     for place in range(blocks_each * cache_ref.shape[0]):
         part = pl.ds(place % blocks_each * QBLK, QBLK)
         cache_value_t_ref[place] = cache_ref[place // blocks_each, part, pl.ds(HD, HD)].T
-    for copy in copies:
+    for copy in copies[: len(x_refs)]:
         copy.wait()
-
-
-def gather(place, depth, cache, pieces):
+    normed_ref[...] = normed_rows(x_buf[...], gain_ref[...])
+    for copy in copies[len(x_refs) :]:
+        copy.wait()
+
+
+def gather(place, gain, cache, pieces, x_parts):
+    depth = x_parts[0].shape[1]
+    rows = sum(part.shape[0] for part in x_parts)
     total_blocks = cache.shape[0] * (cache.shape[1] - NOTE_ROWS) // QBLK
     return pl.pallas_call(
         functools.partial(gather_kernel, len(pieces)),
         out_shape=[
             jax.ShapeDtypeStruct((depth, WIDTH), jnp.bfloat16),
             jax.ShapeDtypeStruct((total_blocks, HD, QBLK), jnp.bfloat16),
+            jax.ShapeDtypeStruct((rows, depth), jnp.bfloat16),
         ],
-        in_specs=[SMEM, VMEM] + [ANY] * len(pieces),
-        out_specs=[VMEM] * 2,
-        scratch_shapes=[pltpu.SemaphoreType.DMA((len(pieces),))],
+        in_specs=[SMEM, VMEM, VMEM] + [ANY] * (len(pieces) + len(x_parts)),
+        out_specs=[VMEM] * 3,
+        scratch_shapes=[
+            pltpu.VMEM((rows, depth), jnp.bfloat16),
+            pltpu.SemaphoreType.DMA((len(pieces) + len(x_parts),)),
+        ],
         compiler_params=pltpu.CompilerParams(vmem_limit_bytes=16 * MIB),
         name="gather",
-    )(place, cache, *pieces)
+    )(place, cache, gain, *pieces, *x_parts)
 
 
 def normed_rows(tokens, gain):
@@ -226,14 +239,6 @@
             return place, pl.ds(0, QBLK)
         return place // blocks_each, pl.ds(pl.multiple_of(place % blocks_each * QBLK, QBLK), QBLK)
 
-    if far == FARS[-1]:
-        x = [normed_rows(x_ref[...], gain_ref[...]) for x_ref in x_refs]
-    else:
-        x = [x_ref[...] for x_ref in x_refs]
-    x = jnp.concatenate(x, axis=0) if x_count > 1 else x[0]
-    for copy in copies:
-        copy.wait()
-
     factor = HD ** (-0.5) * float(np.log2(np.e))
     causal = lax.broadcasted_iota(jnp.int32, (QBLK, QBLK), 0) <= lax.broadcasted_iota(
         jnp.int32, (QBLK, QBLK), 1
@@ -241,7 +246,24 @@
     contract_last = (((1,), (1,)), ((), ()))
     blocks = rows // QBLK
 
-    lin = jnp.dot(x, w_ref[...], preferred_element_type=jnp.float32) + bias_ref[...]
+    (x_ref,) = x_refs
+    others = (place_ref.shape[0] - 3) // 2
+    shard = x_ref.shape[1] // (others + 1)
+    if piece_count and shard % HD == 0:
+        pairs = [(place_ref[2 + 2 * i], place_ref[3 + 2 * i]) for i in range(others)]
+        starts = [place_ref[1]] + [jnp.minimum(*pair) for pair in pairs]
+        lin = bias_ref[...]
+        for index, start in enumerate(starts):
+            if index == others:
+                for copy in copies:
+                    copy.wait()
+            run = pl.ds(pl.multiple_of(start, HD), shard)
+            lin = lin + jnp.dot(x_ref[:, run], w_ref[run, :], preferred_element_type=jnp.float32)
+    else:
+        for copy in copies:
+            copy.wait()
+        lin = jnp.dot(x_ref[...], w_ref[...], preferred_element_type=jnp.float32)
+        lin = lin + bias_ref[...]
     low_half = lax.broadcasted_iota(jnp.int32, (rows, HD), 1) < HD // 2
     all_rows = table_ref.shape[0] // len(FARS)
     table = table_ref[pl.ds(FARS.index(far) * all_rows + first_row, rows), :]
@@ -467,10 +489,12 @@
 
 
     early, late = pieces[:-2], pieces[-2:]
-    w_part, cache_value_t = gather(place, tokens.shape[1], cache, early)
+    w_part, cache_value_t, normed_6 = gather(
+        place, norm_gain[None, :], cache, early, tokens_6
+    )
     late[0], tokens_6 = tie((late[0], tokens_6))
     runs = {
-        (6, 0): tokens_6,
+        (6, 0): normed_6,
         (2, 0): normed[0],
         (4, 0): normed[1],
         (0, 0): normed[2],
@@ -482,7 +506,7 @@
             first_row,
             place,
             lists,
-            x if far == 6 else [x],
+            [x],
             norm_gain[None, :],
             bias,
             tables,

time: 85.9 us -> 85.3 us (level)
    pallas_call x4, Pallas kernels: 17 us -> 15.9 us  [heads(): pl.pallas_call(functools.partial(heads_kernel, far, first_row, len(x_part...]
  transfers between devices with their start and end apart: 15 -> 15, of which waited for: 7 -> 6; matrix products, arithmetic and copies ran while one was open for 7% -> 7% of each run, Pallas kernels for 25% -> 26%
where the time goes in v7:
time: 85.3 us; the launch traced here: 84.9 us
  Pallas kernels  28.5 us (33%)
  waiting for transfers between devices  25.7 us (30%)
  starting transfers between devices  21.5 us (25%)
  local copies, waits for them, and re-layouts  5.42 us (6%)
  other arithmetic  1.96 us (2%)
  between operations  1.84 us (2%)
    ppermute x14, waiting for transfers between devices, swap(): return lax.ppermute(value, axis, [(i, i ^ bit) for i in range(size)])  25.7 us
    ppermute x14, starting transfers between devices, swap(): return lax.ppermute(value, axis, [(i, i ^ bit) for i in range(size)])  18 us
    pallas_call x4, Pallas kernels, heads(): pl.pallas_call(functools.partial(heads_kernel, far, first_row, len(x_part...  15.9 us
    all_to_all x1, starting transfers between devices, on_device(): cache = lax.all_to_all(payload, 'ctx', 0, 0, axis_index_groups=same_core)  3.45 us
    pallas_call x1, Pallas kernels, cut(): pl.pallas_call(cut_kernel, out_shape=[jax.ShapeDtypeStruct((rows, WIDTH),...  2.72 us
    pallas_call x1, Pallas kernels, gather(): pl.pallas_call(functools.partial(gather_kernel, len(pieces)), out_shape=[...  2.62 us
    pallas_call x1, Pallas kernels, finish(): pl.pallas_call(functools.partial(finish_kernel, tuple(parts)), out_shape=...  2.52 us
    pallas_call x1, Pallas kernels, norm(): pl.pallas_call(norm_kernel, out_shape=[jax.ShapeDtypeStruct(part.shape, p...  2.2 us
  transfers between devices with their start and end apart: 15, of which 6 were waited for; matrix products, arithmetic and copies ran while one was open for 7% of the time, Pallas kernels for 26%

profile of v7, /device:TPU:0, one launch (start us, length us, event | category | flops | bytes accessed | tf_op | source)
XLA Modules:
  0.0 84.9 jit_solution(11955319612222136483)
XLA Ops:
  0.7 3.0 %collective-permute-start.1 = (bf16[256,2560]{1,0:T(8,128)(2,1)}, bf16[256,2560]{1,0:T(8,128)(2,1)S(1)}, u32[]{:S(2)}, u32[]{:S(2)}) collective-permute-start(bf16[256,2560]{1,0:T(8,128)(2,1)} %refs_2_.3), channel_id=1, source_target_pairs={{0,8},{4,12},{8,0},{12,4},{16,24},{20,28},{24,16},{28,20},{1,9},{5... | collective-permute-start | bytes 3932168 | tf_op jit(solution)/shard_map/ppermute | solution.py:53
  3.7 1.5 %collective-permute-start.2 = (bf16[256,2560]{1,0:T(8,128)(2,1)}, bf16[256,2560]{1,0:T(8,128)(2,1)S(1)}, u32[]{:S(2)}, u32[]{:S(2)}) collective-permute-start(bf16[256,2560]{1,0:T(8,128)(2,1)} %refs_2_.3), channel_id=1, source_target_pairs={{0,16},{4,20},{8,24},{12,28},{16,0},{20,4},{24,8},{28,12},{1,17},{... | collective-permute-start | bytes 3932168 | tf_op jit(solution)/shard_map/ppermute | solution.py:53
  5.2 2.7 %cut.1 = (bf16[320,896]{1,0:T(8,128)(2,1)}, bf16[640,896]{1,0:T(8,128)(2,1)}) custom-call(bf16[640,512]{1,0:T(8,128)(2,1)} %wk_ref.1, bf16[640,512]{1,0:T(8,128)(2,1)} %wv_ref.1, bf16[640,2560]{1,0:T(8,128)(2,1)} %wq_ref.1), custom_call_target="tpu_custom_call" | custom-call | tf_op jit(solution)/shard_map/cut/pallas_call | solution.py:96
  8.0 1.6 %collective-permute-start.4 = (bf16[320,896]{1,0:T(8,128)(2,1)}, bf16[320,896]{1,0:T(8,128)(2,1)}, u32[]{:S(2)}, u32[]{:S(2)}) collective-permute-start(bf16[320,896]{1,0:T(8,128)(2,1)} %get-tuple-element.22), channel_id=1, source_target_pairs={{0,1},{1,0},{2,3},{3,2},{4,5},{5,4},{6,7},{7,6},{8,9},{9,8},{10,11... | collective-permute-start | bytes 1720328 | tf_op jit(solution)/shard_map/ppermute | solution.py:53
  9.6 2.6 %collective-permute-start = (bf16[320,896]{1,0:T(8,128)(2,1)}, bf16[320,896]{1,0:T(8,128)(2,1)}, u32[]{:S(2)}, u32[]{:S(2)}) collective-permute-start(bf16[320,896]{1,0:T(8,128)(2,1)} %get-tuple-element.22), channel_id=1, source_target_pairs={{0,2},{1,3},{2,0},{3,1},{4,6},{5,7},{6,4},{7,5},{8,10},{9,11},{10,... | collective-permute-start | bytes 1720328 | tf_op jit(solution)/shard_map/ppermute | solution.py:53
  12.5 0.8 pack.1
  13.3 3.5 %all-to-all-start = ((bf16[4,144,256]{2,1,0:T(8,128)(2,1)}), bf16[4,144,256]{2,1,0:T(8,128)(2,1)S(1)}, u32[]{:S(2)}, u32[]{:S(2)}) async-start(bf16[4,144,256]{2,1,0:T(8,128)(2,1)} %pack.1), calls=%async_computation | async-start | bytes 589824 | tf_op jit(solution)/shard_map/all_to_all | solution.py:456
  17.5 1.9 %add_cosine_fusion.refs_5_ = f32[1024,128]{1,0:T(8,128)S(1)} fusion(f32[128]{0:T(128)S(1)} %copy-done.6, f32[1024]{0:T(1024)S(1)} %get-tuple-element.47, f32[128]{0:T(128)S(1)} %copy-done.7, f32[1024]{0:T(1024)S(1)} %get-tuple-element.46, f32[128]{0:T(128)S(1)} %copy-done.8, f32[1024]{0:T(1024)S(1)} %get-tuple-element.41, f32[128]{0:T(128)S(1)} %copy-done.9, ...), kind=kLoop, calls=%fused_computation | loop fusion | flops 1048576 | bytes 543232 | tf_op jit(solution)/shard_map/cos | solution.py:48
  19.4 0.8 dynamic_slice.11
  20.3 13.3 %collective-permute-done.1.refs_0_ = bf16[256,2560]{1,0:T(8,128)(2,1)S(1)} collective-permute-done((bf16[256,2560]{1,0:T(8,128)(2,1)}, bf16[256,2560]{1,0:T(8,128)(2,1)S(1)}, u32[]{:S(2)}, u32[]{:S(2)}) %collective-permute-start.1) | collective-permute-done | bytes 1310752 | tf_op jit(solution)/shard_map/ppermute | solution.py:53
  33.5 0.9 %slice.28 = bf16[128,2560]{1,0:T(8,128)(2,1)} slice(bf16[256,2560]{1,0:T(8,128)(2,1)S(1)} %collective-permute-done.1.refs_0_), slice={[0:128], [0:2560]} | slice | bytes 1310720 | tf_op jit(solution)/shard_map/slice | solution.py:440
  34.4 2.1 %collective-permute-start.7 = (bf16[128,2560]{1,0:T(8,128)(2,1)}, bf16[128,2560]{1,0:T(8,128)(2,1)}, u32[]{:S(2)}, u32[]{:S(2)}) collective-permute-start(bf16[128,2560]{1,0:T(8,128)(2,1)} %slice.28), channel_id=1, source_target_pairs={{0,16},{4,20},{8,24},{12,28},{16,0},{20,4},{24,8},{28,12},{1,17},{... | collective-permute-start | bytes 1966088 | tf_op jit(solution)/shard_map/ppermute | solution.py:53
  36.8 0.9 %slice.29 = bf16[128,2560]{1,0:T(8,128)(2,1)} slice(bf16[256,2560]{1,0:T(8,128)(2,1)S(1)} %collective-permute-done.2.refs_1_), slice={[128:256], [0:2560]} | slice | bytes 1310720 | tf_op jit(solution)/shard_map/slice | solution.py:440
  37.7 1.2 %collective-permute-start.8 = (bf16[128,2560]{1,0:T(8,128)(2,1)}, bf16[128,2560]{1,0:T(8,128)(2,1)}, u32[]{:S(2)}, u32[]{:S(2)}) collective-permute-start(bf16[128,2560]{1,0:T(8,128)(2,1)} %slice.29), channel_id=1, source_target_pairs={{0,8},{4,12},{8,0},{12,4},{16,24},{20,28},{24,16},{28,20},{1,9},{5... | collective-permute-start | bytes 1966088 | tf_op jit(solution)/shard_map/ppermute | solution.py:53
  38.9 1.6 %collective-permute-start.9 = (bf16[320,896]{1,0:T(8,128)(2,1)}, bf16[320,896]{1,0:T(8,128)(2,1)}, u32[]{:S(2)}, u32[]{:S(2)}) collective-permute-start(bf16[320,896]{1,0:T(8,128)(2,1)} %collective-permute-done.refs_3_), channel_id=1, source_target_pairs={{0,1},{1,0},{2,3},{3,2},{4,5},{5,4},{6,7},{7,6},{8,9},{9,8},{10,11... | collective-permute-start | bytes 1720328 | tf_op jit(solution)/shard_map/ppermute | solution.py:53
  40.7 0.6 collective-permute-start.5
  41.2 1.3 %copy-done = bf16[256,2560]{1,0:T(8,128)(2,1)S(1)} copy-done((bf16[256,2560]{1,0:T(8,128)(2,1)S(1)}, bf16[256,2560]{1,0:T(8,128)(2,1)}, u32[]{:S(2)}) %copy-start) | copy-done | bytes 1310744
  42.6 2.2 %norm.1 = (bf16[256,2560]{1,0:T(8,128)(2,1)S(1)}, bf16[256,2560]{1,0:T(8,128)(2,1)S(1)}, bf16[256,2560]{1,0:T(8,128)(2,1)S(1)}) custom-call(bf16[1,2560]{1,0:T(2,128)(2,1)S(1)} %broadcast_in_dim.20.gain_ref.refs_3_, bf16[256,2560]{1,0:T(8,128)(2,1)S(1)} %collective-permute-done.1.refs_0_, bf16[256,2560]{1,0:T(8,128)(2,1)S(1)} %collective-permute-done.2.refs_1_, ...), custom_call_target="tpu_custom_call" | custom-call | tf_op jit(solution)/shard_map/norm/pallas_call | solution.py:170
  44.9 1.1 %constant_dynamic-update-slice_fusion.cache_ref.refs_6_ = bf16[8,144,256]{2,1,0:T(8,128)(2,1)S(1)} fusion(bf16[8,144,256]{2,1,0:T(8,128)(2,1)S(1)} %constant_dynamic-update-slice_fusion.1, bf16[4,144,256]{2,1,0:T(8,128)(2,1)} %collective-permute-done.3), kind=kLoop, calls=%fused_computation.1 | loop fusion | bytes 589824 | tf_op jit(solution)/shard_map/concatenate | solution.py:482
  45.9 5.6 %collective-permute-done.9.refs_9_ = bf16[320,896]{1,0:T(8,128)(2,1)} collective-permute-done((bf16[320,896]{1,0:T(8,128)(2,1)}, bf16[320,896]{1,0:T(8,128)(2,1)}, u32[]{:S(2)}, u32[]{:S(2)}) %collective-permute-start.9) | collective-permute-done | bytes 573472 | tf_op jit(solution)/shard_map/ppermute | solution.py:53
  51.5 0.5 collective-permute-done.8.refs_6_
  52.1 2.6 %gather.1 = (bf16[2560,896]{1,0:T(8,128)(2,1)S(1)}, bf16[8,128,128]{2,1,0:T(8,128)(2,1)S(1)}, bf16[256,2560]{1,0:T(8,128)(2,1)S(1)}) custom-call(s32[9]{0:T(128)S(1)} %stack.39.place_ref.refs_0_, bf16[8,144,256]{2,1,0:T(8,128)(2,1)S(1)} %constant_dynamic-update-slice_fusion.cache_ref.refs_6_, bf16[1,2560]{1,0:T(2,128)(2,1)S(1)} %broadcast_in_dim.20.gain_ref.refs_3_, ...), custom_call_target="tpu_custom_call" | custom-call | tf_op jit(solution)/shard_map/gather/pallas_call | solution.py:136
  54.7 4.5 %heads.4 = (bf16[256,896]{1,0:T(8,128)(2,1)S(1)}, bf16[2560,896]{1,0:T(8,128)(2,1)S(1)}) custom-call(s32[9]{0:T(128)S(1)} %stack.39.place_ref.refs_0_, s32[4,256]{1,0:T(4,128)S(1)} %fusion.6.refs_1_, bf16[256,2560]{1,0:T(8,128)(2,1)S(1)} %get-tuple-element.30.refs_2_, ...), custom_call_target="tpu_custom_call", output_to_operand_aliasing={{1}: (8, {})} | custom-call | flops 1 | bytes 1 | tf_op jit(solution)/shard_map/heads/pallas_call | solution.py:336
  59.2 1.5 %collective-permute-start.13 = (bf16[256,896]{1,0:T(8,128)(2,1)S(1)}, bf16[256,896]{1,0:T(8,128)(2,1)S(1)}, u32[]{:S(2)}, u32[]{:S(2)}) collective-permute-start(bf16[256,896]{1,0:T(8,128)(2,1)S(1)} %get-tuple-element.37), channel_id=1, source_target_pairs={{0,24},{4,28},{8,16},{12,20},{16,8},{20,12},{24,0},{28,4},{1,25},{... | collective-permute-start | bytes 1376264 | tf_op jit(solution)/shard_map/ppermute | solution.py:53
  60.7 3.8 %heads.5 = bf16[256,896]{1,0:T(8,128)(2,1)S(1)} custom-call(s32[9]{0:T(128)S(1)} %stack.39.place_ref.refs_0_, s32[4,256]{1,0:T(4,128)S(1)} %fusion.6.refs_1_, bf16[256,2560]{1,0:T(8,128)(2,1)S(1)} %get-tuple-element.24.refs_2_, bf16[1,2560]{1,0:T(2,128)(2,1)S(1)} %broadcast_in_dim.20.gain_ref.refs_3_, f32[1,896]{1,0:T(1,128)S(1)} %maximum_convert_fusion.refs_4_, ...), custom_call_target="tpu_custom_call" | custom-call | flops 1 | bytes 1 | tf_op jit(solution)/shard_map/heads/pallas_call | solution.py:336
  64.5 1.2 %collective-permute-start.11 = (bf16[256,896]{1,0:T(8,128)(2,1)S(1)}, bf16[256,896]{1,0:T(8,128)(2,1)S(1)}, u32[]{:S(2)}, u32[]{:S(2)}) collective-permute-start(bf16[256,896]{1,0:T(8,128)(2,1)S(1)} %heads.5), channel_id=1, source_target_pairs={{0,8},{4,12},{8,0},{12,4},{16,24},{20,28},{24,16},{28,20},{1,9},{5... | collective-permute-start | bytes 1376264 | tf_op jit(solution)/shard_map/ppermute | solution.py:53
  65.7 3.8 %heads.6 = bf16[256,896]{1,0:T(8,128)(2,1)S(1)} custom-call(s32[9]{0:T(128)S(1)} %stack.39.place_ref.refs_0_, s32[4,256]{1,0:T(4,128)S(1)} %fusion.6.refs_1_, bf16[256,2560]{1,0:T(8,128)(2,1)S(1)} %get-tuple-element.32.refs_2_, bf16[1,2560]{1,0:T(2,128)(2,1)S(1)} %broadcast_in_dim.20.gain_ref.refs_3_, f32[1,896]{1,0:T(1,128)S(1)} %maximum_convert_fusion.refs_4_, ...), custom_call_target="tpu_custom_call" | custom-call | flops 1 | bytes 1 | tf_op jit(solution)/shard_map/heads/pallas_call | solution.py:336
  69.5 1.0 %collective-permute-start.12 = (bf16[256,896]{1,0:T(8,128)(2,1)S(1)}, bf16[256,896]{1,0:T(8,128)(2,1)S(1)}, u32[]{:S(2)}, u32[]{:S(2)}) collective-permute-start(bf16[256,896]{1,0:T(8,128)(2,1)S(1)} %heads.6), channel_id=1, source_target_pairs={{0,16},{4,20},{8,24},{12,28},{16,0},{20,4},{24,8},{28,12},{1,17},{... | collective-permute-start | bytes 1376264 | tf_op jit(solution)/shard_map/ppermute | solution.py:53
  70.5 3.8 %heads.7.refs_1_ = f32[256,896]{1,0:T(8,128)S(1)} custom-call(s32[9]{0:T(128)S(1)} %stack.39.place_ref.refs_0_, s32[4,256]{1,0:T(4,128)S(1)} %fusion.6.refs_1_, bf16[256,2560]{1,0:T(8,128)(2,1)S(1)} %get-tuple-element.33.refs_2_, bf16[1,2560]{1,0:T(2,128)(2,1)S(1)} %broadcast_in_dim.20.gain_ref.refs_3_, f32[1,896]{1,0:T(1,128)S(1)} %maximum_convert_fusion.refs_4_, ...), custom_call_target="tpu_custom_call" | custom-call | flops 1 | bytes 1 | tf_op jit(solution)/shard_map/heads/pallas_call | solution.py:336
  74.3 2.5 %finish.1 = (f32[256,2560]{1,0:T(8,128)}, f32[256,512]{1,0:T(8,128)}, f32[256,512]{1,0:T(8,128)}) custom-call(s32[9]{0:T(128)S(1)} %stack.39.place_ref.refs_0_, bf16[256,896]{1,0:T(8,128)(2,1)S(1)} %collective-permute-done.13.refs_0_, f32[256,896]{1,0:T(8,128)S(1)} %heads.7.refs_1_), custom_call_target="tpu_custom_call" | custom-call | tf_op jit(solution)/shard_map/finish/pallas_call | solution.py:366
  76.9 5.7 %collective-permute-done.11.refs_0_ = bf16[256,896]{1,0:T(8,128)(2,1)S(1)} collective-permute-done((bf16[256,896]{1,0:T(8,128)(2,1)S(1)}, bf16[256,896]{1,0:T(8,128)(2,1)S(1)}, u32[]{:S(2)}, u32[]{:S(2)}) %collective-permute-start.11) | collective-permute-done | bytes 458784 | tf_op jit(solution)/shard_map/ppermute | solution.py:53
  82.9 1.8 %finish_last.1 = (f32[256,2560]{1,0:T(8,128)}, f32[256,512]{1,0:T(8,128)}, f32[256,512]{1,0:T(8,128)}) custom-call(s32[9]{0:T(128)S(1)} %stack.39.place_ref.refs_0_, bf16[256,896]{1,0:T(8,128)(2,1)S(1)} %collective-permute-done.11.refs_0_, ...), custom_call_target="tpu_custom_call", output_to_operand_aliasing={{0}: (3, {}), {1}: (4, {}), {2}: (5, {})} | custom-call | tf_op jit(solution)/shard_map/finish_last/pallas_call | solution.py:400
  (55 shorter events, 1.4 us)
Async XLA Ops:
  0.6 16.8 %copy-start.6 = (f32[128]{0:T(128)S(1)}, f32[128]{0:T(128)}, u32[]{:S(2)}) copy-start(f32[128]{0:T(128)} %constant.171) | copy-start | bytes 1540
  0.6 16.8 %copy-start.7 = (f32[128]{0:T(128)S(1)}, f32[128]{0:T(128)}, u32[]{:S(2)}) copy-start(f32[128]{0:T(128)} %constant.169) | copy-start | bytes 1540
  0.7 16.8 %copy-start.8 = (f32[128]{0:T(128)S(1)}, f32[128]{0:T(128)}, u32[]{:S(2)}) copy-start(f32[128]{0:T(128)} %constant.167) | copy-start | bytes 1540
  0.7 16.8 %copy-start.9 = (f32[128]{0:T(128)S(1)}, f32[128]{0:T(128)}, u32[]{:S(2)}) copy-start(f32[128]{0:T(128)} %constant.165) | copy-start | bytes 1540
  0.7 11.5 %copy-start.5 = (s32[20,2,4]{0,2,1:T(4,128)S(1)}, s32[20,2,4]{0,2,1:T(4,128)}, u32[]{:S(2)}) copy-start(s32[20,2,4]{0,2,1:T(4,128)} %param.23) | copy-start | bytes 1924
  0.7 11.8 %copy-start.3 = (bf16[128,512]{1,0:T(8,128)(2,1)S(1)}, bf16[128,512]{1,0:T(8,128)(2,1)}, u32[]{:S(2)}) copy-start(bf16[128,512]{1,0:T(8,128)(2,1)} %refs_2_.2) | copy-start | bytes 393220
  0.7 11.8 %copy-start.2 = (bf16[128,512]{1,0:T(8,128)(2,1)S(1)}, bf16[128,512]{1,0:T(8,128)(2,1)}, u32[]{:S(2)}) copy-start(bf16[128,512]{1,0:T(8,128)(2,1)} %refs_1_.1) | copy-start | bytes 393220
  0.7 32.8 %collective-permute-start.1 = (bf16[256,2560]{1,0:T(8,128)(2,1)}, bf16[256,2560]{1,0:T(8,128)(2,1)S(1)}, u32[]{:S(2)}, u32[]{:S(2)}) collective-permute-start(bf16[256,2560]{1,0:T(8,128)(2,1)} %refs_2_.3), channel_id=1, source_target_pairs={{0,8},{4,12},{8,0},{12,4},{16,24},{20,28},{24,16},{28,20},{1,9},{5... | collective-permute-start | bytes 3932168 | tf_op jit(solution)/shard_map/ppermute | solution.py:53
  3.7 33.1 %collective-permute-start.2 = (bf16[256,2560]{1,0:T(8,128)(2,1)}, bf16[256,2560]{1,0:T(8,128)(2,1)S(1)}, u32[]{:S(2)}, u32[]{:S(2)}) collective-permute-start(bf16[256,2560]{1,0:T(8,128)(2,1)} %refs_2_.3), channel_id=1, source_target_pairs={{0,16},{4,20},{8,24},{12,28},{16,0},{20,4},{24,8},{28,12},{1,17},{... | collective-permute-start | bytes 3932168 | tf_op jit(solution)/shard_map/ppermute | solution.py:53
  8.0 12.2 %copy-start.10 = (bf16[512]{0:T(512)(128)(2,1)S(1)}, bf16[512]{0:T(512)(128)(2,1)}, u32[]{:S(2)}) copy-start(bf16[512]{0:T(512)(128)(2,1)} %param.20) | copy-start | bytes 3076
  8.0 12.2 %copy-start.11 = (bf16[512]{0:T(512)(128)(2,1)S(1)}, bf16[512]{0:T(512)(128)(2,1)}, u32[]{:S(2)}) copy-start(bf16[512]{0:T(512)(128)(2,1)} %param.19) | copy-start | bytes 3076
  8.0 32.7 %collective-permute-start.4 = (bf16[320,896]{1,0:T(8,128)(2,1)}, bf16[320,896]{1,0:T(8,128)(2,1)}, u32[]{:S(2)}, u32[]{:S(2)}) collective-permute-start(bf16[320,896]{1,0:T(8,128)(2,1)} %get-tuple-element.22), channel_id=1, source_target_pairs={{0,1},{1,0},{2,3},{3,2},{4,5},{5,4},{6,7},{7,6},{8,9},{9,8},{10,11... | collective-permute-start | bytes 1720328 | tf_op jit(solution)/shard_map/ppermute | solution.py:53
  9.6 29.3 %collective-permute-start = (bf16[320,896]{1,0:T(8,128)(2,1)}, bf16[320,896]{1,0:T(8,128)(2,1)}, u32[]{:S(2)}, u32[]{:S(2)}) collective-permute-start(bf16[320,896]{1,0:T(8,128)(2,1)} %get-tuple-element.22), channel_id=1, source_target_pairs={{0,2},{1,3},{2,0},{3,1},{4,6},{5,7},{6,4},{7,5},{8,10},{9,11},{10,... | collective-permute-start | bytes 1720328 | tf_op jit(solution)/shard_map/ppermute | solution.py:53
  13.3 25.6 %all-to-all-start = ((bf16[4,144,256]{2,1,0:T(8,128)(2,1)}), bf16[4,144,256]{2,1,0:T(8,128)(2,1)S(1)}, u32[]{:S(2)}, u32[]{:S(2)}) async-start(bf16[4,144,256]{2,1,0:T(8,128)(2,1)} %pack.1), calls=%async_computation | async-start | bytes 589824 | tf_op jit(solution)/shard_map/all_to_all | solution.py:456
  20.3 20.3 %copy-start.4 = (bf16[2560]{0:T(1024)(128)(2,1)S(1)}, bf16[2560]{0:T(1024)(128)(2,1)}, u32[]{:S(2)}) copy-start(bf16[2560]{0:T(1024)(128)(2,1)} %param.14) | copy-start | bytes 15364
  34.4 17.1 %collective-permute-start.7 = (bf16[128,2560]{1,0:T(8,128)(2,1)}, bf16[128,2560]{1,0:T(8,128)(2,1)}, u32[]{:S(2)}, u32[]{:S(2)}) collective-permute-start(bf16[128,2560]{1,0:T(8,128)(2,1)} %slice.28), channel_id=1, source_target_pairs={{0,16},{4,20},{8,24},{12,28},{16,0},{20,4},{24,8},{28,12},{1,17},{... | collective-permute-start | bytes 1966088 | tf_op jit(solution)/shard_map/ppermute | solution.py:53
  37.7 14.3 %collective-permute-start.8 = (bf16[128,2560]{1,0:T(8,128)(2,1)}, bf16[128,2560]{1,0:T(8,128)(2,1)}, u32[]{:S(2)}, u32[]{:S(2)}) collective-permute-start(bf16[128,2560]{1,0:T(8,128)(2,1)} %slice.29), channel_id=1, source_target_pairs={{0,8},{4,12},{8,0},{12,4},{16,24},{20,28},{24,16},{28,20},{1,9},{5... | collective-permute-start | bytes 1966088 | tf_op jit(solution)/shard_map/ppermute | solution.py:53
  38.9 12.6 %collective-permute-start.9 = (bf16[320,896]{1,0:T(8,128)(2,1)}, bf16[320,896]{1,0:T(8,128)(2,1)}, u32[]{:S(2)}, u32[]{:S(2)}) collective-permute-start(bf16[320,896]{1,0:T(8,128)(2,1)} %collective-permute-done.refs_3_), channel_id=1, source_target_pairs={{0,1},{1,0},{2,3},{3,2},{4,5},{5,4},{6,7},{7,6},{8,9},{9,8},{10,11... | collective-permute-start | bytes 1720328 | tf_op jit(solution)/shard_map/ppermute | solution.py:53
  40.5 4.2 %collective-permute-start.3 = (bf16[4,144,256]{2,1,0:T(8,128)(2,1)S(1)}, bf16[4,144,256]{2,1,0:T(8,128)(2,1)}, u32[]{:S(2)}, u32[]{:S(2)}) collective-permute-start(bf16[4,144,256]{2,1,0:T(8,128)(2,1)S(1)} %all-to-all-done), channel_id=1, source_target_pairs={{0,4},{4,0},{8,12},{12,8},{16,20},{20,16},{24,28},{28,24},{1,5},{5... | collective-permute-start | bytes 884744 | tf_op jit(solution)/shard_map/ppermute | solution.py:53
  40.7 11.4 %collective-permute-start.5 = (bf16[320,896]{1,0:T(8,128)(2,1)}, bf16[320,896]{1,0:T(8,128)(2,1)S(1)}, u32[]{:S(2)}, u32[]{:S(2)}) collective-permute-start(bf16[320,896]{1,0:T(8,128)(2,1)} %collective-permute-done.4.refs_1_), channel_id=1, source_target_pairs={{0,4},{4,0},{8,12},{12,8},{16,20},{20,16},{24,28},{28,24},{1,5},{5... | collective-permute-start | bytes 1720328 | tf_op jit(solution)/shard_map/ppermute | solution.py:53
  41.2 1.3 %copy-start = (bf16[256,2560]{1,0:T(8,128)(2,1)S(1)}, bf16[256,2560]{1,0:T(8,128)(2,1)}, u32[]{:S(2)}) copy-start(bf16[256,2560]{1,0:T(8,128)(2,1)} %refs_2_.3) | copy-start | bytes 3932164
  44.8 7.3 %copy-start.1 = (bf16[640,896]{1,0:T(8,128)(2,1)S(1)}, bf16[640,896]{1,0:T(8,128)(2,1)}, u32[]{:S(2)}) copy-start(bf16[640,896]{1,0:T(8,128)(2,1)} %get-tuple-element.27.refs_0_) | copy-start | bytes 3440644
  44.8 7.3 %collective-permute-start.6 = (bf16[320,896]{1,0:T(8,128)(2,1)}, bf16[320,896]{1,0:T(8,128)(2,1)S(1)}, u32[]{:S(2)}, u32[]{:S(2)}) collective-permute-start(bf16[320,896]{1,0:T(8,128)(2,1)} %collective-permute-done.refs_3_), channel_id=1, source_target_pairs={{0,4},{4,0},{8,12},{12,8},{16,20},{20,16},{24,28},{28,24},{1,5},{5... | collective-permute-start | bytes 1720328 | tf_op jit(solution)/shard_map/ppermute | solution.py:53
  52.0 2.7 %collective-permute-start.10 = (bf16[320,896]{1,0:T(8,128)(2,1)}, bf16[320,896]{1,0:T(8,128)(2,1)S(1)}, u32[]{:S(2)}, u32[]{:S(2)}) collective-permute-start(bf16[320,896]{1,0:T(8,128)(2,1)} %collective-permute-done.9.refs_9_), channel_id=1, source_target_pairs={{0,4},{4,0},{8,12},{12,8},{16,20},{20,16},{24,28},{28,24},{1,5},{5... | collective-permute-start | bytes 1720328 | tf_op jit(solution)/shard_map/ppermute | solution.py:53
  59.2 15.1 %collective-permute-start.13 = (bf16[256,896]{1,0:T(8,128)(2,1)S(1)}, bf16[256,896]{1,0:T(8,128)(2,1)S(1)}, u32[]{:S(2)}, u32[]{:S(2)}) collective-permute-start(bf16[256,896]{1,0:T(8,128)(2,1)S(1)} %get-tuple-element.37), channel_id=1, source_target_pairs={{0,24},{4,28},{8,16},{12,20},{16,8},{20,12},{24,0},{28,4},{1,25},{... | collective-permute-start | bytes 1376264 | tf_op jit(solution)/shard_map/ppermute | solution.py:53
  64.5 18.0 %collective-permute-start.11 = (bf16[256,896]{1,0:T(8,128)(2,1)S(1)}, bf16[256,896]{1,0:T(8,128)(2,1)S(1)}, u32[]{:S(2)}, u32[]{:S(2)}) collective-permute-start(bf16[256,896]{1,0:T(8,128)(2,1)S(1)} %heads.5), channel_id=1, source_target_pairs={{0,8},{4,12},{8,0},{12,4},{16,24},{20,28},{24,16},{28,20},{1,9},{5... | collective-permute-start | bytes 1376264 | tf_op jit(solution)/shard_map/ppermute | solution.py:53
  69.5 13.4 %collective-permute-start.12 = (bf16[256,896]{1,0:T(8,128)(2,1)S(1)}, bf16[256,896]{1,0:T(8,128)(2,1)S(1)}, u32[]{:S(2)}, u32[]{:S(2)}) collective-permute-start(bf16[256,896]{1,0:T(8,128)(2,1)S(1)} %heads.6), channel_id=1, source_target_pairs={{0,16},{4,20},{8,24},{12,28},{16,0},{20,4},{24,8},{28,12},{1,17},{... | collective-permute-start | bytes 1376264 | tf_op jit(solution)/shard_map/ppermute | solution.py:53
